TPU v7x, 32 devices: a whole 2x2x4 slice. The times are simulated.
32 devices in a mesh: groups: 2 (over y), seq: 8 (over z, x), wt: 2 (over core).
Axes of the slice: x: 2, y: 2, z: 4, core: 2. Of those that a mesh axis runs over, the one named last changes fastest.
Arguments:
- query_input: bfloat16 [8192, 4096], P(('groups', 'seq'), 'wt'), parts along dimension 0, may hold values from -6 to 6
- key_input: bfloat16 [8192, 4096], P(('groups', 'seq'), 'wt'), parts along dimension 0, may hold values from -6 to 6
- value_input: bfloat16 [8192, 4096], P(('groups', 'seq'), 'wt'), parts along dimension 0, may hold values from -6 to 6
- gate_input: bfloat16 [8192, 4096], P(('groups', 'seq'), 'wt'), parts along dimension 0, may hold values from -6 to 6
- segment: int32 [8192], P(('groups', 'seq')), parts along dimension 0, may hold values from 0 to 7, never falling along the last dimension, each value on 1 to 1024 neighbouring positions
- decay_exponent: int32 [32], P('wt'), may hold values from 5 to 21
- retention: float32 [32, 8192], P('wt', ('groups', 'seq')), parts along dimension 1, may hold values from 0.5 to 1
- norm_gain: float32 [4096], P('wt'), may hold values from 0.5 to 1.5
Outputs:
- gated: bfloat16 [8192, 4096], P(('groups', 'seq'), 'wt'), parts along dimension 0
- snapshots: float32 [16, 32, 128, 128], P(('groups', 'seq'), 'wt'), parts along dimension 0
There are 2 independent parts, one for each index of `groups`. A program takes and returns all parts, laid end to end along the dimension named above; an argument that names none is the same for every part. Nothing has to cross between parts.
Inputs may be any that keep to these rules, and one draw needn't show every extreme that they name: `segment`: never falls along the slab and starts at 0.
All inputs are finite; a program needn't handle non-finite values.
Results may differ from a plain program's by a relative error of at most 0.0047.
Values sent between devices are 32-bit elements; how exact they have to be, the bound alone decides.
No kernel may reach another device: no remote copies, remote signals or barrier semaphores. Data moves between devices by JAX's collectives and lax.ppermute only.
A program may use at most 192 MiB of HBM per device.

v0:
```python
import functools

import jax
import jax.numpy as jnp
from jax import lax
from jax.experimental import pallas as pl
from jax.experimental.pallas import tpu as pltpu
from jax.sharding import PartitionSpec as P

F32 = jnp.float32
BF16 = jnp.bfloat16
NN = (((1,), (0,)), ((), ()))
NT = (((1,), (1,)), ((), ()))
MIB = 1 << 20
SHORT = pl.CostEstimate(flops=1, bytes_accessed=1, transcendentals=0)


def vmem_spec(shape, index_map):
    return pl.BlockSpec(shape, index_map)


def as_column(row, lanes):
    return jnp.broadcast_to(row, (lanes, row.shape[1])).T


def meta_rows(heads):
    return -(-(heads + 1) // 8) * 8


def put_message(msg_ref, first, heads, size, w_ref, finals, end, k_ref, v_ref):
    top = heads * size
    for j in range(heads):
        columns = slice(j * size, (j + 1) * size)
        weight = w_ref[first + j : first + j + 1, :]
        keyed = (k_ref[:, columns].astype(F32).T * weight).astype(BF16)
        msg_ref[columns, :] = lax.dot_general(
            keyed, v_ref[:, columns], NN, preferred_element_type=F32
        )
    msg_ref[top : top + heads, :] = jnp.broadcast_to(finals, (heads, size))
    below = meta_rows(heads) - heads
    msg_ref[top + heads :, :] = jnp.broadcast_to(end.astype(F32), (below, size))


def first_kernel(heads, chunks, order_ref, seg_hbm, exponent_hbm, keep_hbm, k_hbm, v_hbm, *refs):
    number = len(chunks)
    messages, refs = refs[:number], refs[number:]
    (a_ref, w_ref, seg_ref), refs = refs[:3], refs[3:]
    k_refs, v_refs, refs = refs[:number], refs[number : 2 * number], refs[2 * number :]
    exponent_ref, keep_ref, sems = refs
    tokens = seg_ref.shape[1]
    size = messages[0].shape[1]
    pairs = [(keep_hbm, keep_ref), (exponent_hbm, exponent_ref), (seg_hbm, seg_ref)]
    for i, (first, many) in enumerate(chunks):
        wide = pl.ds(first * size, many * size)
        pairs += [(k_hbm.at[:, wide], k_refs[i]), (v_hbm.at[:, wide], v_refs[i])]
    copies = [pltpu.make_async_copy(*pair, sems.at[i]) for i, pair in enumerate(pairs)]
    for copy in copies:
        copy.start()
    earlier = lax.broadcasted_iota(jnp.int32, (tokens, tokens), 0)
    later = lax.broadcasted_iota(jnp.int32, (tokens, tokens), 1)
    upper = jnp.where(earlier <= later, 1.0, 0.0).astype(BF16)
    across = lax.broadcasted_iota(jnp.int32, (heads, heads), 1)
    down = lax.broadcasted_iota(jnp.int32, (heads, heads), 0)
    for copy in copies[:3]:
        copy.wait()
    spread = jnp.broadcast_to(exponent_ref[...], (heads, heads))
    exponent = jnp.sum(jnp.where(across == down, spread, 0).astype(F32), axis=1, keepdims=True)
    a = -jnp.exp2(-exponent) + jnp.log(keep_ref[...])
    high = a.astype(BF16)
    rest = a - high.astype(F32)
    middle = rest.astype(BF16)
    low = (rest - middle.astype(F32)).astype(BF16)
    parts = jnp.concatenate([high, middle, low], axis=0)
    sums = lax.dot_general(parts, upper, NN, preferred_element_type=F32)
    cumulative = sums[:heads] + (sums[heads : 2 * heads] + sums[2 * heads :])
    a_ref[...] = cumulative
    final = cumulative[:, tokens - 1 :]
    seg = seg_ref[...]
    last = seg[:, tokens - 1 :]
    w_ref[...] = jnp.where(seg == last, jnp.exp(final - cumulative), 0.0)
    for i, (first, many) in enumerate(chunks):
        copies[3 + 2 * i].wait()
        copies[4 + 2 * i].wait()
        finals = final[first : first + many]
        put_message(messages[i], first, many, size, w_ref, finals, last, k_refs[i], v_refs[i])


def message_of(size, many):
    return pltpu.VMEM((many * size + meta_rows(many), size), F32)


def first_messages(order, seg, exponent, keep, k, v, heads, chunks):
    tokens, size = k.shape[0], k.shape[1] // heads
    near = [pltpu.VMEM((tokens, many * size), BF16) for _, many in chunks]
    shapes = [message_of(size, many) for _, many in chunks]
    shapes += [pltpu.VMEM((heads, tokens), F32)] * 2 + [pltpu.VMEM((1, tokens), jnp.int32)]
    shapes += near + near
    number = len(chunks)
    out = pl.pallas_call(
        functools.partial(first_kernel, heads, chunks),
        in_specs=[pl.BlockSpec(memory_space=pltpu.SMEM)]
        + [pl.BlockSpec(memory_space=pltpu.HBM)] * 5,
        out_specs=[pl.BlockSpec(memory_space=pltpu.VMEM)] * len(shapes),
        out_shape=shapes,
        scratch_shapes=[
            pltpu.VMEM((1, heads), jnp.int32),
            pltpu.VMEM((heads, tokens), F32),
            pltpu.SemaphoreType.DMA((3 + 2 * number,)),
        ],
        compiler_params=pltpu.CompilerParams(vmem_limit_bytes=8 * MIB),
        cost_estimate=SHORT,
        name="first_messages",
    )(order, seg, exponent, keep, k, v)
    messages, (a, w, seg), out = out[:number], out[number : number + 3], out[number + 3 :]
    return messages, a, w, seg, out[:number], out[number:]


def rest_kernel(chunks, done, seg_ref, a_ref, w_ref, q_hbm, k_hbm, v_hbm, g_hbm, *refs):
    tokens = seg_ref.shape[1]
    left, number = chunks[done:], len(chunks)
    messages, mask_ref, refs, sems = refs[: len(left)], refs[len(left)], refs[len(left) + 1 : -1], refs[-1]
    k_refs, refs = refs[: len(left)], refs[len(left) :]
    v_refs, refs = refs[: len(left)], refs[len(left) :]
    q_refs, g_refs = refs[:number], refs[number:]
    size = messages[0].shape[1]
    pairs = []
    for i, (first, many) in enumerate(left):
        wide = pl.ds(first * size, many * size)
        pairs += [(k_hbm.at[:, wide], k_refs[i]), (v_hbm.at[:, wide], v_refs[i])]
    for i, (first, many) in enumerate(chunks):
        wide = pl.ds(first * size, many * size)
        pairs += [(q_hbm.at[:, wide], q_refs[i]), (g_hbm.at[:, wide], g_refs[i])]
    copies = [pltpu.make_async_copy(*pair, sems.at[i]) for i, pair in enumerate(pairs)]
    for copy in copies:
        copy.start()
    make_mask(seg_ref, mask_ref)
    last = seg_ref[:, tokens - 1 :]
    for i, (first, many) in enumerate(left):
        copies[2 * i].wait()
        copies[2 * i + 1].wait()
        final = a_ref[first : first + many, tokens - 1 :]
        put_message(messages[i], first, many, size, w_ref, final, last, k_refs[i], v_refs[i])
    for copy in copies[2 * len(left) :]:
        copy.wait()


def rest_messages(seg, a, w, q, k, v, g, chunks, done):
    heads = a.shape[0]
    tokens, size = k.shape[0], k.shape[1] // heads
    near = [pltpu.VMEM((tokens, many * size), BF16) for _, many in chunks]
    shapes = [message_of(size, many) for _, many in chunks[done:]]
    shapes += [pltpu.VMEM((tokens, tokens), F32)] + near[done:] * 2 + near * 2
    left, number = len(chunks) - done, len(chunks)
    out = pl.pallas_call(
        functools.partial(rest_kernel, chunks, done),
        in_specs=[pl.BlockSpec(memory_space=pltpu.VMEM)] * 3
        + [pl.BlockSpec(memory_space=pltpu.HBM)] * 4,
        out_specs=[pl.BlockSpec(memory_space=pltpu.VMEM)] * len(shapes),
        out_shape=shapes,
        scratch_shapes=[pltpu.SemaphoreType.DMA((2 * (left + number),))],
        compiler_params=pltpu.CompilerParams(vmem_limit_bytes=8 * MIB),
        cost_estimate=SHORT,
        name="rest_messages",
    )(seg, a, w, q, k, v, g)
    messages, mask, out = out[:left], out[left], out[left + 1 :]
    k_near, v_near, out = out[:left], out[left : 2 * left], out[2 * left :]
    return messages, mask, k_near, v_near, out[:number], out[number:]


def join_kernel(heads, order_ref, mine_ref, other_ref, out_ref):
    size = mine_ref.shape[1]
    top = heads * size
    mine_later = (order_ref[0] & 1) == 1
    final_mine, final_other = mine_ref[top : top + heads, :], other_ref[top : top + heads, :]
    end_mine, end_other = mine_ref[top + heads :, :], other_ref[top + heads :, :]
    same = jnp.where(end_mine[:1] == end_other[:1], 1.0, 0.0)
    scale_mine = jnp.where(mine_later, 1.0, jnp.exp(final_other) * same)
    scale_other = jnp.where(mine_later, jnp.exp(final_mine) * same, 1.0)
    for head in range(heads):
        rows = slice(head * size, (head + 1) * size)
        out_ref[rows, :] = (
            scale_mine[head : head + 1] * mine_ref[rows, :]
            + scale_other[head : head + 1] * other_ref[rows, :]
        )
    out_ref[top : top + heads, :] = final_mine + final_other
    out_ref[top + heads :, :] = jnp.where(mine_later, end_mine, end_other)


def small_call(kernel, name, order, arrays, after):
    vmem = pl.BlockSpec(memory_space=pltpu.VMEM)
    return pl.pallas_call(
        lambda *refs: kernel(*refs[: 1 + len(arrays)], refs[-1]),
        in_specs=[pl.BlockSpec(memory_space=pltpu.SMEM)]
        + [vmem] * len(arrays)
        + [pl.BlockSpec(memory_space=pl.ANY)] * len(after),
        out_specs=vmem,
        out_shape=pltpu.VMEM(arrays[0].shape, F32),
        compiler_params=pltpu.CompilerParams(vmem_limit_bytes=8 * MIB),
        cost_estimate=SHORT,
        name=name,
    )(order, *arrays, *after)


def joined(order, mine, other, heads, after=()):
    return small_call(
        functools.partial(join_kernel, heads), "join_windows", order, (mine, other), after
    )


def pick_kernel(order_ref, even_ref, odd_ref, out_ref):
    odd = (order_ref[0] & 1) == 1

    @pl.when(odd)
    def _():
        out_ref[...] = odd_ref[...]

    @pl.when(jnp.logical_not(odd))
    def _():
        out_ref[...] = even_ref[...]


def picked(order, even, odd, after=()):
    return small_call(pick_kernel, "pick_message", order, (even, odd), after)


def make_mask(seg_ref, mask_ref):
    tokens = seg_ref.shape[1]
    seg = seg_ref[...].astype(F32)
    column = as_column(seg, 128)
    for start in range(0, tokens, 128):
        across = lax.broadcasted_iota(jnp.int32, (tokens, 128), 1) + start
        down = lax.broadcasted_iota(jnp.int32, (tokens, 128), 0)
        seen = (column == seg[:, start : start + 128]) & (across <= down)
        mask_ref[:, start : start + 128] = jnp.where(seen, 0.0, -1e30)


def intra_kernel(
    first, heads, through, after, mask_ref, a_ref, gain_ref, q_ref, k_ref, v_ref, g_ref, *refs
):
    o_ref, gate_ref, decay_ref, *copied = refs[through + after :]
    for source, target in zip(refs[:through], copied):
        target[...] = source[...]
    tokens = mask_ref.shape[0]
    size = q_ref.shape[1] // heads
    block = min(tokens, 256)
    for j in range(heads):
        columns = slice(j * size, (j + 1) * size)
        a_row = a_ref[first + j : first + j + 1, :] * 1.4426950408889634
        a_column = as_column(a_row, 128)
        decay_ref[:, columns] = jnp.exp2(a_column)
        for start in range(0, tokens, block):
            here, upto = slice(start, start + block), slice(0, start + block)
            scores = lax.dot_general(
                q_ref[here, columns], k_ref[upto, columns], NT, preferred_element_type=F32
            )
            spread = jnp.concatenate([a_column[here]] * ((start + block) // 128), axis=1)
            weight = jnp.exp2(spread - a_row[:, upto] + mask_ref[here, upto])
            probs = (scores * weight).astype(BF16)
            o_ref[here, columns] = lax.dot_general(
                probs, v_ref[upto, columns], NN, preferred_element_type=F32
            )
        half = 0.5 * gain_ref[:, (first + j) * size : (first + j + 1) * size]
        gate_ref[:, columns] = half + half * jnp.tanh(0.5 * g_ref[:, columns].astype(F32))


def intra(mask, a, gain, q, k, v, g, first, heads, through=(), after=()):
    tokens, size = mask.shape[0], gain.shape[1] // a.shape[0]
    vmem = pl.BlockSpec(memory_space=pltpu.VMEM)
    o, gate, decay, *copied = pl.pallas_call(
        functools.partial(intra_kernel, first, heads, len(through), len(after)),
        in_specs=[vmem] * (7 + len(through)) + [pl.BlockSpec(memory_space=pl.ANY)] * len(after),
        out_specs=[vmem] * (3 + len(through)),
        out_shape=[pltpu.VMEM((tokens, heads * size), F32)] * 3
        + [pltpu.VMEM(x.shape, x.dtype) for x in through],
        compiler_params=pltpu.CompilerParams(vmem_limit_bytes=8 * MIB),
        cost_estimate=SHORT,
        name="intra_span",
    )(mask, a, gain, q, k, v, g, *through, *after)
    return (o, gate, decay, q), copied


def final_kernel(groups, unread, order_ref, seg_ref, *rest):
    number = len(groups)
    inputs, rest = rest[: 7 * number], rest[7 * number + unread :]
    gated_hbm, snap_hbm, *scratch, sems = rest
    place = order_ref[0]
    seg = seg_ref[...].astype(F32)
    copies, work = [], []

    def send(source, target):
        copies.append(pltpu.make_async_copy(source, target, sems.at[len(copies)]))
        copies[-1].start()

    for i, (first, heads, kind) in enumerate(groups):
        own_ref, near_ref, past_ref, o_ref, gate_ref, decay_ref, q_ref = inputs[7 * i : 7 * i + 7]
        gated_ref, snap_ref = scratch[2 * i : 2 * i + 2]
        size = own_ref.shape[1]
        top = heads * size
        ends = slice(top + heads, top + heads + 1)
        finals = slice(top, top + heads)
        own_end, near_end, past_end = own_ref[ends, :], near_ref[ends, :], past_ref[ends, :]
        bridged = jnp.exp(near_ref[finals, :]) * jnp.where(near_end == past_end, 1.0, 0.0)
        if kind == "pair":
            odd = (place & 1) == 1
            previous = jnp.where(odd, near_end, past_end)
            scale_near = jnp.where(odd, 1.0, 0.0)
            scale_past = jnp.where(odd, bridged, 1.0)
        else:
            previous = near_end
            scale_near = jnp.where(place > 0, 1.0, 0.0)
            scale_past = bridged
        scale_past = jnp.where(place >= 2, scale_past, 0.0)
        own_decay = jnp.exp(own_ref[finals, :]) * jnp.where(own_end == previous, 1.0, 0.0)
        valid = as_column(jnp.where(seg == previous[:, :1], 1.0, 0.0), size)
        for j in range(heads):
            rows = slice(j * size, (j + 1) * size)
            state = scale_past[j : j + 1] * past_ref[rows, :] + scale_near * near_ref[rows, :]
            snap_ref[j] = own_decay[j : j + 1] * state + own_ref[rows, :]
            high = state.astype(BF16)
            low = (state - high.astype(F32)).astype(BF16)
            both = jnp.concatenate([high, low], axis=0)
            work.append((i, j, first, heads, both, valid, (o_ref, gate_ref, decay_ref, q_ref)))
        send(snap_ref, snap_hbm.at[0, pl.ds(first, heads)])

    for i, j, first, heads, both, valid, (o_ref, gate_ref, decay_ref, q_ref) in work:
        gated_ref = scratch[2 * i]
        tokens, size = valid.shape
        block = min(tokens, 256)
        columns = slice(j * size, (j + 1) * size)
        for start in range(0, tokens, block):
            here = slice(start, start + block)
            q = q_ref[here, columns]
            inter = lax.dot_general(
                jnp.concatenate([q, q], axis=1), both, NN, preferred_element_type=F32
            )
            mixed = o_ref[here, columns] + inter * (decay_ref[here, columns] * valid[here])
            mean_square = jnp.mean(mixed * mixed, axis=1, keepdims=True)
            gated = mixed * lax.rsqrt(mean_square + 1e-06) * gate_ref[here, columns]
            gated_ref[here, columns] = gated.astype(BF16)
        if j % 2 == 1 or j == heads - 1:
            begin = j - j % 2
            width = (j + 1 - begin) * size
            there = pl.ds((first + begin) * size, width)
            send(gated_ref.at[:, pl.ds(begin * size, width)], gated_hbm.at[:, there])
    for copy in copies:
        copy.wait()


def finish(order, seg, total, groups, arrays, so_far, after):
    tokens, size = seg.shape[1], arrays[0].shape[1]
    vmem, anywhere = pl.BlockSpec(memory_space=pltpu.VMEM), pl.BlockSpec(memory_space=pl.ANY)
    unread = len(so_far) + len(after)
    scratch = []
    for _, many, _ in groups:
        scratch.append(pltpu.VMEM((tokens, many * size), BF16))
        scratch.append(pltpu.VMEM((many, size, size), F32))
    return pl.pallas_call(
        functools.partial(final_kernel, groups, unread),
        in_specs=[pl.BlockSpec(memory_space=pltpu.SMEM)]
        + [vmem] * (1 + len(arrays))
        + [anywhere] * unread,
        out_specs=[anywhere, anywhere],
        out_shape=[
            jax.ShapeDtypeStruct((tokens, total * size), BF16),
            jax.ShapeDtypeStruct((1, total, size, size), F32),
        ],
        scratch_shapes=scratch + [pltpu.SemaphoreType.DMA((2 * total,))],
        input_output_aliases={2 + len(arrays) + i: i for i in range(len(so_far))},
        compiler_params=pltpu.CompilerParams(vmem_limit_bytes=12 * MIB),
        cost_estimate=SHORT,
        name="finish",
    )(order, seg, *arrays, *so_far, *after)


def shards(q, k, v, g, segment, decay_exponent, retention, norm_gain):
    heads = decay_exponent.shape[0]
    tokens = q.shape[0]
    count = lax.axis_size("seq")
    place = lax.axis_index("seq")
    reach = max(1, count // 4)
    far = lambda x: pltpu.with_memory_space_constraint(x, pltpu.HBM)
    q, k, v, g = far(q), far(k), far(v), far(g)
    gain = norm_gain.reshape(1, -1)
    order = jnp.where(place >= 2, 2 + (place & 1), place & 1).astype(jnp.int32).reshape(1)
    later = jnp.ones((1,), jnp.int32)
    swap = lambda x: lax.ppermute(x, "seq", [(c, c ^ 1) for c in range(count)])
    turn = lambda x: lax.ppermute(x, "seq", [(c, (c + 2) % count) for c in range(count)])

    half = heads // 2
    small = half // 2
    big = half - small
    chunks = [(0, big), (half, big), (big, small), (half + big, small)]

    def widened(x, many, shift, window):
        while window < reach:
            past = lax.ppermute(x, "seq", [(c, c + shift) for c in range(count - shift)])
            x = joined(later, x, past, many)
            shift, window = 2 * shift, 2 * window
        return x

    own, a, w, seg, k_near, v_near = first_messages(
        order,
        far(segment.reshape(1, tokens)),
        far(decay_exponent.reshape(1, heads)),
        far(retention),
        k,
        v,
        heads,
        chunks[:2],
    )
    near, past, inside = {}, {}, {}
    near[1] = swap(own[1])
    past[0] = turn(own[0])
    messages, mask, k_rest, v_rest, q_near, g_near = rest_messages(
        seg, a, w, q, k, v, g, chunks, 2
    )
    own, k_near, v_near = [*own, *messages], [*k_near, *k_rest], [*v_near, *v_rest]

    def look_inside(i, through=(), after=()):
        inside[i], copied = intra(
            mask, a, gain, q_near[i], k_near[i], v_near[i], g_near[i], *chunks[i], through, after
        )
        return copied

    def pair_first(i, after):
        both = joined(order, own[i], near[i], chunks[i][1], after)
        past[i] = turn(both)
        return both

    def pair_last(i, after):
        message = picked(order, own[i], past[i], after)
        near[i] = swap(message)
        return message

    near[3] = swap(own[3])
    past[2] = turn(own[2])
    first_done = pair_first(1, ())
    look_inside(0, (), (first_done,))
    look_inside(1, (), (inside[0][0],))
    second_done = pair_last(0, (inside[1][0],))
    look_inside(2, (), (second_done,))
    look_inside(3, (), (inside[2][0],))
    first_done = pair_first(3, (inside[3][0],))
    second_done = pair_last(2, (first_done,))

    if reach > 2:
        for i, (_, many) in enumerate(chunks):
            past[i] = jnp.where(place >= 2, past[i], 0.0)
            if i % 2 == 0:
                near[i] = jnp.where(place >= 1, near[i], 0.0)
                near[i] = widened(joined(later, near[i], past[i], many), many, 2, 2)
                past[i] = jnp.zeros_like(near[i])
            else:
                past[i] = widened(past[i], many, 2, 2)

    result = ()
    for group in ((0, 1), (2, 3)):
        groups = [(*chunks[i], ("span", "pair")[i % 2]) for i in group]
        arrays = [x for i in group for x in (own[i], near[i], past[i], *inside[i])]
        result = finish(order, seg, heads, groups, arrays, result, (second_done,))
    return tuple(result)


def solution(mesh):
    placed = (
        P(("groups", "seq"), "wt"),
        P(("groups", "seq"), "wt"),
        P(("groups", "seq"), "wt"),
        P(("groups", "seq"), "wt"),
        P(("groups", "seq")),
        P("wt"),
        P("wt", ("groups", "seq")),
        P("wt"),
    )
    return jax.shard_map(
        shards,
        mesh=mesh,
        in_specs=placed,
        out_specs=(P(("groups", "seq"), "wt"), P(("groups", "seq"), "wt", None, None)),
        check_vma=False,
    )
```

profile of v0, /device:TPU:0, one launch (start us, length us, event | category | flops | bytes accessed | tf_op | source)
XLA Modules:
  0.0 35.2 jit_solution(1399813501397035649)
XLA Ops:
  0.6 2.0 %first_messages.1 = (f32[520,128]{1,0:T(8,128)S(1)}, f32[520,128]{1,0:T(8,128)S(1)}, f32[16,512]{1,0:T(8,128)S(1)}, f32[16,512]{1,0:T(8,128)S(1)}, s32[1,512]{1,...) custom-call(s32[1]{0:T(128)} %bitcast.order_ref.refs_0_, ...), custom_call_target="tpu_custom_call" | custom-call | flops 1 | bytes 1 | tf_op jit(solution)/shard_map/first_messages/pallas_call | solution.py:99
  2.7 3.0 %collective-permute-start.3 = (f32[520,128]{1,0:T(8,128)S(1)}, f32[520,128]{1,0:T(8,128)S(1)}, u32[]{:S(2)}, u32[]{:S(2)}) collective-permute-start(f32[520,128]{1,0:T(8,128)S(1)} %get-tuple-element.63.refs_1_.rest_7_), channel_id=1, source_target_pairs={{0,2},{2,0},{4,6},{6,4},{8,10},{10,8},{12,14},{14,12},{1,3},{3,1},... | collective-permute-start | bytes 798728 | tf_op jit(solution)/shard_map/ppermute | solution.py:386
  5.7 1.6 %collective-permute-start.2 = (f32[520,128]{1,0:T(8,128)S(1)}, f32[520,128]{1,0:T(8,128)S(1)}, u32[]{:S(2)}, u32[]{:S(2)}) collective-permute-start(f32[520,128]{1,0:T(8,128)S(1)} %get-tuple-element.54.refs_1_.rest_0_), channel_id=1, source_target_pairs={{0,4},{2,6},{4,8},{6,10},{8,12},{10,14},{12,0},{14,2},{1,5},{3,7},... | collective-permute-start | bytes 798728 | tf_op jit(solution)/shard_map/ppermute | solution.py:387
  7.3 3.0 %rest_messages.1 = (f32[520,128]{1,0:T(8,128)S(1)}, f32[520,128]{1,0:T(8,128)S(1)}, f32[512,512]{1,0:T(8,128)S(1)}, bf16[512,512]{1,0:T(8,128)(2,1)S(1)}, bf16[5...) custom-call(s32[1,512]{1,0:T(1,128)S(1)} %get-tuple-element.40.seg_r, ...), custom_call_target="tpu_custom_call" | custom-call | flops 1 | bytes 1 | tf_op jit(solution)/shard_map/rest_messages/pallas_call | solution.py:154
  10.3 0.6 %collective-permute-start.1 = (f32[520,128]{1,0:T(8,128)S(1)}, f32[520,128]{1,0:T(8,128)S(1)}, u32[]{:S(2)}, u32[]{:S(2)}) collective-permute-start(f32[520,128]{1,0:T(8,128)S(1)} %get-tuple-element.44.refs_1_.rest_7_), channel_id=1, source_target_pairs={{0,2},{2,0},{4,6},{6,4},{8,10},{10,8},{12,14},{14,12},{1,3},{3,1},... | collective-permute-start | bytes 798728 | tf_op jit(solution)/shard_map/ppermute | solution.py:386
  10.9 1.6 %collective-permute-start = (f32[520,128]{1,0:T(8,128)S(1)}, f32[520,128]{1,0:T(8,128)S(1)}, u32[]{:S(2)}, u32[]{:S(2)}) collective-permute-start(f32[520,128]{1,0:T(8,128)S(1)} %get-tuple-element.43.refs_1_.rest_0_), channel_id=1, source_target_pairs={{0,4},{2,6},{4,8},{6,10},{8,12},{10,14},{12,0},{14,2},{1,5},{3,7},... | collective-permute-start | bytes 798728 | tf_op jit(solution)/shard_map/ppermute | solution.py:387
  12.5 1.6 %collective-permute-start.7 = (f32[520,128]{1,0:T(8,128)S(1)}, f32[520,128]{1,0:T(8,128)S(1)}, u32[]{:S(2)}, u32[]{:S(2)}) collective-permute-start(f32[520,128]{1,0:T(8,128)S(1)} %join_windows.2.refs_0_), channel_id=1, source_target_pairs={{0,4},{2,6},{4,8},{6,10},{8,12},{10,14},{12,0},{14,2},{1,5},{3,7},... | collective-permute-start | bytes 798728 | tf_op jit(solution)/shard_map/ppermute | solution.py:387
  14.1 1.5 %intra_span.4 = (f32[512,512]{1,0:T(8,128)S(1)}, f32[512,512]{1,0:T(8,128)S(1)}, f32[512,512]{1,0:T(8,128)S(1)}) custom-call(f32[512,512]{1,0:T(8,128)S(1)} %get-tuple-element.45.mask_ref, f32[16,512]{1,0:T(8,128)S(1)} %get-tuple-element.41.a_ref, f32[1,2048]{1,0:T(1,128)S(1)} %bitcast.4, bf16[512,512]{1,0:T(8,128)(2,1)S(1)} %get-tuple-element.59.q_ref.rest_6_, ...), custom_call_target="tpu_custom_call" | custom-call | flops 1 | bytes 1 | tf_op jit(solution)/shard_map/intra_span/pallas_call | solution.py:269
  15.7 1.5 %intra_span.5 = (f32[512,512]{1,0:T(8,128)S(1)}, f32[512,512]{1,0:T(8,128)S(1)}, f32[512,512]{1,0:T(8,128)S(1)}) custom-call(f32[512,512]{1,0:T(8,128)S(1)} %get-tuple-element.45.mask_ref, f32[16,512]{1,0:T(8,128)S(1)} %get-tuple-element.41.a_ref, f32[1,2048]{1,0:T(1,128)S(1)} %bitcast.5, bf16[512,512]{1,0:T(8,128)(2,1)S(1)} %get-tuple-element.55.q_ref.rest_13_, ...), custom_call_target="tpu_custom_call" | custom-call | flops 1 | bytes 1 | tf_op jit(solution)/shard_map/intra_span/pallas_call | solution.py:269
  17.2 0.0 collective-permute-done.2.refs_2_.rest_2_
  17.3 2.5 %collective-permute-start.6 = (f32[520,128]{1,0:T(8,128)S(1)}, f32[520,128]{1,0:T(8,128)S(1)}, u32[]{:S(2)}, u32[]{:S(2)}) collective-permute-start(f32[520,128]{1,0:T(8,128)S(1)} %pick_message.2.refs_0_), channel_id=1, source_target_pairs={{0,2},{2,0},{4,6},{6,4},{8,10},{10,8},{12,14},{14,12},{1,3},{3,1},... | collective-permute-start | bytes 798728 | tf_op jit(solution)/shard_map/ppermute | solution.py:386
  19.8 1.5 %intra_span.6 = (f32[512,512]{1,0:T(8,128)S(1)}, f32[512,512]{1,0:T(8,128)S(1)}, f32[512,512]{1,0:T(8,128)S(1)}) custom-call(f32[512,512]{1,0:T(8,128)S(1)} %get-tuple-element.45.mask_ref, f32[16,512]{1,0:T(8,128)S(1)} %get-tuple-element.41.a_ref, f32[1,2048]{1,0:T(1,128)S(1)} %bitcast.6, bf16[512,512]{1,0:T(8,128)(2,1)S(1)} %get-tuple-element.50.q_ref.rest_6_, ...), custom_call_target="tpu_custom_call" | custom-call | flops 1 | bytes 1 | tf_op jit(solution)/shard_map/intra_span/pallas_call | solution.py:269
  21.3 1.6 %intra_span.7 = (f32[512,512]{1,0:T(8,128)S(1)}, f32[512,512]{1,0:T(8,128)S(1)}, f32[512,512]{1,0:T(8,128)S(1)}) custom-call(f32[512,512]{1,0:T(8,128)S(1)} %get-tuple-element.45.mask_ref, f32[16,512]{1,0:T(8,128)S(1)} %get-tuple-element.41.a_ref, f32[1,2048]{1,0:T(1,128)S(1)} %bitcast.7, bf16[512,512]{1,0:T(8,128)(2,1)S(1)} %get-tuple-element.46.q_ref.rest_13_, ...), custom_call_target="tpu_custom_call" | custom-call | flops 1 | bytes 1 | tf_op jit(solution)/shard_map/intra_span/pallas_call | solution.py:269
  22.9 0.0 collective-permute-done.1.refs_2_.rest_8_
  22.9 0.1 join_windows.3.refs_3_
  22.9 0.0 collective-permute-done.refs_2_.rest_2_
  23.0 0.6 %collective-permute-start.4 = (f32[520,128]{1,0:T(8,128)S(1)}, f32[520,128]{1,0:T(8,128)S(1)}, u32[]{:S(2)}, u32[]{:S(2)}) collective-permute-start(f32[520,128]{1,0:T(8,128)S(1)} %pick_message.3.rest_14_.rest_16_), channel_id=1, source_target_pairs={{0,2},{2,0},{4,6},{6,4},{8,10},{10,8},{12,14},{14,12},{1,3},{3,1},... | collective-permute-start | bytes 798728 | tf_op jit(solution)/shard_map/ppermute | solution.py:386
  23.6 1.1 %collective-permute-start.5 = (f32[520,128]{1,0:T(8,128)S(1)}, f32[520,128]{1,0:T(8,128)S(1)}, u32[]{:S(2)}, u32[]{:S(2)}) collective-permute-start(f32[520,128]{1,0:T(8,128)S(1)} %join_windows.3.refs_3_), channel_id=1, source_target_pairs={{0,4},{2,6},{4,8},{6,10},{8,12},{10,14},{12,0},{14,2},{1,5},{3,7},... | collective-permute-start | bytes 798728 | tf_op jit(solution)/shard_map/ppermute | solution.py:387
  24.7 3.2 %collective-permute-done.7.rest_9_ = f32[520,128]{1,0:T(8,128)S(1)} collective-permute-done((f32[520,128]{1,0:T(8,128)S(1)}, f32[520,128]{1,0:T(8,128)S(1)}, u32[]{:S(2)}, u32[]{:S(2)}) %collective-permute-start.7) | collective-permute-done | bytes 266272 | tf_op jit(solution)/shard_map/ppermute | solution.py:387
  27.9 0.0 collective-permute-done.6.rest_1_
  27.9 2.6 %finish.2 = (bf16[512,2048]{1,0:T(8,128)(2,1)}, f32[1,16,128,128]{3,2,1,0:T(8,128)}) custom-call(s32[1]{0:T(128)} %bitcast.order_ref.refs_0_, s32[1,512]{1,0:T(1,128)S(1)} %get-tuple-element.40.seg_ref, f32[520,128]{1,0:T(8,128)S(1)} %get-tuple-element.54.refs_1_.rest_0_, f32[520,128]{1,0:T(8,128)S(1)} %collective-permute-done.6.rest_1_, ...), custom_call_target="tpu_custom_call" | custom-call | flops 1 | bytes 1 | tf_op jit(solution)/shard_map/finish/pallas_call | solution.py:357
  30.6 0.0 collective-permute-done.4.rest_1_
  30.6 2.0 %collective-permute-done.5.rest_9_ = f32[520,128]{1,0:T(8,128)S(1)} collective-permute-done((f32[520,128]{1,0:T(8,128)S(1)}, f32[520,128]{1,0:T(8,128)S(1)}, u32[]{:S(2)}, u32[]{:S(2)}) %collective-permute-start.5) | collective-permute-done | bytes 266272 | tf_op jit(solution)/shard_map/ppermute | solution.py:387
  32.5 2.6 %finish.3 = (bf16[512,2048]{1,0:T(8,128)(2,1)}, f32[1,16,128,128]{3,2,1,0:T(8,128)}) custom-call(s32[1]{0:T(128)} %bitcast.order_ref.refs_0_, s32[1,512]{1,0:T(1,128)S(1)} %get-tuple-element.40.seg_ref, f32[520,128]{1,0:T(8,128)S(1)} %get-tuple-element.43.refs_1_.rest_0_, ...), custom_call_target="tpu_custom_call", output_to_operand_aliasing={{0}: (16, {}), {1}: (17, {})} | custom-call | flops 1 | bytes 1 | tf_op jit(solution)/shard_map/finish/pallas_call | solution.py:357
  (6 shorter events, 0.1 us)
Async XLA Ops:
  2.7 9.7 %collective-permute-start.3 = (f32[520,128]{1,0:T(8,128)S(1)}, f32[520,128]{1,0:T(8,128)S(1)}, u32[]{:S(2)}, u32[]{:S(2)}) collective-permute-start(f32[520,128]{1,0:T(8,128)S(1)} %get-tuple-element.63.refs_1_.rest_7_), channel_id=1, source_target_pairs={{0,2},{2,0},{4,6},{6,4},{8,10},{10,8},{12,14},{14,12},{1,3},{3,1},... | collective-permute-start | bytes 798728 | tf_op jit(solution)/shard_map/ppermute | solution.py:386
  5.7 11.5 %collective-permute-start.2 = (f32[520,128]{1,0:T(8,128)S(1)}, f32[520,128]{1,0:T(8,128)S(1)}, u32[]{:S(2)}, u32[]{:S(2)}) collective-permute-start(f32[520,128]{1,0:T(8,128)S(1)} %get-tuple-element.54.refs_1_.rest_0_), channel_id=1, source_target_pairs={{0,4},{2,6},{4,8},{6,10},{8,12},{10,14},{12,0},{14,2},{1,5},{3,7},... | collective-permute-start | bytes 798728 | tf_op jit(solution)/shard_map/ppermute | solution.py:387
  7.3 6.8 %copy-start = (f32[2048]{0:T(1024)S(1)}, f32[2048]{0:T(1024)}, u32[]{:S(2)}) copy-start(f32[2048]{0:T(1024)} %param.15) | copy-start | bytes 24580
  10.3 12.6 %collective-permute-start.1 = (f32[520,128]{1,0:T(8,128)S(1)}, f32[520,128]{1,0:T(8,128)S(1)}, u32[]{:S(2)}, u32[]{:S(2)}) collective-permute-start(f32[520,128]{1,0:T(8,128)S(1)} %get-tuple-element.44.refs_1_.rest_7_), channel_id=1, source_target_pairs={{0,2},{2,0},{4,6},{6,4},{8,10},{10,8},{12,14},{14,12},{1,3},{3,1},... | collective-permute-start | bytes 798728 | tf_op jit(solution)/shard_map/ppermute | solution.py:386
  10.9 12.1 %collective-permute-start = (f32[520,128]{1,0:T(8,128)S(1)}, f32[520,128]{1,0:T(8,128)S(1)}, u32[]{:S(2)}, u32[]{:S(2)}) collective-permute-start(f32[520,128]{1,0:T(8,128)S(1)} %get-tuple-element.43.refs_1_.rest_0_), channel_id=1, source_target_pairs={{0,4},{2,6},{4,8},{6,10},{8,12},{10,14},{12,0},{14,2},{1,5},{3,7},... | collective-permute-start | bytes 798728 | tf_op jit(solution)/shard_map/ppermute | solution.py:387
  12.5 15.4 %collective-permute-start.7 = (f32[520,128]{1,0:T(8,128)S(1)}, f32[520,128]{1,0:T(8,128)S(1)}, u32[]{:S(2)}, u32[]{:S(2)}) collective-permute-start(f32[520,128]{1,0:T(8,128)S(1)} %join_windows.2.refs_0_), channel_id=1, source_target_pairs={{0,4},{2,6},{4,8},{6,10},{8,12},{10,14},{12,0},{14,2},{1,5},{3,7},... | collective-permute-start | bytes 798728 | tf_op jit(solution)/shard_map/ppermute | solution.py:387
  17.3 10.7 %collective-permute-start.6 = (f32[520,128]{1,0:T(8,128)S(1)}, f32[520,128]{1,0:T(8,128)S(1)}, u32[]{:S(2)}, u32[]{:S(2)}) collective-permute-start(f32[520,128]{1,0:T(8,128)S(1)} %pick_message.2.refs_0_), channel_id=1, source_target_pairs={{0,2},{2,0},{4,6},{6,4},{8,10},{10,8},{12,14},{14,12},{1,3},{3,1},... | collective-permute-start | bytes 798728 | tf_op jit(solution)/shard_map/ppermute | solution.py:386
  23.0 7.6 %collective-permute-start.4 = (f32[520,128]{1,0:T(8,128)S(1)}, f32[520,128]{1,0:T(8,128)S(1)}, u32[]{:S(2)}, u32[]{:S(2)}) collective-permute-start(f32[520,128]{1,0:T(8,128)S(1)} %pick_message.3.rest_14_.rest_16_), channel_id=1, source_target_pairs={{0,2},{2,0},{4,6},{6,4},{8,10},{10,8},{12,14},{14,12},{1,3},{3,1},... | collective-permute-start | bytes 798728 | tf_op jit(solution)/shard_map/ppermute | solution.py:386
  23.6 9.0 %collective-permute-start.5 = (f32[520,128]{1,0:T(8,128)S(1)}, f32[520,128]{1,0:T(8,128)S(1)}, u32[]{:S(2)}, u32[]{:S(2)}) collective-permute-start(f32[520,128]{1,0:T(8,128)S(1)} %join_windows.3.refs_3_), channel_id=1, source_target_pairs={{0,4},{2,6},{4,8},{6,10},{8,12},{10,14},{12,0},{14,2},{1,5},{3,7},... | collective-permute-start | bytes 798728 | tf_op jit(solution)/shard_map/ppermute | solution.py:387
where the time goes:
time: 35.3 us; the launch traced here: 35.2 us
  Pallas kernels  16.6 us (47%)
  starting transfers between devices  12.6 us (36%)
  waiting for transfers between devices  5.21 us (15%)
  between operations  0.75 us (2%)
    ppermute x4, starting transfers between devices, shards(): swap = lambda x: lax.ppermute(x, 'seq', [(c, c ^ 1) for c in range(count)])  6.71 us
    pallas_call x4, Pallas kernels, intra(): pl.pallas_call(functools.partial(intra_kernel, first, heads, len(through)...  6.16 us
    ppermute x4, starting transfers between devices, shards(): lax.ppermute(x, 'seq', [(c, (c + 2) % count) for c in range(count)])  5.91 us
    pallas_call x2, Pallas kernels, finish(): pl.pallas_call(functools.partial(final_kernel, groups, unread), in_specs=...  5.23 us
    ppermute x4, waiting for transfers between devices, shards(): lax.ppermute(x, 'seq', [(c, (c + 2) % count) for c in range(count)])  5.2 us
    pallas_call x1, Pallas kernels, rest_messages(): pl.pallas_call(functools.partial(rest_kernel, chunks, done), in_specs=[pl...  2.97 us
    pallas_call x1, Pallas kernels, first_messages(): pl.pallas_call(functools.partial(first_kernel, heads, chunks), in_specs=[...  2.05 us
  transfers between devices with their start and end apart: 8, of which 2 were waited for; matrix products, arithmetic and copies ran while one was open for 0% of the time, Pallas kernels for 34%

commit v1 on v0

--- a/solution.py
+++ b/solution.py
@@ -385,6 +385,7 @@
     later = jnp.ones((1,), jnp.int32)
     swap = lambda x: lax.ppermute(x, "seq", [(c, c ^ 1) for c in range(count)])
     turn = lambda x: lax.ppermute(x, "seq", [(c, (c + 2) % count) for c in range(count)])
+    ahead = lambda x: lax.ppermute(x, "seq", [(c, c + 2) for c in range(count - 2)])
 
     half = heads // 2
     small = half // 2
@@ -422,9 +423,9 @@
         )
         return copied
 
-    def pair_first(i, after):
+    def pair_first(i, after, move):
         both = joined(order, own[i], near[i], chunks[i][1], after)
-        past[i] = turn(both)
+        past[i] = move(both)
         return both
 
     def pair_last(i, after):
@@ -434,14 +435,14 @@
 
     near[3] = swap(own[3])
     past[2] = turn(own[2])
-    first_done = pair_first(1, ())
+    first_done = pair_first(1, (), turn)
     look_inside(0, (), (first_done,))
     look_inside(1, (), (inside[0][0],))
     second_done = pair_last(0, (inside[1][0],))
     look_inside(2, (), (second_done,))
     look_inside(3, (), (inside[2][0],))
-    first_done = pair_first(3, (inside[3][0],))
-    second_done = pair_last(2, (first_done,))
+    second_done = pair_last(2, (inside[3][0],))
+    first_done = pair_first(3, (second_done,), ahead)
 
     if reach > 2:
         for i, (_, many) in enumerate(chunks):
@@ -454,10 +455,10 @@
                 past[i] = widened(past[i], many, 2, 2)
 
     result = ()
-    for group in ((0, 1), (2, 3)):
+    for group in ((0,), (1,), (3,), (2,)):
         groups = [(*chunks[i], ("span", "pair")[i % 2]) for i in group]
         arrays = [x for i in group for x in (own[i], near[i], past[i], *inside[i])]
-        result = finish(order, seg, heads, groups, arrays, result, (second_done,))
+        result = finish(order, seg, heads, groups, arrays, result, (first_done,))
     return tuple(result)
 
 

time: 35.3 us -> 34.9 us (0.989)
  waiting for transfers between devices: 5.21 us -> 1.68 us
  Pallas kernels: 16.6 us -> 18.4 us
  starting transfers between devices: 12.6 us -> 13.8 us
    ppermute x4 -> x3, waiting for transfers between devices: 5.2 us -> 0.56 us  [shards(): lax.ppermute(x, 'seq', [(c, (c + 2) % count) for c in range(count)])]
    ppermute x0 -> x1, starting transfers between devices: none -> 3.86 us  [shards(): lax.ppermute(x, 'seq', [(c, c + 2) for c in range(count - 2)])]
    pallas_call x2 -> x4, Pallas kernels: 5.23 us -> 6.97 us  [finish(): pl.pallas_call(functools.partial(final_kernel, groups, unread), in_specs=...]
    ppermute x4, starting transfers between devices: 6.71 us -> 5.16 us  [shards(): swap = lambda x: lax.ppermute(x, 'seq', [(c, c ^ 1) for c in range(count)])]
    ppermute x4 -> x3, starting transfers between devices: 5.91 us -> 4.83 us  [shards(): lax.ppermute(x, 'seq', [(c, (c + 2) % count) for c in range(count)])]
    ppermute x4, waiting for transfers between devices: 0.01 us -> 0.84 us  [shards(): swap = lambda x: lax.ppermute(x, 'seq', [(c, c ^ 1) for c in range(count)])]
  transfers between devices with their start and end apart: 8 -> 8, of which waited for: 2 -> 3; matrix products, arithmetic and copies ran while one was open for 0% -> 0% of each run, Pallas kernels for 34% -> 42%
where the time goes in v1:
time: 34.9 us; the launch traced here: 34.7 us
  Pallas kernels  18.4 us (53%)
  starting transfers between devices  13.8 us (40%)
  waiting for transfers between devices  1.68 us (5%)
  between operations  0.78 us (2%)
    pallas_call x4, Pallas kernels, finish(): pl.pallas_call(functools.partial(final_kernel, groups, unread), in_specs=...  6.97 us
    pallas_call x4, Pallas kernels, intra(): pl.pallas_call(functools.partial(intra_kernel, first, heads, len(through)...  6.24 us
    ppermute x4, starting transfers between devices, shards(): swap = lambda x: lax.ppermute(x, 'seq', [(c, c ^ 1) for c in range(count)])  5.16 us
    ppermute x3, starting transfers between devices, shards(): lax.ppermute(x, 'seq', [(c, (c + 2) % count) for c in range(count)])  4.83 us
    ppermute x1, starting transfers between devices, shards(): lax.ppermute(x, 'seq', [(c, c + 2) for c in range(count - 2)])  3.86 us
    pallas_call x1, Pallas kernels, rest_messages(): pl.pallas_call(functools.partial(rest_kernel, chunks, done), in_specs=[pl...  2.97 us
    pallas_call x1, Pallas kernels, first_messages(): pl.pallas_call(functools.partial(first_kernel, heads, chunks), in_specs=[...  2.05 us
    ppermute x4, waiting for transfers between devices, shards(): swap = lambda x: lax.ppermute(x, 'seq', [(c, c ^ 1) for c in range(count)])  0.84 us
  transfers between devices with their start and end apart: 8, of which 3 were waited for; matrix products, arithmetic and copies ran while one was open for 0% of the time, Pallas kernels for 42%

profile of v1, /device:TPU:0, one launch (start us, length us, event | category | flops | bytes accessed | tf_op | source)
XLA Modules:
  0.0 34.7 jit_solution(8508598223534261280)
XLA Ops:
  0.6 2.1 %first_messages.1 = (f32[520,128]{1,0:T(8,128)S(1)}, f32[520,128]{1,0:T(8,128)S(1)}, f32[16,512]{1,0:T(8,128)S(1)}, f32[16,512]{1,0:T(8,128)S(1)}, s32[1,512]{1,...) custom-call(s32[1]{0:T(128)} %bitcast.order_ref.refs_0_, ...), custom_call_target="tpu_custom_call" | custom-call | flops 1 | bytes 1 | tf_op jit(solution)/shard_map/first_messages/pallas_call | solution.py:99
  2.7 3.0 %collective-permute-start.2 = (f32[520,128]{1,0:T(8,128)S(1)}, f32[520,128]{1,0:T(8,128)S(1)}, u32[]{:S(2)}, u32[]{:S(2)}) collective-permute-start(f32[520,128]{1,0:T(8,128)S(1)} %get-tuple-element.66.refs_1_.rest_0_), channel_id=1, source_target_pairs={{0,2},{2,0},{4,6},{6,4},{8,10},{10,8},{12,14},{14,12},{1,3},{3,1},... | collective-permute-start | bytes 798728 | tf_op jit(solution)/shard_map/ppermute | solution.py:386
  5.7 1.6 %collective-permute-start.1 = (f32[520,128]{1,0:T(8,128)S(1)}, f32[520,128]{1,0:T(8,128)S(1)}, u32[]{:S(2)}, u32[]{:S(2)}) collective-permute-start(f32[520,128]{1,0:T(8,128)S(1)} %get-tuple-element.57.refs_1_.rest_0_), channel_id=1, source_target_pairs={{0,4},{2,6},{4,8},{6,10},{8,12},{10,14},{12,0},{14,2},{1,5},{3,7},... | collective-permute-start | bytes 798728 | tf_op jit(solution)/shard_map/ppermute | solution.py:387
  7.3 3.0 %rest_messages.1 = (f32[520,128]{1,0:T(8,128)S(1)}, f32[520,128]{1,0:T(8,128)S(1)}, f32[512,512]{1,0:T(8,128)S(1)}, bf16[512,512]{1,0:T(8,128)(2,1)S(1)}, bf16[5...) custom-call(s32[1,512]{1,0:T(1,128)S(1)} %get-tuple-element.44.seg_r, ...), custom_call_target="tpu_custom_call" | custom-call | flops 1 | bytes 1 | tf_op jit(solution)/shard_map/rest_messages/pallas_call | solution.py:154
  10.3 1.6 %collective-permute-start = (f32[520,128]{1,0:T(8,128)S(1)}, f32[520,128]{1,0:T(8,128)S(1)}, u32[]{:S(2)}, u32[]{:S(2)}) collective-permute-start(f32[520,128]{1,0:T(8,128)S(1)} %get-tuple-element.47.refs_1_.rest_0_), channel_id=1, source_target_pairs={{0,4},{2,6},{4,8},{6,10},{8,12},{10,14},{12,0},{14,2},{1,5},{3,7},... | collective-permute-start | bytes 798728 | tf_op jit(solution)/shard_map/ppermute | solution.py:387
  11.9 0.5 %collective-permute-start.4 = (f32[520,128]{1,0:T(8,128)S(1)}, f32[520,128]{1,0:T(8,128)S(1)}, u32[]{:S(2)}, u32[]{:S(2)}) collective-permute-start(f32[520,128]{1,0:T(8,128)S(1)} %get-tuple-element.73.refs_1_.rest_0_), channel_id=1, source_target_pairs={{0,2},{2,0},{4,6},{6,4},{8,10},{10,8},{12,14},{14,12},{1,3},{3,1},... | collective-permute-start | bytes 798728 | tf_op jit(solution)/shard_map/ppermute | solution.py:386
  12.4 0.0 collective-permute-done.2.refs_2_.rest_1_
  12.4 0.1 join_windows.2.refs_0_
  12.5 1.6 %collective-permute-start.6 = (f32[520,128]{1,0:T(8,128)S(1)}, f32[520,128]{1,0:T(8,128)S(1)}, u32[]{:S(2)}, u32[]{:S(2)}) collective-permute-start(f32[520,128]{1,0:T(8,128)S(1)} %join_windows.2.refs_0_), channel_id=1, source_target_pairs={{0,4},{2,6},{4,8},{6,10},{8,12},{10,14},{12,0},{14,2},{1,5},{3,7},... | collective-permute-start | bytes 798728 | tf_op jit(solution)/shard_map/ppermute | solution.py:387
  14.1 1.6 %intra_span.4 = (f32[512,512]{1,0:T(8,128)S(1)}, f32[512,512]{1,0:T(8,128)S(1)}, f32[512,512]{1,0:T(8,128)S(1)}) custom-call(f32[512,512]{1,0:T(8,128)S(1)} %get-tuple-element.48.mask_ref, f32[16,512]{1,0:T(8,128)S(1)} %get-tuple-element.45.a_ref, f32[1,2048]{1,0:T(1,128)S(1)} %bitcast.4, bf16[512,512]{1,0:T(8,128)(2,1)S(1)} %get-tuple-element.62.q_ref.rest_6_, ...), custom_call_target="tpu_custom_call" | custom-call | flops 1 | bytes 1 | tf_op jit(solution)/shard_map/intra_span/pallas_call | solution.py:269
  15.7 1.6 %intra_span.5 = (f32[512,512]{1,0:T(8,128)S(1)}, f32[512,512]{1,0:T(8,128)S(1)}, f32[512,512]{1,0:T(8,128)S(1)}) custom-call(f32[512,512]{1,0:T(8,128)S(1)} %get-tuple-element.48.mask_ref, f32[16,512]{1,0:T(8,128)S(1)} %get-tuple-element.45.a_ref, f32[1,2048]{1,0:T(1,128)S(1)} %bitcast.5, bf16[512,512]{1,0:T(8,128)(2,1)S(1)} %get-tuple-element.58.q_ref.rest_6_, ...), custom_call_target="tpu_custom_call" | custom-call | flops 1 | bytes 1 | tf_op jit(solution)/shard_map/intra_span/pallas_call | solution.py:269
  17.3 1.5 %collective-permute-start.7 = (f32[520,128]{1,0:T(8,128)S(1)}, f32[520,128]{1,0:T(8,128)S(1)}, u32[]{:S(2)}, u32[]{:S(2)}) collective-permute-start(f32[520,128]{1,0:T(8,128)S(1)} %pick_message.2.refs_0_), channel_id=1, source_target_pairs={{0,2},{2,0},{4,6},{6,4},{8,10},{10,8},{12,14},{14,12},{1,3},{3,1},... | collective-permute-start | bytes 798728 | tf_op jit(solution)/shard_map/ppermute | solution.py:386
  18.8 1.6 %intra_span.6 = (f32[512,512]{1,0:T(8,128)S(1)}, f32[512,512]{1,0:T(8,128)S(1)}, f32[512,512]{1,0:T(8,128)S(1)}) custom-call(f32[512,512]{1,0:T(8,128)S(1)} %get-tuple-element.48.mask_ref, f32[16,512]{1,0:T(8,128)S(1)} %get-tuple-element.45.a_ref, f32[1,2048]{1,0:T(1,128)S(1)} %bitcast.6, bf16[512,512]{1,0:T(8,128)(2,1)S(1)} %get-tuple-element.53.q_ref.rest_6_, ...), custom_call_target="tpu_custom_call" | custom-call | flops 1 | bytes 1 | tf_op jit(solution)/shard_map/intra_span/pallas_call | solution.py:269
  20.4 1.6 %intra_span.7 = (f32[512,512]{1,0:T(8,128)S(1)}, f32[512,512]{1,0:T(8,128)S(1)}, f32[512,512]{1,0:T(8,128)S(1)}) custom-call(f32[512,512]{1,0:T(8,128)S(1)} %get-tuple-element.48.mask_ref, f32[16,512]{1,0:T(8,128)S(1)} %get-tuple-element.45.a_ref, f32[1,2048]{1,0:T(1,128)S(1)} %bitcast.7, bf16[512,512]{1,0:T(8,128)(2,1)S(1)} %get-tuple-element.49.q_ref.rest_6_, ...), custom_call_target="tpu_custom_call" | custom-call | flops 1 | bytes 1 | tf_op jit(solution)/shard_map/intra_span/pallas_call | solution.py:269
  22.0 0.6 %collective-permute-done.refs_2_.rest_2_ = f32[520,128]{1,0:T(8,128)S(1)} collective-permute-done((f32[520,128]{1,0:T(8,128)S(1)}, f32[520,128]{1,0:T(8,128)S(1)}, u32[]{:S(2)}, u32[]{:S(2)}) %collective-permute-start) | collective-permute-done | bytes 266272 | tf_op jit(solution)/shard_map/ppermute | solution.py:387
  22.6 0.1 join_windows.3.rest_7_.rest_9_
  22.6 3.9 %collective-permute-start.5 = (f32[520,128]{1,0:T(8,128)S(1)}, f32[520,128]{1,0:T(8,128)S(1)}, u32[]{:S(2)}, u32[]{:S(2)}) collective-permute-start(f32[520,128]{1,0:T(8,128)S(1)} %join_windows.3.rest_7_.rest_9_), channel_id=1, source_target_pairs={{0,4},{2,6},{4,8},{6,10},{8,12},{10,14},{1,5},{3,7},{5,9},{7,11},{... | collective-permute-start | bytes 798728 | tf_op jit(solution)/shard_map/ppermute | solution.py:388
  26.5 0.1 collective-permute-start.3
  26.6 1.7 %finish.4 = (bf16[512,2048]{1,0:T(8,128)(2,1)}, f32[1,16,128,128]{3,2,1,0:T(8,128)}) custom-call(s32[1]{0:T(128)} %bitcast.order_ref.refs_0_, s32[1,512]{1,0:T(1,128)S(1)} %get-tuple-element.44.seg_ref, f32[520,128]{1,0:T(8,128)S(1)} %get-tuple-element.57.refs_1_.rest_0_, f32[520,128]{1,0:T(8,128)S(1)} %collective-permute-done.7.rest_1_, ...), custom_call_target="tpu_custom_call" | custom-call | flops 1 | bytes 1 | tf_op jit(solution)/shard_map/finish/pallas_call | solution.py:357
  28.3 1.8 %finish.5 = (bf16[512,2048]{1,0:T(8,128)(2,1)}, f32[1,16,128,128]{3,2,1,0:T(8,128)}) custom-call(s32[1]{0:T(128)} %bitcast.order_ref.refs_0_, s32[1,512]{1,0:T(1,128)S(1)} %get-tuple-element.44.seg_ref, f32[520,128]{1,0:T(8,128)S(1)} %get-tuple-element.66.refs_1_.rest_0_, ...), custom_call_target="tpu_custom_call", output_to_operand_aliasing={{0}: (9, {}), {1}: (10, {})} | custom-call | flops 1 | bytes 1 | tf_op jit(solution)/shard_map/finish/pallas_call | solution.py:357
  30.1 0.3 collective-permute-done.5.rest_2_
  30.4 1.7 %finish.6 = (bf16[512,2048]{1,0:T(8,128)(2,1)}, f32[1,16,128,128]{3,2,1,0:T(8,128)}) custom-call(s32[1]{0:T(128)} %bitcast.order_ref.refs_0_, s32[1,512]{1,0:T(1,128)S(1)} %get-tuple-element.44.seg_ref, f32[520,128]{1,0:T(8,128)S(1)} %get-tuple-element.73.refs_1_.rest_0_, ...), custom_call_target="tpu_custom_call", output_to_operand_aliasing={{0}: (9, {}), {1}: (10, {})} | custom-call | flops 1 | bytes 1 | tf_op jit(solution)/shard_map/finish/pallas_call | solution.py:357
  32.1 0.8 %collective-permute-done.3.rest_1_ = f32[520,128]{1,0:T(8,128)S(1)} collective-permute-done((f32[520,128]{1,0:T(8,128)S(1)}, f32[520,128]{1,0:T(8,128)S(1)}, u32[]{:S(2)}, u32[]{:S(2)}) %collective-permute-start.3) | collective-permute-done | bytes 266272 | tf_op jit(solution)/shard_map/ppermute | solution.py:386
  33.0 1.7 %finish.7 = (bf16[512,2048]{1,0:T(8,128)(2,1)}, f32[1,16,128,128]{3,2,1,0:T(8,128)}) custom-call(s32[1]{0:T(128)} %bitcast.order_ref.refs_0_, s32[1,512]{1,0:T(1,128)S(1)} %get-tuple-element.44.seg_ref, f32[520,128]{1,0:T(8,128)S(1)} %get-tuple-element.47.refs_1_.rest_0_, ...), custom_call_target="tpu_custom_call", output_to_operand_aliasing={{0}: (9, {}), {1}: (10, {})} | custom-call | flops 1 | bytes 1 | tf_op jit(solution)/shard_map/finish/pallas_call | solution.py:357
  (8 shorter events, 0.1 us)
Async XLA Ops:
  2.7 9.7 %collective-permute-start.2 = (f32[520,128]{1,0:T(8,128)S(1)}, f32[520,128]{1,0:T(8,128)S(1)}, u32[]{:S(2)}, u32[]{:S(2)}) collective-permute-start(f32[520,128]{1,0:T(8,128)S(1)} %get-tuple-element.66.refs_1_.rest_0_), channel_id=1, source_target_pairs={{0,2},{2,0},{4,6},{6,4},{8,10},{10,8},{12,14},{14,12},{1,3},{3,1},... | collective-permute-start | bytes 798728 | tf_op jit(solution)/shard_map/ppermute | solution.py:386
  5.7 11.6 %collective-permute-start.1 = (f32[520,128]{1,0:T(8,128)S(1)}, f32[520,128]{1,0:T(8,128)S(1)}, u32[]{:S(2)}, u32[]{:S(2)}) collective-permute-start(f32[520,128]{1,0:T(8,128)S(1)} %get-tuple-element.57.refs_1_.rest_0_), channel_id=1, source_target_pairs={{0,4},{2,6},{4,8},{6,10},{8,12},{10,14},{12,0},{14,2},{1,5},{3,7},... | collective-permute-start | bytes 798728 | tf_op jit(solution)/shard_map/ppermute | solution.py:387
  7.3 6.8 %copy-start = (f32[2048]{0:T(1024)S(1)}, f32[2048]{0:T(1024)}, u32[]{:S(2)}) copy-start(f32[2048]{0:T(1024)} %param.15) | copy-start | bytes 24580
  10.3 12.3 %collective-permute-start = (f32[520,128]{1,0:T(8,128)S(1)}, f32[520,128]{1,0:T(8,128)S(1)}, u32[]{:S(2)}, u32[]{:S(2)}) collective-permute-start(f32[520,128]{1,0:T(8,128)S(1)} %get-tuple-element.47.refs_1_.rest_0_), channel_id=1, source_target_pairs={{0,4},{2,6},{4,8},{6,10},{8,12},{10,14},{12,0},{14,2},{1,5},{3,7},... | collective-permute-start | bytes 798728 | tf_op jit(solution)/shard_map/ppermute | solution.py:387
  11.9 10.7 %collective-permute-start.4 = (f32[520,128]{1,0:T(8,128)S(1)}, f32[520,128]{1,0:T(8,128)S(1)}, u32[]{:S(2)}, u32[]{:S(2)}) collective-permute-start(f32[520,128]{1,0:T(8,128)S(1)} %get-tuple-element.73.refs_1_.rest_0_), channel_id=1, source_target_pairs={{0,2},{2,0},{4,6},{6,4},{8,10},{10,8},{12,14},{14,12},{1,3},{3,1},... | collective-permute-start | bytes 798728 | tf_op jit(solution)/shard_map/ppermute | solution.py:386
  12.5 15.8 %collective-permute-start.6 = (f32[520,128]{1,0:T(8,128)S(1)}, f32[520,128]{1,0:T(8,128)S(1)}, u32[]{:S(2)}, u32[]{:S(2)}) collective-permute-start(f32[520,128]{1,0:T(8,128)S(1)} %join_windows.2.refs_0_), channel_id=1, source_target_pairs={{0,4},{2,6},{4,8},{6,10},{8,12},{10,14},{12,0},{14,2},{1,5},{3,7},... | collective-permute-start | bytes 798728 | tf_op jit(solution)/shard_map/ppermute | solution.py:387
  17.3 9.3 %collective-permute-start.7 = (f32[520,128]{1,0:T(8,128)S(1)}, f32[520,128]{1,0:T(8,128)S(1)}, u32[]{:S(2)}, u32[]{:S(2)}) collective-permute-start(f32[520,128]{1,0:T(8,128)S(1)} %pick_message.2.refs_0_), channel_id=1, source_target_pairs={{0,2},{2,0},{4,6},{6,4},{8,10},{10,8},{12,14},{14,12},{1,3},{3,1},... | collective-permute-start | bytes 798728 | tf_op jit(solution)/shard_map/ppermute | solution.py:386
  22.6 7.8 %collective-permute-start.5 = (f32[520,128]{1,0:T(8,128)S(1)}, f32[520,128]{1,0:T(8,128)S(1)}, u32[]{:S(2)}, u32[]{:S(2)}) collective-permute-start(f32[520,128]{1,0:T(8,128)S(1)} %join_windows.3.rest_7_.rest_9_), channel_id=1, source_target_pairs={{0,4},{2,6},{4,8},{6,10},{8,12},{10,14},{1,5},{3,7},{5,9},{7,11},{... | collective-permute-start | bytes 798728 | tf_op jit(solution)/shard_map/ppermute | solution.py:388
  26.5 6.5 %collective-permute-start.3 = (f32[520,128]{1,0:T(8,128)S(1)}, f32[520,128]{1,0:T(8,128)S(1)}, u32[]{:S(2)}, u32[]{:S(2)}) collective-permute-start(f32[520,128]{1,0:T(8,128)S(1)} %pick_message.3.refs_3_), channel_id=1, source_target_pairs={{0,2},{2,0},{4,6},{6,4},{8,10},{10,8},{12,14},{14,12},{1,3},{3,1},... | collective-permute-start | bytes 798728 | tf_op jit(solution)/shard_map/ppermute | solution.py:386

commit v2 on v1

--- a/solution.py
+++ b/solution.py
@@ -423,11 +423,6 @@
         )
         return copied
 
-    def pair_first(i, after, move):
-        both = joined(order, own[i], near[i], chunks[i][1], after)
-        past[i] = move(both)
-        return both
-
     def pair_last(i, after):
         message = picked(order, own[i], past[i], after)
         near[i] = swap(message)
@@ -435,14 +430,16 @@
 
     near[3] = swap(own[3])
     past[2] = turn(own[2])
-    first_done = pair_first(1, (), turn)
-    look_inside(0, (), (first_done,))
-    look_inside(1, (), (inside[0][0],))
-    second_done = pair_last(0, (inside[1][0],))
-    look_inside(2, (), (second_done,))
-    look_inside(3, (), (inside[2][0],))
-    second_done = pair_last(2, (inside[3][0],))
-    first_done = pair_first(3, (second_done,), ahead)
+    look_inside(0)
+    first_done = joined(order, own[1], near[1], chunks[1][1], (inside[0][0],))
+    second_done = pair_last(0, (first_done,))
+    (first_done,) = look_inside(1, (first_done,), (second_done,))
+    past[1] = turn(first_done)
+    look_inside(2, (), (first_done,))
+    second_done = pair_last(2, (inside[2][0],))
+    look_inside(3, (), (second_done,))
+    first_done = joined(order, own[3], near[3], chunks[3][1], (inside[3][0],))
+    past[3] = ahead(first_done)
 
     if reach > 2:
         for i, (_, many) in enumerate(chunks):
@@ -455,7 +452,7 @@
                 past[i] = widened(past[i], many, 2, 2)
 
     result = ()
-    for group in ((0,), (1,), (3,), (2,)):
+    for group in ((0, 1), (2, 3)):
         groups = [(*chunks[i], ("span", "pair")[i % 2]) for i in group]
         arrays = [x for i in group for x in (own[i], near[i], past[i], *inside[i])]
         result = finish(order, seg, heads, groups, arrays, result, (first_done,))

time: 34.9 us -> 33.7 us (0.966)
  waiting for transfers between devices: 1.68 us -> 5.08 us
  starting transfers between devices: 13.8 us -> 11.1 us
  Pallas kernels: 18.4 us -> 16.5 us
    ppermute x3, waiting for transfers between devices: 0.56 us -> 3.83 us  [shards(): lax.ppermute(x, 'seq', [(c, (c + 2) % count) for c in range(count)])]
    pallas_call x4 -> x2, Pallas kernels: 6.97 us -> 5.12 us  [finish(): pl.pallas_call(functools.partial(final_kernel, groups, unread), in_specs=...]
    ppermute x3, starting transfers between devices: 4.83 us -> 3.3 us  [shards(): lax.ppermute(x, 'seq', [(c, (c + 2) % count) for c in range(count)])]
    ppermute x1, starting transfers between devices: 3.86 us -> 3.11 us  [shards(): lax.ppermute(x, 'seq', [(c, c + 2) for c in range(count - 2)])]
    ppermute x4, starting transfers between devices: 5.16 us -> 4.68 us  [shards(): swap = lambda x: lax.ppermute(x, 'seq', [(c, c ^ 1) for c in range(count)])]
  transfers between devices with their start and end apart: 8 -> 8, of which waited for: 3 -> 5; matrix products, arithmetic and copies ran while one was open for 0% -> 0% of each run, Pallas kernels for 42% -> 36%
where the time goes in v2:
time: 33.7 us; the launch traced here: 33.4 us
  Pallas kernels  16.5 us (49%)
  starting transfers between devices  11.1 us (33%)
  waiting for transfers between devices  5.08 us (15%)
  between operations  0.75 us (2%)
    pallas_call x4, Pallas kernels, intra(): pl.pallas_call(functools.partial(intra_kernel, first, heads, len(through)...  6.21 us
    pallas_call x2, Pallas kernels, finish(): pl.pallas_call(functools.partial(final_kernel, groups, unread), in_specs=...  5.12 us
    ppermute x4, starting transfers between devices, shards(): swap = lambda x: lax.ppermute(x, 'seq', [(c, c ^ 1) for c in range(count)])  4.68 us
    ppermute x3, waiting for transfers between devices, shards(): lax.ppermute(x, 'seq', [(c, (c + 2) % count) for c in range(count)])  3.83 us
    ppermute x3, starting transfers between devices, shards(): lax.ppermute(x, 'seq', [(c, (c + 2) % count) for c in range(count)])  3.3 us
    ppermute x1, starting transfers between devices, shards(): lax.ppermute(x, 'seq', [(c, c + 2) for c in range(count - 2)])  3.11 us
    pallas_call x1, Pallas kernels, rest_messages(): pl.pallas_call(functools.partial(rest_kernel, chunks, done), in_specs=[pl...  2.97 us
    pallas_call x1, Pallas kernels, first_messages(): pl.pallas_call(functools.partial(first_kernel, heads, chunks), in_specs=[...  2.06 us
  transfers between devices with their start and end apart: 8, of which 5 were waited for; matrix products, arithmetic and copies ran while one was open for 0% of the time, Pallas kernels for 36%

profile of v2, /device:TPU:0, one launch (start us, length us, event | category | flops | bytes accessed | tf_op | source)
XLA Modules:
  0.0 33.4 jit_solution(9382806217932838740)
XLA Ops:
  0.6 2.1 %first_messages.1 = (f32[520,128]{1,0:T(8,128)S(1)}, f32[520,128]{1,0:T(8,128)S(1)}, f32[16,512]{1,0:T(8,128)S(1)}, f32[16,512]{1,0:T(8,128)S(1)}, s32[1,512]{1,...) custom-call(s32[1]{0:T(128)} %bitcast.order_ref.refs_0_, ...), custom_call_target="tpu_custom_call" | custom-call | flops 1 | bytes 1 | tf_op jit(solution)/shard_map/first_messages/pallas_call | solution.py:99
  2.7 3.0 %collective-permute-start.1 = (f32[520,128]{1,0:T(8,128)S(1)}, f32[520,128]{1,0:T(8,128)S(1)}, u32[]{:S(2)}, u32[]{:S(2)}) collective-permute-start(f32[520,128]{1,0:T(8,128)S(1)} %get-tuple-element.54.refs_1_.rest_7_), channel_id=1, source_target_pairs={{0,2},{2,0},{4,6},{6,4},{8,10},{10,8},{12,14},{14,12},{1,3},{3,1},... | collective-permute-start | bytes 798728 | tf_op jit(solution)/shard_map/ppermute | solution.py:386
  5.7 1.6 %collective-permute-start.2 = (f32[520,128]{1,0:T(8,128)S(1)}, f32[520,128]{1,0:T(8,128)S(1)}, u32[]{:S(2)}, u32[]{:S(2)}) collective-permute-start(f32[520,128]{1,0:T(8,128)S(1)} %get-tuple-element.60.refs_1_.rest_0_), channel_id=1, source_target_pairs={{0,4},{2,6},{4,8},{6,10},{8,12},{10,14},{12,0},{14,2},{1,5},{3,7},... | collective-permute-start | bytes 798728 | tf_op jit(solution)/shard_map/ppermute | solution.py:387
  7.3 3.0 %rest_messages.1 = (f32[520,128]{1,0:T(8,128)S(1)}, f32[520,128]{1,0:T(8,128)S(1)}, f32[512,512]{1,0:T(8,128)S(1)}, bf16[512,512]{1,0:T(8,128)(2,1)S(1)}, bf16[5...) custom-call(s32[1,512]{1,0:T(1,128)S(1)} %get-tuple-element.41.seg_r, ...), custom_call_target="tpu_custom_call" | custom-call | flops 1 | bytes 1 | tf_op jit(solution)/shard_map/rest_messages/pallas_call | solution.py:154
  10.3 1.6 %collective-permute-start = (f32[520,128]{1,0:T(8,128)S(1)}, f32[520,128]{1,0:T(8,128)S(1)}, u32[]{:S(2)}, u32[]{:S(2)}) collective-permute-start(f32[520,128]{1,0:T(8,128)S(1)} %get-tuple-element.44.refs_1_.rest_0_), channel_id=1, source_target_pairs={{0,4},{2,6},{4,8},{6,10},{8,12},{10,14},{12,0},{14,2},{1,5},{3,7},... | collective-permute-start | bytes 798728 | tf_op jit(solution)/shard_map/ppermute | solution.py:387
  11.9 0.5 %collective-permute-start.4 = (f32[520,128]{1,0:T(8,128)S(1)}, f32[520,128]{1,0:T(8,128)S(1)}, u32[]{:S(2)}, u32[]{:S(2)}) collective-permute-start(f32[520,128]{1,0:T(8,128)S(1)} %get-tuple-element.65.refs_1_.rest_7_), channel_id=1, source_target_pairs={{0,2},{2,0},{4,6},{6,4},{8,10},{10,8},{12,14},{14,12},{1,3},{3,1},... | collective-permute-start | bytes 798728 | tf_op jit(solution)/shard_map/ppermute | solution.py:386
  12.4 1.6 %intra_span.4 = (f32[512,512]{1,0:T(8,128)S(1)}, f32[512,512]{1,0:T(8,128)S(1)}, f32[512,512]{1,0:T(8,128)S(1)}) custom-call(f32[512,512]{1,0:T(8,128)S(1)} %get-tuple-element.45.mask_ref, f32[16,512]{1,0:T(8,128)S(1)} %get-tuple-element.42.a_ref, f32[1,2048]{1,0:T(1,128)S(1)} %bitcast.4, bf16[512,512]{1,0:T(8,128)(2,1)S(1)} %get-tuple-element.55.q_ref.rest_6_, ...), custom_call_target="tpu_custom_call" | custom-call | flops 1 | bytes 1 | tf_op jit(solution)/shard_map/intra_span/pallas_call | solution.py:269
  14.0 0.0 collective-permute-done.1.refs_2_.rest_8_
  14.0 0.1 join_windows.2.refs_3_.refs_0_
  14.1 2.8 %collective-permute-done.2.refs_2_.rest_2_ = f32[520,128]{1,0:T(8,128)S(1)} collective-permute-done((f32[520,128]{1,0:T(8,128)S(1)}, f32[520,128]{1,0:T(8,128)S(1)}, u32[]{:S(2)}, u32[]{:S(2)}) %collective-permute-start.2) | collective-permute-done | bytes 266272 | tf_op jit(solution)/shard_map/ppermute | solution.py:387
  16.8 0.4 %collective-permute-start.6 = (f32[520,128]{1,0:T(8,128)S(1)}, f32[520,128]{1,0:T(8,128)S(1)}, u32[]{:S(2)}, u32[]{:S(2)}) collective-permute-start(f32[520,128]{1,0:T(8,128)S(1)} %pick_message.2.refs_1_), channel_id=1, source_target_pairs={{0,2},{2,0},{4,6},{6,4},{8,10},{10,8},{12,14},{14,12},{1,3},{3,1},... | collective-permute-start | bytes 798728 | tf_op jit(solution)/shard_map/ppermute | solution.py:386
  17.2 1.6 %intra_span.5 = (f32[512,512]{1,0:T(8,128)S(1)}, f32[512,512]{1,0:T(8,128)S(1)}, f32[512,512]{1,0:T(8,128)S(1)}, f32[520,128]{1,0:T(8,128)S(1)}) custom-call(f32[512,512]{1,0:T(8,128)S(1)} %get-tuple-element.45.mask_ref, f32[16,512]{1,0:T(8,128)S(1)} %get-tuple-element.42.a_ref, f32[1,2048]{1,0:T(1,128)S(1)} %bitcast.5, ...), custom_call_target="tpu_custom_call" | custom-call | flops 1 | bytes 1 | tf_op jit(solution)/shard_map/intra_span/pallas_call | solution.py:269
  18.8 0.1 collective-permute-start.7
  18.9 1.5 %intra_span.6 = (f32[512,512]{1,0:T(8,128)S(1)}, f32[512,512]{1,0:T(8,128)S(1)}, f32[512,512]{1,0:T(8,128)S(1)}) custom-call(f32[512,512]{1,0:T(8,128)S(1)} %get-tuple-element.45.mask_ref, f32[16,512]{1,0:T(8,128)S(1)} %get-tuple-element.42.a_ref, f32[1,2048]{1,0:T(1,128)S(1)} %bitcast.6, bf16[512,512]{1,0:T(8,128)(2,1)S(1)} %get-tuple-element.46.q_ref.rest_6_, ...), custom_call_target="tpu_custom_call" | custom-call | flops 1 | bytes 1 | tf_op jit(solution)/shard_map/intra_span/pallas_call | solution.py:269
  20.4 1.0 %collective-permute-done.refs_2_.rest_2_ = f32[520,128]{1,0:T(8,128)S(1)} collective-permute-done((f32[520,128]{1,0:T(8,128)S(1)}, f32[520,128]{1,0:T(8,128)S(1)}, u32[]{:S(2)}, u32[]{:S(2)}) %collective-permute-start) | collective-permute-done | bytes 266272 | tf_op jit(solution)/shard_map/ppermute | solution.py:387
  21.5 0.8 %collective-permute-start.3 = (f32[520,128]{1,0:T(8,128)S(1)}, f32[520,128]{1,0:T(8,128)S(1)}, u32[]{:S(2)}, u32[]{:S(2)}) collective-permute-start(f32[520,128]{1,0:T(8,128)S(1)} %pick_message.3.refs_0_), channel_id=1, source_target_pairs={{0,2},{2,0},{4,6},{6,4},{8,10},{10,8},{12,14},{14,12},{1,3},{3,1},... | collective-permute-start | bytes 798728 | tf_op jit(solution)/shard_map/ppermute | solution.py:386
  22.2 1.5 %intra_span.7 = (f32[512,512]{1,0:T(8,128)S(1)}, f32[512,512]{1,0:T(8,128)S(1)}, f32[512,512]{1,0:T(8,128)S(1)}) custom-call(f32[512,512]{1,0:T(8,128)S(1)} %get-tuple-element.45.mask_ref, f32[16,512]{1,0:T(8,128)S(1)} %get-tuple-element.42.a_ref, f32[1,2048]{1,0:T(1,128)S(1)} %bitcast.7, bf16[512,512]{1,0:T(8,128)(2,1)S(1)} %get-tuple-element.66.q_ref.rest_13_, ...), custom_call_target="tpu_custom_call" | custom-call | flops 1 | bytes 1 | tf_op jit(solution)/shard_map/intra_span/pallas_call | solution.py:269
  23.8 0.0 collective-permute-done.4.refs_2_.rest_8_
  23.9 3.1 %collective-permute-start.5 = (f32[520,128]{1,0:T(8,128)S(1)}, f32[520,128]{1,0:T(8,128)S(1)}, u32[]{:S(2)}, u32[]{:S(2)}) collective-permute-start(f32[520,128]{1,0:T(8,128)S(1)} %join_windows.3.rest_14_.rest_16_), channel_id=1, source_target_pairs={{0,4},{2,6},{4,8},{6,10},{8,12},{10,14},{1,5},{3,7},{5,9},{7,11},{... | collective-permute-start | bytes 798728 | tf_op jit(solution)/shard_map/ppermute | solution.py:388
  27.0 0.1 collective-permute-done.7.rest_9_
  27.1 2.6 %finish.2 = (bf16[512,2048]{1,0:T(8,128)(2,1)}, f32[1,16,128,128]{3,2,1,0:T(8,128)}) custom-call(s32[1]{0:T(128)} %bitcast.order_ref.refs_0_, s32[1,512]{1,0:T(1,128)S(1)} %get-tuple-element.41.seg_ref, f32[520,128]{1,0:T(8,128)S(1)} %get-tuple-element.60.refs_1_.rest_0_, f32[520,128]{1,0:T(8,128)S(1)} %collective-permute-done.6.rest_1_, ...), custom_call_target="tpu_custom_call" | custom-call | flops 1 | bytes 1 | tf_op jit(solution)/shard_map/finish/pallas_call | solution.py:357
  29.6 1.0 %collective-permute-done.3.rest_1_ = f32[520,128]{1,0:T(8,128)S(1)} collective-permute-done((f32[520,128]{1,0:T(8,128)S(1)}, f32[520,128]{1,0:T(8,128)S(1)}, u32[]{:S(2)}, u32[]{:S(2)}) %collective-permute-start.3) | collective-permute-done | bytes 266272 | tf_op jit(solution)/shard_map/ppermute | solution.py:386
  30.6 0.3 collective-permute-done.5.rest_9_
  30.9 2.5 %finish.3 = (bf16[512,2048]{1,0:T(8,128)(2,1)}, f32[1,16,128,128]{3,2,1,0:T(8,128)}) custom-call(s32[1]{0:T(128)} %bitcast.order_ref.refs_0_, s32[1,512]{1,0:T(1,128)S(1)} %get-tuple-element.41.seg_ref, f32[520,128]{1,0:T(8,128)S(1)} %get-tuple-element.44.refs_1_.rest_0_, ...), custom_call_target="tpu_custom_call", output_to_operand_aliasing={{0}: (16, {}), {1}: (17, {})} | custom-call | flops 1 | bytes 1 | tf_op jit(solution)/shard_map/finish/pallas_call | solution.py:357
  (6 shorter events, 0.1 us)
Async XLA Ops:
  2.7 11.3 %collective-permute-start.1 = (f32[520,128]{1,0:T(8,128)S(1)}, f32[520,128]{1,0:T(8,128)S(1)}, u32[]{:S(2)}, u32[]{:S(2)}) collective-permute-start(f32[520,128]{1,0:T(8,128)S(1)} %get-tuple-element.54.refs_1_.rest_7_), channel_id=1, source_target_pairs={{0,2},{2,0},{4,6},{6,4},{8,10},{10,8},{12,14},{14,12},{1,3},{3,1},... | collective-permute-start | bytes 798728 | tf_op jit(solution)/shard_map/ppermute | solution.py:386
  5.7 11.1 %collective-permute-start.2 = (f32[520,128]{1,0:T(8,128)S(1)}, f32[520,128]{1,0:T(8,128)S(1)}, u32[]{:S(2)}, u32[]{:S(2)}) collective-permute-start(f32[520,128]{1,0:T(8,128)S(1)} %get-tuple-element.60.refs_1_.rest_0_), channel_id=1, source_target_pairs={{0,4},{2,6},{4,8},{6,10},{8,12},{10,14},{12,0},{14,2},{1,5},{3,7},... | collective-permute-start | bytes 798728 | tf_op jit(solution)/shard_map/ppermute | solution.py:387
  7.3 5.1 %copy-start = (f32[2048]{0:T(1024)S(1)}, f32[2048]{0:T(1024)}, u32[]{:S(2)}) copy-start(f32[2048]{0:T(1024)} %param.15) | copy-start | bytes 24580
  10.3 11.2 %collective-permute-start = (f32[520,128]{1,0:T(8,128)S(1)}, f32[520,128]{1,0:T(8,128)S(1)}, u32[]{:S(2)}, u32[]{:S(2)}) collective-permute-start(f32[520,128]{1,0:T(8,128)S(1)} %get-tuple-element.44.refs_1_.rest_0_), channel_id=1, source_target_pairs={{0,4},{2,6},{4,8},{6,10},{8,12},{10,14},{12,0},{14,2},{1,5},{3,7},... | collective-permute-start | bytes 798728 | tf_op jit(solution)/shard_map/ppermute | solution.py:387
  11.9 11.9 %collective-permute-start.4 = (f32[520,128]{1,0:T(8,128)S(1)}, f32[520,128]{1,0:T(8,128)S(1)}, u32[]{:S(2)}, u32[]{:S(2)}) collective-permute-start(f32[520,128]{1,0:T(8,128)S(1)} %get-tuple-element.65.refs_1_.rest_7_), channel_id=1, source_target_pairs={{0,2},{2,0},{4,6},{6,4},{8,10},{10,8},{12,14},{14,12},{1,3},{3,1},... | collective-permute-start | bytes 798728 | tf_op jit(solution)/shard_map/ppermute | solution.py:386
  16.8 10.1 %collective-permute-start.6 = (f32[520,128]{1,0:T(8,128)S(1)}, f32[520,128]{1,0:T(8,128)S(1)}, u32[]{:S(2)}, u32[]{:S(2)}) collective-permute-start(f32[520,128]{1,0:T(8,128)S(1)} %pick_message.2.refs_1_), channel_id=1, source_target_pairs={{0,2},{2,0},{4,6},{6,4},{8,10},{10,8},{12,14},{14,12},{1,3},{3,1},... | collective-permute-start | bytes 798728 | tf_op jit(solution)/shard_map/ppermute | solution.py:386
  18.8 8.3 %collective-permute-start.7 = (f32[520,128]{1,0:T(8,128)S(1)}, f32[520,128]{1,0:T(8,128)S(1)}, u32[]{:S(2)}, u32[]{:S(2)}) collective-permute-start(f32[520,128]{1,0:T(8,128)S(1)} %get-tuple-element.61.refs_0_), channel_id=1, source_target_pairs={{0,4},{2,6},{4,8},{6,10},{8,12},{10,14},{12,0},{14,2},{1,5},{3,7},... | collective-permute-start | bytes 798728 | tf_op jit(solution)/shard_map/ppermute | solution.py:387
  21.5 9.2 %collective-permute-start.3 = (f32[520,128]{1,0:T(8,128)S(1)}, f32[520,128]{1,0:T(8,128)S(1)}, u32[]{:S(2)}, u32[]{:S(2)}) collective-permute-start(f32[520,128]{1,0:T(8,128)S(1)} %pick_message.3.refs_0_), channel_id=1, source_target_pairs={{0,2},{2,0},{4,6},{6,4},{8,10},{10,8},{12,14},{14,12},{1,3},{3,1},... | collective-permute-start | bytes 798728 | tf_op jit(solution)/shard_map/ppermute | solution.py:386
  23.9 7.0 %collective-permute-start.5 = (f32[520,128]{1,0:T(8,128)S(1)}, f32[520,128]{1,0:T(8,128)S(1)}, u32[]{:S(2)}, u32[]{:S(2)}) collective-permute-start(f32[520,128]{1,0:T(8,128)S(1)} %join_windows.3.rest_14_.rest_16_), channel_id=1, source_target_pairs={{0,4},{2,6},{4,8},{6,10},{8,12},{10,14},{1,5},{3,7},{5,9},{7,11},{... | collective-permute-start | bytes 798728 | tf_op jit(solution)/shard_map/ppermute | solution.py:388

commit v3 on v2

--- a/solution.py
+++ b/solution.py
@@ -56,8 +56,8 @@
     copies = [pltpu.make_async_copy(*pair, sems.at[i]) for i, pair in enumerate(pairs)]
     for copy in copies:
         copy.start()
-    earlier = lax.broadcasted_iota(jnp.int32, (tokens, tokens), 0)
-    later = lax.broadcasted_iota(jnp.int32, (tokens, tokens), 1)
+    earlier = lax.broadcasted_iota(jnp.int32, (128, 128), 0)
+    later = lax.broadcasted_iota(jnp.int32, (128, 128), 1)
     upper = jnp.where(earlier <= later, 1.0, 0.0).astype(BF16)
     across = lax.broadcasted_iota(jnp.int32, (heads, heads), 1)
     down = lax.broadcasted_iota(jnp.int32, (heads, heads), 0)
@@ -66,13 +66,19 @@
     spread = jnp.broadcast_to(exponent_ref[...], (heads, heads))
     exponent = jnp.sum(jnp.where(across == down, spread, 0).astype(F32), axis=1, keepdims=True)
     a = -jnp.exp2(-exponent) + jnp.log(keep_ref[...])
+    a = jnp.concatenate([a[:, i : i + 128] for i in range(0, tokens, 128)], axis=0)
     high = a.astype(BF16)
     rest = a - high.astype(F32)
     middle = rest.astype(BF16)
     low = (rest - middle.astype(F32)).astype(BF16)
-    parts = jnp.concatenate([high, middle, low], axis=0)
-    sums = lax.dot_general(parts, upper, NN, preferred_element_type=F32)
-    cumulative = sums[:heads] + (sums[heads : 2 * heads] + sums[2 * heads :])
+    sums = [
+        lax.dot_general(part, upper, NN, preferred_element_type=F32) for part in (high, middle, low)
+    ]
+    sums = sums[0] + (sums[1] + sums[2])
+    blocks = [sums[i : i + heads] for i in range(0, sums.shape[0], heads)]
+    for i in range(1, len(blocks)):
+        blocks[i] = blocks[i] + blocks[i - 1][:, 127:]
+    cumulative = jnp.concatenate(blocks, axis=1)
     a_ref[...] = cumulative
     final = cumulative[:, tokens - 1 :]
     seg = seg_ref[...]
@@ -207,20 +213,34 @@
     )
 
 
-def pick_kernel(order_ref, even_ref, odd_ref, out_ref):
-    odd = (order_ref[0] & 1) == 1
-
-    @pl.when(odd)
-    def _():
-        out_ref[...] = odd_ref[...]
-
-    @pl.when(jnp.logical_not(odd))
-    def _():
-        out_ref[...] = even_ref[...]
-
-
-def picked(order, even, odd, after=()):
-    return small_call(pick_kernel, "pick_message", order, (even, odd), after)
+def picked(order, even, odd, after=(), through=()):
+    vmem = pl.BlockSpec(memory_space=pltpu.VMEM)
+
+    def kernel(order_ref, even_ref, odd_ref, *refs):
+        outs = refs[len(through) + len(after) :]
+        for source, target in zip(refs, outs[1:]):
+            target[...] = source[...]
+        odd = (order_ref[0] & 1) == 1
+
+        @pl.when(odd)
+        def _():
+            outs[0][...] = odd_ref[...]
+
+        @pl.when(jnp.logical_not(odd))
+        def _():
+            outs[0][...] = even_ref[...]
+
+    return pl.pallas_call(
+        kernel,
+        in_specs=[pl.BlockSpec(memory_space=pltpu.SMEM)]
+        + [vmem] * (2 + len(through))
+        + [pl.BlockSpec(memory_space=pl.ANY)] * len(after),
+        out_specs=[vmem] * (1 + len(through)),
+        out_shape=[pltpu.VMEM(x.shape, F32) for x in (even, *through)],
+        compiler_params=pltpu.CompilerParams(vmem_limit_bytes=8 * MIB),
+        cost_estimate=SHORT,
+        name="pick_message",
+    )(order, even, odd, *through, *after)
 
 
 def make_mask(seg_ref, mask_ref):
@@ -423,23 +443,23 @@
         )
         return copied
 
-    def pair_last(i, after):
-        message = picked(order, own[i], past[i], after)
+    def pair_last(i, after, through=()):
+        message, *copied = picked(order, own[i], past[i], after, through)
         near[i] = swap(message)
-        return message
+        return message, *copied
 
     near[3] = swap(own[3])
     past[2] = turn(own[2])
     look_inside(0)
-    first_done = joined(order, own[1], near[1], chunks[1][1], (inside[0][0],))
-    second_done = pair_last(0, (first_done,))
-    (first_done,) = look_inside(1, (first_done,), (second_done,))
-    past[1] = turn(first_done)
-    look_inside(2, (), (first_done,))
-    second_done = pair_last(2, (inside[2][0],))
-    look_inside(3, (), (second_done,))
-    first_done = joined(order, own[3], near[3], chunks[3][1], (inside[3][0],))
-    past[3] = ahead(first_done)
+    both = joined(order, own[1], near[1], chunks[1][1], (inside[0][0],))
+    message, both = pair_last(0, (), (both,))
+    past[1] = turn(both)
+    look_inside(1, (), (message,))
+    look_inside(2, (), (inside[1][0],))
+    both = joined(order, own[3], near[3], chunks[3][1], (inside[2][0],))
+    message, both = pair_last(2, (), (both,))
+    past[3] = ahead(both)
+    look_inside(3, (), (message,))
 
     if reach > 2:
         for i, (_, many) in enumerate(chunks):
@@ -455,7 +475,7 @@
     for group in ((0, 1), (2, 3)):
         groups = [(*chunks[i], ("span", "pair")[i % 2]) for i in group]
         arrays = [x for i in group for x in (own[i], near[i], past[i], *inside[i])]
-        result = finish(order, seg, heads, groups, arrays, result, (first_done,))
+        result = finish(order, seg, heads, groups, arrays, result, (inside[3][0],))
     return tuple(result)
 
 

time: 33.7 us -> 32.5 us (0.964)
  starting transfers between devices: 11.1 us -> 10.5 us
  waiting for transfers between devices: 5.08 us -> 4.56 us
    ppermute x4, waiting for transfers between devices: 0.99 us -> 0.01 us  [shards(): swap = lambda x: lax.ppermute(x, 'seq', [(c, c ^ 1) for c in range(count)])]
    ppermute x1, starting transfers between devices: 3.11 us -> 2.29 us  [shards(): lax.ppermute(x, 'seq', [(c, c + 2) for c in range(count - 2)])]
    ppermute x3, starting transfers between devices: 3.3 us -> 3.78 us  [shards(): lax.ppermute(x, 'seq', [(c, (c + 2) % count) for c in range(count)])]
    ppermute x3, waiting for transfers between devices: 3.83 us -> 4.2 us  [shards(): lax.ppermute(x, 'seq', [(c, (c + 2) % count) for c in range(count)])]
  transfers between devices with their start and end apart: 8 -> 8, of which waited for: 5 -> 3; matrix products, arithmetic and copies ran while one was open for 0% -> 0% of each run, Pallas kernels for 36% -> 37%
where the time goes in v3:
time: 32.5 us; the launch traced here: 32.3 us
  Pallas kernels  16.5 us (51%)
  starting transfers between devices  10.5 us (32%)
  waiting for transfers between devices  4.56 us (14%)
  between operations  0.76 us (2%)
    pallas_call x4, Pallas kernels, intra(): pl.pallas_call(functools.partial(intra_kernel, first, heads, len(through)...  6.25 us
    pallas_call x2, Pallas kernels, finish(): pl.pallas_call(functools.partial(final_kernel, groups, unread), in_specs=...  4.97 us
    ppermute x4, starting transfers between devices, shards(): swap = lambda x: lax.ppermute(x, 'seq', [(c, c ^ 1) for c in range(count)])  4.4 us
    ppermute x3, waiting for transfers between devices, shards(): lax.ppermute(x, 'seq', [(c, (c + 2) % count) for c in range(count)])  4.2 us
    ppermute x3, starting transfers between devices, shards(): lax.ppermute(x, 'seq', [(c, (c + 2) % count) for c in range(count)])  3.78 us
    pallas_call x1, Pallas kernels, rest_messages(): pl.pallas_call(functools.partial(rest_kernel, chunks, done), in_specs=[pl...  2.97 us
    ppermute x1, starting transfers between devices, shards(): lax.ppermute(x, 'seq', [(c, c + 2) for c in range(count - 2)])  2.29 us
    pallas_call x1, Pallas kernels, first_messages(): pl.pallas_call(functools.partial(first_kernel, heads, chunks), in_specs=[...  2.12 us
  transfers between devices with their start and end apart: 8, of which 3 were waited for; matrix products, arithmetic and copies ran while one was open for 0% of the time, Pallas kernels for 37%

profile of v3, /device:TPU:0, one launch (start us, length us, event | category | flops | bytes accessed | tf_op | source)
XLA Modules:
  0.0 32.3 jit_solution(14629114585044103264)
XLA Ops:
  0.6 2.1 %first_messages.1 = (f32[520,128]{1,0:T(8,128)S(1)}, f32[520,128]{1,0:T(8,128)S(1)}, f32[16,512]{1,0:T(8,128)S(1)}, f32[16,512]{1,0:T(8,128)S(1)}, s32[1,512]{1,...) custom-call(s32[1]{0:T(128)} %bitcast.order_ref.refs_0_, ...), custom_call_target="tpu_custom_call" | custom-call | flops 1 | bytes 1 | tf_op jit(solution)/shard_map/first_messages/pallas_call | solution.py:105
  2.8 3.0 %collective-permute-start.3 = (f32[520,128]{1,0:T(8,128)S(1)}, f32[520,128]{1,0:T(8,128)S(1)}, u32[]{:S(2)}, u32[]{:S(2)}) collective-permute-start(f32[520,128]{1,0:T(8,128)S(1)} %get-tuple-element.59.refs_1_.rest_7_), channel_id=1, source_target_pairs={{0,2},{2,0},{4,6},{6,4},{8,10},{10,8},{12,14},{14,12},{1,3},{3,1},... | collective-permute-start | bytes 798728 | tf_op jit(solution)/shard_map/ppermute | solution.py:406
  5.8 1.6 %collective-permute-start.2 = (f32[520,128]{1,0:T(8,128)S(1)}, f32[520,128]{1,0:T(8,128)S(1)}, u32[]{:S(2)}, u32[]{:S(2)}) collective-permute-start(f32[520,128]{1,0:T(8,128)S(1)} %get-tuple-element.58.even_ref.rest_0_), channel_id=1, source_target_pairs={{0,4},{2,6},{4,8},{6,10},{8,12},{10,14},{12,0},{14,2},{1,5},{3,7},... | collective-permute-start | bytes 798728 | tf_op jit(solution)/shard_map/ppermute | solution.py:407
  7.4 3.0 %rest_messages.1 = (f32[520,128]{1,0:T(8,128)S(1)}, f32[520,128]{1,0:T(8,128)S(1)}, f32[512,512]{1,0:T(8,128)S(1)}, bf16[512,512]{1,0:T(8,128)(2,1)S(1)}, bf16[5...) custom-call(s32[1,512]{1,0:T(1,128)S(1)} %get-tuple-element.44.seg_r, ...), custom_call_target="tpu_custom_call" | custom-call | flops 1 | bytes 1 | tf_op jit(solution)/shard_map/rest_messages/pallas_call | solution.py:160
  10.3 0.6 %collective-permute-start.1 = (f32[520,128]{1,0:T(8,128)S(1)}, f32[520,128]{1,0:T(8,128)S(1)}, u32[]{:S(2)}, u32[]{:S(2)}) collective-permute-start(f32[520,128]{1,0:T(8,128)S(1)} %get-tuple-element.48.refs_1_.rest_7_), channel_id=1, source_target_pairs={{0,2},{2,0},{4,6},{6,4},{8,10},{10,8},{12,14},{14,12},{1,3},{3,1},... | collective-permute-start | bytes 798728 | tf_op jit(solution)/shard_map/ppermute | solution.py:406
  10.9 1.6 %collective-permute-start = (f32[520,128]{1,0:T(8,128)S(1)}, f32[520,128]{1,0:T(8,128)S(1)}, u32[]{:S(2)}, u32[]{:S(2)}) collective-permute-start(f32[520,128]{1,0:T(8,128)S(1)} %get-tuple-element.47.even_ref.rest_0_), channel_id=1, source_target_pairs={{0,4},{2,6},{4,8},{6,10},{8,12},{10,14},{12,0},{14,2},{1,5},{3,7},... | collective-permute-start | bytes 798728 | tf_op jit(solution)/shard_map/ppermute | solution.py:407
  12.5 1.6 %intra_span.4 = (f32[512,512]{1,0:T(8,128)S(1)}, f32[512,512]{1,0:T(8,128)S(1)}, f32[512,512]{1,0:T(8,128)S(1)}) custom-call(f32[512,512]{1,0:T(8,128)S(1)} %get-tuple-element.49.mask_ref, f32[16,512]{1,0:T(8,128)S(1)} %get-tuple-element.45.a_ref, f32[1,2048]{1,0:T(1,128)S(1)} %bitcast.4, bf16[512,512]{1,0:T(8,128)(2,1)S(1)} %get-tuple-element.60.q_ref.rest_6_, ...), custom_call_target="tpu_custom_call" | custom-call | flops 1 | bytes 1 | tf_op jit(solution)/shard_map/intra_span/pallas_call | solution.py:289
  14.1 0.0 collective-permute-done.3.refs_2_.rest_8_
  14.1 0.1 join_windows.2.refs_0_
  14.1 2.4 %collective-permute-done.2.odd_ref.rest_2_ = f32[520,128]{1,0:T(8,128)S(1)} collective-permute-done((f32[520,128]{1,0:T(8,128)S(1)}, f32[520,128]{1,0:T(8,128)S(1)}, u32[]{:S(2)}, u32[]{:S(2)}) %collective-permute-start.2) | collective-permute-done | bytes 266272 | tf_op jit(solution)/shard_map/ppermute | solution.py:407
  16.6 0.1 collective-permute-start.6
  16.7 0.6 %collective-permute-start.7 = (f32[520,128]{1,0:T(8,128)S(1)}, f32[520,128]{1,0:T(8,128)S(1)}, u32[]{:S(2)}, u32[]{:S(2)}) collective-permute-start(f32[520,128]{1,0:T(8,128)S(1)} %get-tuple-element.81), channel_id=1, source_target_pairs={{0,4},{2,6},{4,8},{6,10},{8,12},{10,14},{12,0},{14,2},{1,5},{3,7},... | collective-permute-start | bytes 798728 | tf_op jit(solution)/shard_map/ppermute | solution.py:407
  17.3 1.5 %intra_span.5 = (f32[512,512]{1,0:T(8,128)S(1)}, f32[512,512]{1,0:T(8,128)S(1)}, f32[512,512]{1,0:T(8,128)S(1)}) custom-call(f32[512,512]{1,0:T(8,128)S(1)} %get-tuple-element.49.mask_ref, f32[16,512]{1,0:T(8,128)S(1)} %get-tuple-element.45.a_ref, f32[1,2048]{1,0:T(1,128)S(1)} %bitcast.5, bf16[512,512]{1,0:T(8,128)(2,1)S(1)} %get-tuple-element.54.q_ref.rest_13_, ...), custom_call_target="tpu_custom_call" | custom-call | flops 1 | bytes 1 | tf_op jit(solution)/shard_map/intra_span/pallas_call | solution.py:289
  18.9 1.6 %intra_span.6 = (f32[512,512]{1,0:T(8,128)S(1)}, f32[512,512]{1,0:T(8,128)S(1)}, f32[512,512]{1,0:T(8,128)S(1)}) custom-call(f32[512,512]{1,0:T(8,128)S(1)} %get-tuple-element.49.mask_ref, f32[16,512]{1,0:T(8,128)S(1)} %get-tuple-element.45.a_ref, f32[1,2048]{1,0:T(1,128)S(1)} %bitcast.6, bf16[512,512]{1,0:T(8,128)(2,1)S(1)} %get-tuple-element.50.q_ref.rest_6_, ...), custom_call_target="tpu_custom_call" | custom-call | flops 1 | bytes 1 | tf_op jit(solution)/shard_map/intra_span/pallas_call | solution.py:289
  20.5 0.0 collective-permute-done.1.refs_2_.rest_8_
  20.5 0.1 join_windows.3.refs_0_
  20.5 1.8 %collective-permute-done.odd_ref.rest_2_ = f32[520,128]{1,0:T(8,128)S(1)} collective-permute-done((f32[520,128]{1,0:T(8,128)S(1)}, f32[520,128]{1,0:T(8,128)S(1)}, u32[]{:S(2)}, u32[]{:S(2)}) %collective-permute-start) | collective-permute-done | bytes 266272 | tf_op jit(solution)/shard_map/ppermute | solution.py:407
  22.3 0.7 %collective-permute-start.4 = (f32[520,128]{1,0:T(8,128)S(1)}, f32[520,128]{1,0:T(8,128)S(1)}, u32[]{:S(2)}, u32[]{:S(2)}) collective-permute-start(f32[520,128]{1,0:T(8,128)S(1)} %get-tuple-element.68.refs_0_), channel_id=1, source_target_pairs={{0,2},{2,0},{4,6},{6,4},{8,10},{10,8},{12,14},{14,12},{1,3},{3,1},... | collective-permute-start | bytes 798728 | tf_op jit(solution)/shard_map/ppermute | solution.py:406
  23.1 2.3 %collective-permute-start.5 = (f32[520,128]{1,0:T(8,128)S(1)}, f32[520,128]{1,0:T(8,128)S(1)}, u32[]{:S(2)}, u32[]{:S(2)}) collective-permute-start(f32[520,128]{1,0:T(8,128)S(1)} %get-tuple-element.71), channel_id=1, source_target_pairs={{0,4},{2,6},{4,8},{6,10},{8,12},{10,14},{1,5},{3,7},{5,9},{7,11},{... | collective-permute-start | bytes 798728 | tf_op jit(solution)/shard_map/ppermute | solution.py:408
  25.4 1.6 %intra_span.7 = (f32[512,512]{1,0:T(8,128)S(1)}, f32[512,512]{1,0:T(8,128)S(1)}, f32[512,512]{1,0:T(8,128)S(1)}) custom-call(f32[512,512]{1,0:T(8,128)S(1)} %get-tuple-element.49.mask_ref, f32[16,512]{1,0:T(8,128)S(1)} %get-tuple-element.45.a_ref, f32[1,2048]{1,0:T(1,128)S(1)} %bitcast.7, bf16[512,512]{1,0:T(8,128)(2,1)S(1)} %get-tuple-element.72.q_ref.rest_13_, ...), custom_call_target="tpu_custom_call" | custom-call | flops 1 | bytes 1 | tf_op jit(solution)/shard_map/intra_span/pallas_call | solution.py:289
  26.9 0.0 collective-permute-done.6.rest_1_
  27.0 2.5 %finish.2 = (bf16[512,2048]{1,0:T(8,128)(2,1)}, f32[1,16,128,128]{3,2,1,0:T(8,128)}) custom-call(s32[1]{0:T(128)} %bitcast.order_ref.refs_0_, s32[1,512]{1,0:T(1,128)S(1)} %get-tuple-element.44.seg_ref, f32[520,128]{1,0:T(8,128)S(1)} %get-tuple-element.58.even_ref.rest_0_, f32[520,128]{1,0:T(8,128)S(1)} %collective-permute-done.6.rest_1_, ...), custom_call_target="tpu_custom_call" | custom-call | flops 1 | bytes 1 | tf_op jit(solution)/shard_map/finish/pallas_call | solution.py:377
  29.5 0.3 %collective-permute-done.5.rest_9_ = f32[520,128]{1,0:T(8,128)S(1)} collective-permute-done((f32[520,128]{1,0:T(8,128)S(1)}, f32[520,128]{1,0:T(8,128)S(1)}, u32[]{:S(2)}, u32[]{:S(2)}) %collective-permute-start.5) | collective-permute-done | bytes 266272 | tf_op jit(solution)/shard_map/ppermute | solution.py:408
  29.8 2.5 %finish.3 = (bf16[512,2048]{1,0:T(8,128)(2,1)}, f32[1,16,128,128]{3,2,1,0:T(8,128)}) custom-call(s32[1]{0:T(128)} %bitcast.order_ref.refs_0_, s32[1,512]{1,0:T(1,128)S(1)} %get-tuple-element.44.seg_ref, f32[520,128]{1,0:T(8,128)S(1)} %get-tuple-element.47.even_ref.rest_0_, ...), custom_call_target="tpu_custom_call", output_to_operand_aliasing={{0}: (16, {}), {1}: (17, {})} | custom-call | flops 1 | bytes 1 | tf_op jit(solution)/shard_map/finish/pallas_call | solution.py:377
  (6 shorter events, 0.1 us)
Async XLA Ops:
  2.8 11.3 %collective-permute-start.3 = (f32[520,128]{1,0:T(8,128)S(1)}, f32[520,128]{1,0:T(8,128)S(1)}, u32[]{:S(2)}, u32[]{:S(2)}) collective-permute-start(f32[520,128]{1,0:T(8,128)S(1)} %get-tuple-element.59.refs_1_.rest_7_), channel_id=1, source_target_pairs={{0,2},{2,0},{4,6},{6,4},{8,10},{10,8},{12,14},{14,12},{1,3},{3,1},... | collective-permute-start | bytes 798728 | tf_op jit(solution)/shard_map/ppermute | solution.py:406
  5.8 10.8 %collective-permute-start.2 = (f32[520,128]{1,0:T(8,128)S(1)}, f32[520,128]{1,0:T(8,128)S(1)}, u32[]{:S(2)}, u32[]{:S(2)}) collective-permute-start(f32[520,128]{1,0:T(8,128)S(1)} %get-tuple-element.58.even_ref.rest_0_), channel_id=1, source_target_pairs={{0,4},{2,6},{4,8},{6,10},{8,12},{10,14},{12,0},{14,2},{1,5},{3,7},... | collective-permute-start | bytes 798728 | tf_op jit(solution)/shard_map/ppermute | solution.py:407
  7.4 5.2 %copy-start = (f32[2048]{0:T(1024)S(1)}, f32[2048]{0:T(1024)}, u32[]{:S(2)}) copy-start(f32[2048]{0:T(1024)} %param.15) | copy-start | bytes 24580
  10.3 10.1 %collective-permute-start.1 = (f32[520,128]{1,0:T(8,128)S(1)}, f32[520,128]{1,0:T(8,128)S(1)}, u32[]{:S(2)}, u32[]{:S(2)}) collective-permute-start(f32[520,128]{1,0:T(8,128)S(1)} %get-tuple-element.48.refs_1_.rest_7_), channel_id=1, source_target_pairs={{0,2},{2,0},{4,6},{6,4},{8,10},{10,8},{12,14},{14,12},{1,3},{3,1},... | collective-permute-start | bytes 798728 | tf_op jit(solution)/shard_map/ppermute | solution.py:406
  10.9 11.4 %collective-permute-start = (f32[520,128]{1,0:T(8,128)S(1)}, f32[520,128]{1,0:T(8,128)S(1)}, u32[]{:S(2)}, u32[]{:S(2)}) collective-permute-start(f32[520,128]{1,0:T(8,128)S(1)} %get-tuple-element.47.even_ref.rest_0_), channel_id=1, source_target_pairs={{0,4},{2,6},{4,8},{6,10},{8,12},{10,14},{12,0},{14,2},{1,5},{3,7},... | collective-permute-start | bytes 798728 | tf_op jit(solution)/shard_map/ppermute | solution.py:407
  16.6 10.3 %collective-permute-start.6 = (f32[520,128]{1,0:T(8,128)S(1)}, f32[520,128]{1,0:T(8,128)S(1)}, u32[]{:S(2)}, u32[]{:S(2)}) collective-permute-start(f32[520,128]{1,0:T(8,128)S(1)} %get-tuple-element.65.refs_0_), channel_id=1, source_target_pairs={{0,2},{2,0},{4,6},{6,4},{8,10},{10,8},{12,14},{14,12},{1,3},{3,1},... | collective-permute-start | bytes 798728 | tf_op jit(solution)/shard_map/ppermute | solution.py:406
  16.7 10.2 %collective-permute-start.7 = (f32[520,128]{1,0:T(8,128)S(1)}, f32[520,128]{1,0:T(8,128)S(1)}, u32[]{:S(2)}, u32[]{:S(2)}) collective-permute-start(f32[520,128]{1,0:T(8,128)S(1)} %get-tuple-element.81), channel_id=1, source_target_pairs={{0,4},{2,6},{4,8},{6,10},{8,12},{10,14},{12,0},{14,2},{1,5},{3,7},... | collective-permute-start | bytes 798728 | tf_op jit(solution)/shard_map/ppermute | solution.py:407
  22.3 7.2 %collective-permute-start.4 = (f32[520,128]{1,0:T(8,128)S(1)}, f32[520,128]{1,0:T(8,128)S(1)}, u32[]{:S(2)}, u32[]{:S(2)}) collective-permute-start(f32[520,128]{1,0:T(8,128)S(1)} %get-tuple-element.68.refs_0_), channel_id=1, source_target_pairs={{0,2},{2,0},{4,6},{6,4},{8,10},{10,8},{12,14},{14,12},{1,3},{3,1},... | collective-permute-start | bytes 798728 | tf_op jit(solution)/shard_map/ppermute | solution.py:406
  23.1 6.8 %collective-permute-start.5 = (f32[520,128]{1,0:T(8,128)S(1)}, f32[520,128]{1,0:T(8,128)S(1)}, u32[]{:S(2)}, u32[]{:S(2)}) collective-permute-start(f32[520,128]{1,0:T(8,128)S(1)} %get-tuple-element.71), channel_id=1, source_target_pairs={{0,4},{2,6},{4,8},{6,10},{8,12},{10,14},{1,5},{3,7},{5,9},{7,11},{... | collective-permute-start | bytes 798728 | tf_op jit(solution)/shard_map/ppermute | solution.py:408

commit v4 on v3

--- a/solution.py
+++ b/solution.py
@@ -43,12 +43,11 @@
 
 def first_kernel(heads, chunks, order_ref, seg_hbm, exponent_hbm, keep_hbm, k_hbm, v_hbm, *refs):
     number = len(chunks)
-    messages, refs = refs[:number], refs[number:]
-    (a_ref, w_ref, seg_ref), refs = refs[:3], refs[3:]
+    (msg_ref, a_ref, w_ref, seg_ref), refs = refs[:4], refs[4:]
     k_refs, v_refs, refs = refs[:number], refs[number : 2 * number], refs[2 * number :]
     exponent_ref, keep_ref, sems = refs
     tokens = seg_ref.shape[1]
-    size = messages[0].shape[1]
+    size = msg_ref.shape[1]
     pairs = [(keep_hbm, keep_ref), (exponent_hbm, exponent_ref), (seg_hbm, seg_ref)]
     for i, (first, many) in enumerate(chunks):
         wide = pl.ds(first * size, many * size)
@@ -56,8 +55,8 @@
     copies = [pltpu.make_async_copy(*pair, sems.at[i]) for i, pair in enumerate(pairs)]
     for copy in copies:
         copy.start()
-    earlier = lax.broadcasted_iota(jnp.int32, (128, 128), 0)
-    later = lax.broadcasted_iota(jnp.int32, (128, 128), 1)
+    earlier = lax.broadcasted_iota(jnp.int32, (tokens, tokens), 0)
+    later = lax.broadcasted_iota(jnp.int32, (tokens, tokens), 1)
     upper = jnp.where(earlier <= later, 1.0, 0.0).astype(BF16)
     across = lax.broadcasted_iota(jnp.int32, (heads, heads), 1)
     down = lax.broadcasted_iota(jnp.int32, (heads, heads), 0)
@@ -66,39 +65,35 @@
     spread = jnp.broadcast_to(exponent_ref[...], (heads, heads))
     exponent = jnp.sum(jnp.where(across == down, spread, 0).astype(F32), axis=1, keepdims=True)
     a = -jnp.exp2(-exponent) + jnp.log(keep_ref[...])
-    a = jnp.concatenate([a[:, i : i + 128] for i in range(0, tokens, 128)], axis=0)
     high = a.astype(BF16)
     rest = a - high.astype(F32)
     middle = rest.astype(BF16)
     low = (rest - middle.astype(F32)).astype(BF16)
-    sums = [
-        lax.dot_general(part, upper, NN, preferred_element_type=F32) for part in (high, middle, low)
-    ]
-    sums = sums[0] + (sums[1] + sums[2])
-    blocks = [sums[i : i + heads] for i in range(0, sums.shape[0], heads)]
-    for i in range(1, len(blocks)):
-        blocks[i] = blocks[i] + blocks[i - 1][:, 127:]
-    cumulative = jnp.concatenate(blocks, axis=1)
+    parts = jnp.concatenate([high, middle, low], axis=0)
+    sums = lax.dot_general(parts, upper, NN, preferred_element_type=F32)
+    cumulative = sums[:heads] + (sums[heads : 2 * heads] + sums[2 * heads :])
     a_ref[...] = cumulative
     final = cumulative[:, tokens - 1 :]
     seg = seg_ref[...]
     last = seg[:, tokens - 1 :]
     w_ref[...] = jnp.where(seg == last, jnp.exp(final - cumulative), 0.0)
-    for i, (first, many) in enumerate(chunks):
-        copies[3 + 2 * i].wait()
-        copies[4 + 2 * i].wait()
-        finals = final[first : first + many]
-        put_message(messages[i], first, many, size, w_ref, finals, last, k_refs[i], v_refs[i])
+    for copy in copies[3:5]:
+        copy.wait()
+    first, many = chunks[0]
+    finals = final[first : first + many]
+    put_message(msg_ref, first, many, size, w_ref, finals, last, k_refs[0], v_refs[0])
+    for copy in copies[5:]:
+        copy.wait()
 
 
 def message_of(size, many):
     return pltpu.VMEM((many * size + meta_rows(many), size), F32)
 
 
-def first_messages(order, seg, exponent, keep, k, v, heads, chunks):
+def first_message(order, seg, exponent, keep, k, v, heads, chunks):
     tokens, size = k.shape[0], k.shape[1] // heads
     near = [pltpu.VMEM((tokens, many * size), BF16) for _, many in chunks]
-    shapes = [message_of(size, many) for _, many in chunks]
+    shapes = [message_of(size, chunks[0][1])]
     shapes += [pltpu.VMEM((heads, tokens), F32)] * 2 + [pltpu.VMEM((1, tokens), jnp.int32)]
     shapes += near + near
     number = len(chunks)
@@ -115,10 +110,29 @@
         ],
         compiler_params=pltpu.CompilerParams(vmem_limit_bytes=8 * MIB),
         cost_estimate=SHORT,
-        name="first_messages",
+        name="first_message",
     )(order, seg, exponent, keep, k, v)
-    messages, (a, w, seg), out = out[:number], out[number : number + 3], out[number + 3 :]
-    return messages, a, w, seg, out[:number], out[number:]
+    (message, a, w, seg), out = out[:4], out[4:]
+    return message, a, w, seg, out[:number], out[number:]
+
+
+def second_message(seg, a, w, k, v, first, heads):
+    tokens, size = k.shape[0], k.shape[1] // heads
+
+    def kernel(seg_ref, a_ref, w_ref, k_ref, v_ref, msg_ref):
+        final = a_ref[first : first + heads, tokens - 1 :]
+        last = seg_ref[:, tokens - 1 :]
+        put_message(msg_ref, first, heads, size, w_ref, final, last, k_ref, v_ref)
+
+    return pl.pallas_call(
+        kernel,
+        in_specs=[pl.BlockSpec(memory_space=pltpu.VMEM)] * 5,
+        out_specs=pl.BlockSpec(memory_space=pltpu.VMEM),
+        out_shape=message_of(size, heads),
+        compiler_params=pltpu.CompilerParams(vmem_limit_bytes=8 * MIB),
+        cost_estimate=SHORT,
+        name="second_message",
+    )(seg, a, w, k, v)
 
 
 def rest_kernel(chunks, done, seg_ref, a_ref, w_ref, q_hbm, k_hbm, v_hbm, g_hbm, *refs):
@@ -279,7 +293,7 @@
             o_ref[here, columns] = lax.dot_general(
                 probs, v_ref[upto, columns], NN, preferred_element_type=F32
             )
-        half = 0.5 * gain_ref[:, (first + j) * size : (first + j + 1) * size]
+        half = 0.5 * size**0.5 * gain_ref[:, (first + j) * size : (first + j + 1) * size]
         gate_ref[:, columns] = half + half * jnp.tanh(0.5 * g_ref[:, columns].astype(F32))
 
 
@@ -302,7 +316,7 @@
 def final_kernel(groups, unread, order_ref, seg_ref, *rest):
     number = len(groups)
     inputs, rest = rest[: 7 * number], rest[7 * number + unread :]
-    gated_hbm, snap_hbm, *scratch, sems = rest
+    gated_hbm, snap_hbm, *scratch, inter_ref, sems = rest
     place = order_ref[0]
     seg = seg_ref[...].astype(F32)
     copies, work = [], []
@@ -342,20 +356,21 @@
             work.append((i, j, first, heads, both, valid, (o_ref, gate_ref, decay_ref, q_ref)))
         send(snap_ref, snap_hbm.at[0, pl.ds(first, heads)])
 
-    for i, j, first, heads, both, valid, (o_ref, gate_ref, decay_ref, q_ref) in work:
+    for number, (i, j, first, heads, both, valid, arrays) in enumerate(work):
+        o_ref, gate_ref, decay_ref, q_ref = arrays
         gated_ref = scratch[2 * i]
         tokens, size = valid.shape
-        block = min(tokens, 256)
         columns = slice(j * size, (j + 1) * size)
-        for start in range(0, tokens, block):
-            here = slice(start, start + block)
-            q = q_ref[here, columns]
-            inter = lax.dot_general(
-                jnp.concatenate([q, q], axis=1), both, NN, preferred_element_type=F32
-            )
+        q = q_ref[:, columns]
+        inter_ref[number % 4] = lax.dot_general(
+            jnp.concatenate([q, q], axis=1), both, NN, preferred_element_type=F32
+        )
+        for start in range(0, tokens, 64):
+            here = slice(start, start + 64)
+            inter = inter_ref[number % 4, here, :]
             mixed = o_ref[here, columns] + inter * (decay_ref[here, columns] * valid[here])
-            mean_square = jnp.mean(mixed * mixed, axis=1, keepdims=True)
-            gated = mixed * lax.rsqrt(mean_square + 1e-06) * gate_ref[here, columns]
+            square = jnp.sum(mixed * mixed, axis=1, keepdims=True)
+            gated = mixed * lax.rsqrt(square + size * 1e-06) * gate_ref[here, columns]
             gated_ref[here, columns] = gated.astype(BF16)
         if j % 2 == 1 or j == heads - 1:
             begin = j - j % 2
@@ -384,7 +399,8 @@
             jax.ShapeDtypeStruct((tokens, total * size), BF16),
             jax.ShapeDtypeStruct((1, total, size, size), F32),
         ],
-        scratch_shapes=scratch + [pltpu.SemaphoreType.DMA((2 * total,))],
+        scratch_shapes=scratch
+        + [pltpu.VMEM((4, tokens, size), F32), pltpu.SemaphoreType.DMA((2 * total,))],
         input_output_aliases={2 + len(arrays) + i: i for i in range(len(so_far))},
         compiler_params=pltpu.CompilerParams(vmem_limit_bytes=12 * MIB),
         cost_estimate=SHORT,
@@ -408,9 +424,8 @@
     ahead = lambda x: lax.ppermute(x, "seq", [(c, c + 2) for c in range(count - 2)])
 
     half = heads // 2
-    small = half // 2
-    big = half - small
-    chunks = [(0, big), (half, big), (big, small), (half + big, small)]
+    even, odd = half // 2, half // 2
+    chunks = [(0, half - even), (half, half - odd), (half - even, even), (heads - odd, odd)]
 
     def widened(x, many, shift, window):
         while window < reach:
@@ -419,7 +434,7 @@
             shift, window = 2 * shift, 2 * window
         return x
 
-    own, a, w, seg, k_near, v_near = first_messages(
+    message, a, w, seg, k_near, v_near = first_message(
         order,
         far(segment.reshape(1, tokens)),
         far(decay_exponent.reshape(1, heads)),
@@ -427,10 +442,12 @@
         k,
         v,
         heads,
-        chunks[:2],
+        (chunks[1], chunks[0]),
     )
+    k_near, v_near = k_near[::-1], v_near[::-1]
     near, past, inside = {}, {}, {}
-    near[1] = swap(own[1])
+    near[1] = swap(message)
+    own = [second_message(seg, a, w, k_near[0], v_near[0], *chunks[0]), message]
     past[0] = turn(own[0])
     messages, mask, k_rest, v_rest, q_near, g_near = rest_messages(
         seg, a, w, q, k, v, g, chunks, 2

time: 32.5 us -> 32.3 us (level)
  Pallas kernels: 16.5 us -> 16 us
    pallas_call x2, Pallas kernels: 4.97 us -> 4.56 us  [finish(): pl.pallas_call(functools.partial(final_kernel, groups, unread), in_specs=...]
    pallas_call x1 -> x2, Pallas kernels: 2.12 us -> 2.05 us  [the longest x1 1.69 us: first_message(): pl.pallas_call(functools.partial(first_kernel, heads, chunks), in_specs=[...]
  transfers between devices with their start and end apart: 8 -> 8, of which waited for: 3 -> 4; matrix products, arithmetic and copies ran while one was open for 0% -> 0% of each run, Pallas kernels for 37% -> 37%
where the time goes in v4:
time: 32.3 us; the launch traced here: 32.1 us
  Pallas kernels  16 us (50%)
  starting transfers between devices  10.5 us (33%)
  waiting for transfers between devices  4.86 us (15%)
  between operations  0.77 us (2%)
    pallas_call x4, Pallas kernels, intra(): pl.pallas_call(functools.partial(intra_kernel, first, heads, len(through)...  6.2 us
    pallas_call x2, Pallas kernels, finish(): pl.pallas_call(functools.partial(final_kernel, groups, unread), in_specs=...  4.56 us
    ppermute x4, starting transfers between devices, shards(): swap = lambda x: lax.ppermute(x, 'seq', [(c, c ^ 1) for c in range(count)])  4.39 us
    ppermute x3, waiting for transfers between devices, shards(): lax.ppermute(x, 'seq', [(c, (c + 2) % count) for c in range(count)])  4.25 us
    ppermute x3, starting transfers between devices, shards(): lax.ppermute(x, 'seq', [(c, (c + 2) % count) for c in range(count)])  3.81 us
    pallas_call x1, Pallas kernels, rest_messages(): pl.pallas_call(functools.partial(rest_kernel, chunks, done), in_specs=[pl...  2.97 us
    ppermute x1, starting transfers between devices, shards(): lax.ppermute(x, 'seq', [(c, c + 2) for c in range(count - 2)])  2.29 us
    pallas_call x1, Pallas kernels, first_message(): pl.pallas_call(functools.partial(first_kernel, heads, chunks), in_specs=[...  1.69 us
  transfers between devices with their start and end apart: 8, of which 4 were waited for; matrix products, arithmetic and copies ran while one was open for 0% of the time, Pallas kernels for 37%

profile of v4, /device:TPU:0, one launch (start us, length us, event | category | flops | bytes accessed | tf_op | source)
XLA Modules:
  0.0 32.1 jit_solution(2144704402341892930)
XLA Ops:
  0.6 1.7 %first_message.1 = (f32[520,128]{1,0:T(8,128)S(1)}, f32[16,512]{1,0:T(8,128)S(1)}, f32[16,512]{1,0:T(8,128)S(1)}, s32[1,512]{1,0:T(1,128)S(1)}, bf16[512,512]{1,...) custom-call(s32[1]{0:T(128)} %bitcast.order_ref.refs_0_, ...), custom_call_target="tpu_custom_call" | custom-call | flops 1 | bytes 1 | tf_op jit(solution)/shard_map/first_message/pallas_call | solution.py:100
  2.3 3.0 %collective-permute-start.3 = (f32[520,128]{1,0:T(8,128)S(1)}, f32[520,128]{1,0:T(8,128)S(1)}, u32[]{:S(2)}, u32[]{:S(2)}) collective-permute-start(f32[520,128]{1,0:T(8,128)S(1)} %get-tuple-element.59.refs_1_.rest_7_), channel_id=1, source_target_pairs={{0,2},{2,0},{4,6},{6,4},{8,10},{10,8},{12,14},{14,12},{1,3},{3,1},... | collective-permute-start | bytes 798728 | tf_op jit(solution)/shard_map/ppermute | solution.py:422
  5.3 0.4 %second_message.1.even_ref.rest_0_ = f32[520,128]{1,0:T(8,128)S(1)} custom-call(s32[1,512]{1,0:T(1,128)S(1)} %get-tuple-element.43.seg_ref, f32[16,512]{1,0:T(8,128)S(1)} %get-tuple-element.44.a_ref, f32[16,512]{1,0:T(8,128)S(1)} %get-tuple-element.45.w_ref, bf16[512,512]{1,0:T(8,128)(2,1)S(1)} %get-tuple-element.57.k_ref, ...), custom_call_target="tpu_custom_call" | custom-call | flops 1 | bytes 1 | tf_op jit(solution)/shard_map/second_message/pallas_call | solution.py:127
  5.7 0.0 copy-start
  5.7 1.6 %collective-permute-start.2 = (f32[520,128]{1,0:T(8,128)S(1)}, f32[520,128]{1,0:T(8,128)S(1)}, u32[]{:S(2)}, u32[]{:S(2)}) collective-permute-start(f32[520,128]{1,0:T(8,128)S(1)} %second_message.1.even_ref.rest_0_), channel_id=1, source_target_pairs={{0,4},{2,6},{4,8},{6,10},{8,12},{10,14},{12,0},{14,2},{1,5},{3,7},... | collective-permute-start | bytes 798728 | tf_op jit(solution)/shard_map/ppermute | solution.py:423
  7.3 3.0 %rest_messages.1 = (f32[520,128]{1,0:T(8,128)S(1)}, f32[520,128]{1,0:T(8,128)S(1)}, f32[512,512]{1,0:T(8,128)S(1)}, bf16[512,512]{1,0:T(8,128)(2,1)S(1)}, bf16[5...) custom-call(s32[1,512]{1,0:T(1,128)S(1)} %get-tuple-element.43.seg_r, ...), custom_call_target="tpu_custom_call" | custom-call | flops 1 | bytes 1 | tf_op jit(solution)/shard_map/rest_messages/pallas_call | solution.py:174
  10.3 0.6 %collective-permute-start.1 = (f32[520,128]{1,0:T(8,128)S(1)}, f32[520,128]{1,0:T(8,128)S(1)}, u32[]{:S(2)}, u32[]{:S(2)}) collective-permute-start(f32[520,128]{1,0:T(8,128)S(1)} %get-tuple-element.47.refs_1_.rest_7_), channel_id=1, source_target_pairs={{0,2},{2,0},{4,6},{6,4},{8,10},{10,8},{12,14},{14,12},{1,3},{3,1},... | collective-permute-start | bytes 798728 | tf_op jit(solution)/shard_map/ppermute | solution.py:422
  10.9 1.6 %collective-permute-start = (f32[520,128]{1,0:T(8,128)S(1)}, f32[520,128]{1,0:T(8,128)S(1)}, u32[]{:S(2)}, u32[]{:S(2)}) collective-permute-start(f32[520,128]{1,0:T(8,128)S(1)} %get-tuple-element.46.even_ref.rest_0_), channel_id=1, source_target_pairs={{0,4},{2,6},{4,8},{6,10},{8,12},{10,14},{12,0},{14,2},{1,5},{3,7},... | collective-permute-start | bytes 798728 | tf_op jit(solution)/shard_map/ppermute | solution.py:423
  12.5 1.5 %intra_span.4 = (f32[512,512]{1,0:T(8,128)S(1)}, f32[512,512]{1,0:T(8,128)S(1)}, f32[512,512]{1,0:T(8,128)S(1)}) custom-call(f32[512,512]{1,0:T(8,128)S(1)} %get-tuple-element.48.mask_ref, f32[16,512]{1,0:T(8,128)S(1)} %get-tuple-element.44.a_ref, f32[1,2048]{1,0:T(1,128)S(1)} %bitcast.4, bf16[512,512]{1,0:T(8,128)(2,1)S(1)} %get-tuple-element.60.q_ref.rest_6_, ...), custom_call_target="tpu_custom_call" | custom-call | flops 1 | bytes 1 | tf_op jit(solution)/shard_map/intra_span/pallas_call | solution.py:303
  14.1 0.1 join_windows.2.refs_0_
  14.1 2.5 %collective-permute-done.2.odd_ref.rest_2_ = f32[520,128]{1,0:T(8,128)S(1)} collective-permute-done((f32[520,128]{1,0:T(8,128)S(1)}, f32[520,128]{1,0:T(8,128)S(1)}, u32[]{:S(2)}, u32[]{:S(2)}) %collective-permute-start.2) | collective-permute-done | bytes 266272 | tf_op jit(solution)/shard_map/ppermute | solution.py:423
  16.6 0.1 collective-permute-start.6
  16.7 0.6 %collective-permute-start.7 = (f32[520,128]{1,0:T(8,128)S(1)}, f32[520,128]{1,0:T(8,128)S(1)}, u32[]{:S(2)}, u32[]{:S(2)}) collective-permute-start(f32[520,128]{1,0:T(8,128)S(1)} %get-tuple-element.79), channel_id=1, source_target_pairs={{0,4},{2,6},{4,8},{6,10},{8,12},{10,14},{12,0},{14,2},{1,5},{3,7},... | collective-permute-start | bytes 798728 | tf_op jit(solution)/shard_map/ppermute | solution.py:423
  17.3 1.6 %intra_span.5 = (f32[512,512]{1,0:T(8,128)S(1)}, f32[512,512]{1,0:T(8,128)S(1)}, f32[512,512]{1,0:T(8,128)S(1)}) custom-call(f32[512,512]{1,0:T(8,128)S(1)} %get-tuple-element.48.mask_ref, f32[16,512]{1,0:T(8,128)S(1)} %get-tuple-element.44.a_ref, f32[1,2048]{1,0:T(1,128)S(1)} %bitcast.5, bf16[512,512]{1,0:T(8,128)(2,1)S(1)} %get-tuple-element.53.q_ref.rest_13_, ...), custom_call_target="tpu_custom_call" | custom-call | flops 1 | bytes 1 | tf_op jit(solution)/shard_map/intra_span/pallas_call | solution.py:303
  18.9 1.6 %intra_span.6 = (f32[512,512]{1,0:T(8,128)S(1)}, f32[512,512]{1,0:T(8,128)S(1)}, f32[512,512]{1,0:T(8,128)S(1)}) custom-call(f32[512,512]{1,0:T(8,128)S(1)} %get-tuple-element.48.mask_ref, f32[16,512]{1,0:T(8,128)S(1)} %get-tuple-element.44.a_ref, f32[1,2048]{1,0:T(1,128)S(1)} %bitcast.6, bf16[512,512]{1,0:T(8,128)(2,1)S(1)} %get-tuple-element.49.q_ref.rest_6_, ...), custom_call_target="tpu_custom_call" | custom-call | flops 1 | bytes 1 | tf_op jit(solution)/shard_map/intra_span/pallas_call | solution.py:303
  20.4 0.1 join_windows.3.refs_0_
  20.5 1.8 %collective-permute-done.odd_ref.rest_2_ = f32[520,128]{1,0:T(8,128)S(1)} collective-permute-done((f32[520,128]{1,0:T(8,128)S(1)}, f32[520,128]{1,0:T(8,128)S(1)}, u32[]{:S(2)}, u32[]{:S(2)}) %collective-permute-start) | collective-permute-done | bytes 266272 | tf_op jit(solution)/shard_map/ppermute | solution.py:423
  22.3 0.7 %collective-permute-start.4 = (f32[520,128]{1,0:T(8,128)S(1)}, f32[520,128]{1,0:T(8,128)S(1)}, u32[]{:S(2)}, u32[]{:S(2)}) collective-permute-start(f32[520,128]{1,0:T(8,128)S(1)} %get-tuple-element.66.refs_0_), channel_id=1, source_target_pairs={{0,2},{2,0},{4,6},{6,4},{8,10},{10,8},{12,14},{14,12},{1,3},{3,1},... | collective-permute-start | bytes 798728 | tf_op jit(solution)/shard_map/ppermute | solution.py:422
  23.1 2.3 %collective-permute-start.5 = (f32[520,128]{1,0:T(8,128)S(1)}, f32[520,128]{1,0:T(8,128)S(1)}, u32[]{:S(2)}, u32[]{:S(2)}) collective-permute-start(f32[520,128]{1,0:T(8,128)S(1)} %get-tuple-element.69), channel_id=1, source_target_pairs={{0,4},{2,6},{4,8},{6,10},{8,12},{10,14},{1,5},{3,7},{5,9},{7,11},{... | collective-permute-start | bytes 798728 | tf_op jit(solution)/shard_map/ppermute | solution.py:424
  25.3 1.5 %intra_span.7 = (f32[512,512]{1,0:T(8,128)S(1)}, f32[512,512]{1,0:T(8,128)S(1)}, f32[512,512]{1,0:T(8,128)S(1)}) custom-call(f32[512,512]{1,0:T(8,128)S(1)} %get-tuple-element.48.mask_ref, f32[16,512]{1,0:T(8,128)S(1)} %get-tuple-element.44.a_ref, f32[1,2048]{1,0:T(1,128)S(1)} %bitcast.7, bf16[512,512]{1,0:T(8,128)(2,1)S(1)} %get-tuple-element.70.q_ref.rest_13_, ...), custom_call_target="tpu_custom_call" | custom-call | flops 1 | bytes 1 | tf_op jit(solution)/shard_map/intra_span/pallas_call | solution.py:303
  26.9 2.3 %finish.2 = (bf16[512,2048]{1,0:T(8,128)(2,1)}, f32[1,16,128,128]{3,2,1,0:T(8,128)}) custom-call(s32[1]{0:T(128)} %bitcast.order_ref.refs_0_, s32[1,512]{1,0:T(1,128)S(1)} %get-tuple-element.43.seg_ref, f32[520,128]{1,0:T(8,128)S(1)} %second_message.1.even_ref.rest_0_, f32[520,128]{1,0:T(8,128)S(1)} %collective-permute-done.6.rest_1_, ...), custom_call_target="tpu_custom_call" | custom-call | flops 1 | bytes 1 | tf_op jit(solution)/shard_map/finish/pallas_call | solution.py:392
  29.2 0.1 collective-permute-done.4.rest_1_
  29.4 0.5 %collective-permute-done.5.rest_9_ = f32[520,128]{1,0:T(8,128)S(1)} collective-permute-done((f32[520,128]{1,0:T(8,128)S(1)}, f32[520,128]{1,0:T(8,128)S(1)}, u32[]{:S(2)}, u32[]{:S(2)}) %collective-permute-start.5) | collective-permute-done | bytes 266272 | tf_op jit(solution)/shard_map/ppermute | solution.py:424
  29.8 2.3 %finish.3 = (bf16[512,2048]{1,0:T(8,128)(2,1)}, f32[1,16,128,128]{3,2,1,0:T(8,128)}) custom-call(s32[1]{0:T(128)} %bitcast.order_ref.refs_0_, s32[1,512]{1,0:T(1,128)S(1)} %get-tuple-element.43.seg_ref, f32[520,128]{1,0:T(8,128)S(1)} %get-tuple-element.46.even_ref.rest_0_, ...), custom_call_target="tpu_custom_call", output_to_operand_aliasing={{0}: (16, {}), {1}: (17, {})} | custom-call | flops 1 | bytes 1 | tf_op jit(solution)/shard_map/finish/pallas_call | solution.py:392
  (7 shorter events, 0.1 us)
Async XLA Ops:
  2.3 11.7 %collective-permute-start.3 = (f32[520,128]{1,0:T(8,128)S(1)}, f32[520,128]{1,0:T(8,128)S(1)}, u32[]{:S(2)}, u32[]{:S(2)}) collective-permute-start(f32[520,128]{1,0:T(8,128)S(1)} %get-tuple-element.59.refs_1_.rest_7_), channel_id=1, source_target_pairs={{0,2},{2,0},{4,6},{6,4},{8,10},{10,8},{12,14},{14,12},{1,3},{3,1},... | collective-permute-start | bytes 798728 | tf_op jit(solution)/shard_map/ppermute | solution.py:422
  5.7 6.8 %copy-start = (f32[2048]{0:T(1024)S(1)}, f32[2048]{0:T(1024)}, u32[]{:S(2)}) copy-start(f32[2048]{0:T(1024)} %param.15) | copy-start | bytes 24580
  5.7 10.9 %collective-permute-start.2 = (f32[520,128]{1,0:T(8,128)S(1)}, f32[520,128]{1,0:T(8,128)S(1)}, u32[]{:S(2)}, u32[]{:S(2)}) collective-permute-start(f32[520,128]{1,0:T(8,128)S(1)} %second_message.1.even_ref.rest_0_), channel_id=1, source_target_pairs={{0,4},{2,6},{4,8},{6,10},{8,12},{10,14},{12,0},{14,2},{1,5},{3,7},... | collective-permute-start | bytes 798728 | tf_op jit(solution)/shard_map/ppermute | solution.py:423
  10.3 10.1 %collective-permute-start.1 = (f32[520,128]{1,0:T(8,128)S(1)}, f32[520,128]{1,0:T(8,128)S(1)}, u32[]{:S(2)}, u32[]{:S(2)}) collective-permute-start(f32[520,128]{1,0:T(8,128)S(1)} %get-tuple-element.47.refs_1_.rest_7_), channel_id=1, source_target_pairs={{0,2},{2,0},{4,6},{6,4},{8,10},{10,8},{12,14},{14,12},{1,3},{3,1},... | collective-permute-start | bytes 798728 | tf_op jit(solution)/shard_map/ppermute | solution.py:422
  10.9 11.4 %collective-permute-start = (f32[520,128]{1,0:T(8,128)S(1)}, f32[520,128]{1,0:T(8,128)S(1)}, u32[]{:S(2)}, u32[]{:S(2)}) collective-permute-start(f32[520,128]{1,0:T(8,128)S(1)} %get-tuple-element.46.even_ref.rest_0_), channel_id=1, source_target_pairs={{0,4},{2,6},{4,8},{6,10},{8,12},{10,14},{12,0},{14,2},{1,5},{3,7},... | collective-permute-start | bytes 798728 | tf_op jit(solution)/shard_map/ppermute | solution.py:423
  16.6 10.3 %collective-permute-start.6 = (f32[520,128]{1,0:T(8,128)S(1)}, f32[520,128]{1,0:T(8,128)S(1)}, u32[]{:S(2)}, u32[]{:S(2)}) collective-permute-start(f32[520,128]{1,0:T(8,128)S(1)} %get-tuple-element.63.refs_0_), channel_id=1, source_target_pairs={{0,2},{2,0},{4,6},{6,4},{8,10},{10,8},{12,14},{14,12},{1,3},{3,1},... | collective-permute-start | bytes 798728 | tf_op jit(solution)/shard_map/ppermute | solution.py:422
  16.7 10.2 %collective-permute-start.7 = (f32[520,128]{1,0:T(8,128)S(1)}, f32[520,128]{1,0:T(8,128)S(1)}, u32[]{:S(2)}, u32[]{:S(2)}) collective-permute-start(f32[520,128]{1,0:T(8,128)S(1)} %get-tuple-element.79), channel_id=1, source_target_pairs={{0,4},{2,6},{4,8},{6,10},{8,12},{10,14},{12,0},{14,2},{1,5},{3,7},... | collective-permute-start | bytes 798728 | tf_op jit(solution)/shard_map/ppermute | solution.py:423
  22.3 7.0 %collective-permute-start.4 = (f32[520,128]{1,0:T(8,128)S(1)}, f32[520,128]{1,0:T(8,128)S(1)}, u32[]{:S(2)}, u32[]{:S(2)}) collective-permute-start(f32[520,128]{1,0:T(8,128)S(1)} %get-tuple-element.66.refs_0_), channel_id=1, source_target_pairs={{0,2},{2,0},{4,6},{6,4},{8,10},{10,8},{12,14},{14,12},{1,3},{3,1},... | collective-permute-start | bytes 798728 | tf_op jit(solution)/shard_map/ppermute | solution.py:422
  23.1 6.8 %collective-permute-start.5 = (f32[520,128]{1,0:T(8,128)S(1)}, f32[520,128]{1,0:T(8,128)S(1)}, u32[]{:S(2)}, u32[]{:S(2)}) collective-permute-start(f32[520,128]{1,0:T(8,128)S(1)} %get-tuple-element.69), channel_id=1, source_target_pairs={{0,4},{2,6},{4,8},{6,10},{8,12},{10,14},{1,5},{3,7},{5,9},{7,11},{... | collective-permute-start | bytes 798728 | tf_op jit(solution)/shard_map/ppermute | solution.py:424

commit v5 on v4

--- a/solution.py
+++ b/solution.py
@@ -326,7 +326,7 @@
         copies[-1].start()
 
     for i, (first, heads, kind) in enumerate(groups):
-        own_ref, near_ref, past_ref, o_ref, gate_ref, decay_ref, q_ref = inputs[7 * i : 7 * i + 7]
+        own_ref, near_ref, past_ref = inputs[7 * i : 7 * i + 3]
         gated_ref, snap_ref = scratch[2 * i : 2 * i + 2]
         size = own_ref.shape[1]
         top = heads * size
@@ -345,7 +345,9 @@
             scale_past = bridged
         scale_past = jnp.where(place >= 2, scale_past, 0.0)
         own_decay = jnp.exp(own_ref[finals, :]) * jnp.where(own_end == previous, 1.0, 0.0)
-        valid = as_column(jnp.where(seg == previous[:, :1], 1.0, 0.0), size)
+        number_valid = jnp.sum(
+            jnp.where(seg == previous[:, :1], 1.0, 0.0), axis=1, keepdims=True
+        )
         for j in range(heads):
             rows = slice(j * size, (j + 1) * size)
             state = scale_past[j : j + 1] * past_ref[rows, :] + scale_near * near_ref[rows, :]
@@ -353,13 +355,14 @@
             high = state.astype(BF16)
             low = (state - high.astype(F32)).astype(BF16)
             both = jnp.concatenate([high, low], axis=0)
-            work.append((i, j, first, heads, both, valid, (o_ref, gate_ref, decay_ref, q_ref)))
+            work.append((i, j, first, heads, both, number_valid, inputs[7 * i + 3 : 7 * i + 7]))
         send(snap_ref, snap_hbm.at[0, pl.ds(first, heads)])
 
-    for number, (i, j, first, heads, both, valid, arrays) in enumerate(work):
+    rows = lax.broadcasted_iota(jnp.int32, (64, 128), 0).astype(F32)
+    for number, (i, j, first, heads, both, number_valid, arrays) in enumerate(work):
         o_ref, gate_ref, decay_ref, q_ref = arrays
         gated_ref = scratch[2 * i]
-        tokens, size = valid.shape
+        tokens, size = seg.shape[1], q_ref.shape[1] // heads
         columns = slice(j * size, (j + 1) * size)
         q = q_ref[:, columns]
         inter_ref[number % 4] = lax.dot_general(
@@ -368,7 +371,8 @@
         for start in range(0, tokens, 64):
             here = slice(start, start + 64)
             inter = inter_ref[number % 4, here, :]
-            mixed = o_ref[here, columns] + inter * (decay_ref[here, columns] * valid[here])
+            inter = jnp.where(rows < number_valid - start, inter * decay_ref[here, columns], 0.0)
+            mixed = o_ref[here, columns] + inter
             square = jnp.sum(mixed * mixed, axis=1, keepdims=True)
             gated = mixed * lax.rsqrt(square + size * 1e-06) * gate_ref[here, columns]
             gated_ref[here, columns] = gated.astype(BF16)
@@ -472,11 +476,11 @@
     message, both = pair_last(0, (), (both,))
     past[1] = turn(both)
     look_inside(1, (), (message,))
-    look_inside(2, (), (inside[1][0],))
-    both = joined(order, own[3], near[3], chunks[3][1], (inside[2][0],))
-    message, both = pair_last(2, (), (both,))
+    both = joined(order, own[3], near[3], chunks[3][1], (inside[1][0],))
     past[3] = ahead(both)
-    look_inside(3, (), (message,))
+    (message,) = pair_last(2, (both,))
+    look_inside(2, (), (message,))
+    look_inside(3, (), (inside[2][0],))
 
     if reach > 2:
         for i, (_, many) in enumerate(chunks):
@@ -489,7 +493,7 @@
                 past[i] = widened(past[i], many, 2, 2)
 
     result = ()
-    for group in ((0, 1), (2, 3)):
+    for group in ((0, 1), (3, 2)):
         groups = [(*chunks[i], ("span", "pair")[i % 2]) for i in group]
         arrays = [x for i in group for x in (own[i], near[i], past[i], *inside[i])]
         result = finish(order, seg, heads, groups, arrays, result, (inside[3][0],))

time: 32.3 us -> 32.2 us (level)
  starting transfers between devices: 10.5 us -> 12.3 us
  waiting for transfers between devices: 4.86 us -> 3.22 us
    ppermute x1, starting transfers between devices: 2.29 us -> 4.26 us  [shards(): lax.ppermute(x, 'seq', [(c, c + 2) for c in range(count - 2)])]
    ppermute x3, waiting for transfers between devices: 4.25 us -> 2.48 us  [shards(): lax.ppermute(x, 'seq', [(c, (c + 2) % count) for c in range(count)])]
  transfers between devices with their start and end apart: 8 -> 8, of which waited for: 4 -> 3; matrix products, arithmetic and copies ran while one was open for 0% -> 0% of each run, Pallas kernels for 37% -> 37%
where the time goes in v5:
time: 32.2 us; the launch traced here: 32 us
  Pallas kernels  15.7 us (49%)
  starting transfers between devices  12.3 us (38%)
  waiting for transfers between devices  3.22 us (10%)
  between operations  0.77 us (2%)
    pallas_call x4, Pallas kernels, intra(): pl.pallas_call(functools.partial(intra_kernel, first, heads, len(through)...  6.16 us
    pallas_call x2, Pallas kernels, finish(): pl.pallas_call(functools.partial(final_kernel, groups, unread), in_specs=...  4.33 us
    ppermute x1, starting transfers between devices, shards(): lax.ppermute(x, 'seq', [(c, c + 2) for c in range(count - 2)])  4.26 us
    ppermute x4, starting transfers between devices, shards(): swap = lambda x: lax.ppermute(x, 'seq', [(c, c ^ 1) for c in range(count)])  4.26 us
    ppermute x3, starting transfers between devices, shards(): lax.ppermute(x, 'seq', [(c, (c + 2) % count) for c in range(count)])  3.8 us
    pallas_call x1, Pallas kernels, rest_messages(): pl.pallas_call(functools.partial(rest_kernel, chunks, done), in_specs=[pl...  2.97 us
    ppermute x3, waiting for transfers between devices, shards(): lax.ppermute(x, 'seq', [(c, (c + 2) % count) for c in range(count)])  2.48 us
    pallas_call x1, Pallas kernels, first_message(): pl.pallas_call(functools.partial(first_kernel, heads, chunks), in_specs=[...  1.69 us
  transfers between devices with their start and end apart: 8, of which 3 were waited for; matrix products, arithmetic and copies ran while one was open for 0% of the time, Pallas kernels for 37%

profile of v5, /device:TPU:0, one launch (start us, length us, event | category | flops | bytes accessed | tf_op | source)
XLA Modules:
  0.0 32.0 jit_solution(11219681416057657776)
XLA Ops:
  0.6 1.7 %first_message.1 = (f32[520,128]{1,0:T(8,128)S(1)}, f32[16,512]{1,0:T(8,128)S(1)}, f32[16,512]{1,0:T(8,128)S(1)}, s32[1,512]{1,0:T(1,128)S(1)}, bf16[512,512]{1,...) custom-call(s32[1]{0:T(128)} %bitcast.order_ref.refs_0_, ...), custom_call_target="tpu_custom_call" | custom-call | flops 1 | bytes 1 | tf_op jit(solution)/shard_map/first_message/pallas_call | solution.py:100
  2.3 3.0 %collective-permute-start.2 = (f32[520,128]{1,0:T(8,128)S(1)}, f32[520,128]{1,0:T(8,128)S(1)}, u32[]{:S(2)}, u32[]{:S(2)}) collective-permute-start(f32[520,128]{1,0:T(8,128)S(1)} %get-tuple-element.52.refs_1_.rest_7_), channel_id=1, source_target_pairs={{0,2},{2,0},{4,6},{6,4},{8,10},{10,8},{12,14},{14,12},{1,3},{3,1},... | collective-permute-start | bytes 798728 | tf_op jit(solution)/shard_map/ppermute | solution.py:426
  5.3 0.4 %second_message.1.even_ref.rest_0_ = f32[520,128]{1,0:T(8,128)S(1)} custom-call(s32[1,512]{1,0:T(1,128)S(1)} %get-tuple-element.41.seg_ref, f32[16,512]{1,0:T(8,128)S(1)} %get-tuple-element.42.a_ref, f32[16,512]{1,0:T(8,128)S(1)} %get-tuple-element.43.w_ref, bf16[512,512]{1,0:T(8,128)(2,1)S(1)} %get-tuple-element.50.k_ref, ...), custom_call_target="tpu_custom_call" | custom-call | flops 1 | bytes 1 | tf_op jit(solution)/shard_map/second_message/pallas_call | solution.py:127
  5.7 0.0 copy-start
  5.7 1.6 %collective-permute-start.1 = (f32[520,128]{1,0:T(8,128)S(1)}, f32[520,128]{1,0:T(8,128)S(1)}, u32[]{:S(2)}, u32[]{:S(2)}) collective-permute-start(f32[520,128]{1,0:T(8,128)S(1)} %second_message.1.even_ref.rest_0_), channel_id=1, source_target_pairs={{0,4},{2,6},{4,8},{6,10},{8,12},{10,14},{12,0},{14,2},{1,5},{3,7},... | collective-permute-start | bytes 798728 | tf_op jit(solution)/shard_map/ppermute | solution.py:427
  7.3 3.0 %rest_messages.1 = (f32[520,128]{1,0:T(8,128)S(1)}, f32[520,128]{1,0:T(8,128)S(1)}, f32[512,512]{1,0:T(8,128)S(1)}, bf16[512,512]{1,0:T(8,128)(2,1)S(1)}, bf16[5...) custom-call(s32[1,512]{1,0:T(1,128)S(1)} %get-tuple-element.41.seg_r, ...), custom_call_target="tpu_custom_call" | custom-call | flops 1 | bytes 1 | tf_op jit(solution)/shard_map/rest_messages/pallas_call | solution.py:174
  10.3 0.6 %collective-permute-start = (f32[520,128]{1,0:T(8,128)S(1)}, f32[520,128]{1,0:T(8,128)S(1)}, u32[]{:S(2)}, u32[]{:S(2)}) collective-permute-start(f32[520,128]{1,0:T(8,128)S(1)} %get-tuple-element.44.refs_1_.rest_0_), channel_id=1, source_target_pairs={{0,2},{2,0},{4,6},{6,4},{8,10},{10,8},{12,14},{14,12},{1,3},{3,1},... | collective-permute-start | bytes 798728 | tf_op jit(solution)/shard_map/ppermute | solution.py:426
  10.9 1.6 %collective-permute-start.4 = (f32[520,128]{1,0:T(8,128)S(1)}, f32[520,128]{1,0:T(8,128)S(1)}, u32[]{:S(2)}, u32[]{:S(2)}) collective-permute-start(f32[520,128]{1,0:T(8,128)S(1)} %get-tuple-element.66.even_ref.rest_7_), channel_id=1, source_target_pairs={{0,4},{2,6},{4,8},{6,10},{8,12},{10,14},{12,0},{14,2},{1,5},{3,7},... | collective-permute-start | bytes 798728 | tf_op jit(solution)/shard_map/ppermute | solution.py:427
  12.5 1.5 %intra_span.4 = (f32[512,512]{1,0:T(8,128)S(1)}, f32[512,512]{1,0:T(8,128)S(1)}, f32[512,512]{1,0:T(8,128)S(1)}) custom-call(f32[512,512]{1,0:T(8,128)S(1)} %get-tuple-element.45.mask_ref, f32[16,512]{1,0:T(8,128)S(1)} %get-tuple-element.42.a_ref, f32[1,2048]{1,0:T(1,128)S(1)} %bitcast.4, bf16[512,512]{1,0:T(8,128)(2,1)S(1)} %get-tuple-element.53.q_ref.rest_6_, ...), custom_call_target="tpu_custom_call" | custom-call | flops 1 | bytes 1 | tf_op jit(solution)/shard_map/intra_span/pallas_call | solution.py:303
  14.0 0.1 join_windows.2.refs_0_
  14.1 2.5 %collective-permute-done.1.odd_ref.rest_2_ = f32[520,128]{1,0:T(8,128)S(1)} collective-permute-done((f32[520,128]{1,0:T(8,128)S(1)}, f32[520,128]{1,0:T(8,128)S(1)}, u32[]{:S(2)}, u32[]{:S(2)}) %collective-permute-start.1) | collective-permute-done | bytes 266272 | tf_op jit(solution)/shard_map/ppermute | solution.py:427
  16.6 0.1 collective-permute-start.6
  16.7 0.6 %collective-permute-start.7 = (f32[520,128]{1,0:T(8,128)S(1)}, f32[520,128]{1,0:T(8,128)S(1)}, u32[]{:S(2)}, u32[]{:S(2)}) collective-permute-start(f32[520,128]{1,0:T(8,128)S(1)} %get-tuple-element.75), channel_id=1, source_target_pairs={{0,4},{2,6},{4,8},{6,10},{8,12},{10,14},{12,0},{14,2},{1,5},{3,7},... | collective-permute-start | bytes 798728 | tf_op jit(solution)/shard_map/ppermute | solution.py:427
  17.3 1.5 %intra_span.5 = (f32[512,512]{1,0:T(8,128)S(1)}, f32[512,512]{1,0:T(8,128)S(1)}, f32[512,512]{1,0:T(8,128)S(1)}) custom-call(f32[512,512]{1,0:T(8,128)S(1)} %get-tuple-element.45.mask_ref, f32[16,512]{1,0:T(8,128)S(1)} %get-tuple-element.42.a_ref, f32[1,2048]{1,0:T(1,128)S(1)} %bitcast.5, bf16[512,512]{1,0:T(8,128)(2,1)S(1)} %get-tuple-element.46.q_ref.rest_13_, ...), custom_call_target="tpu_custom_call" | custom-call | flops 1 | bytes 1 | tf_op jit(solution)/shard_map/intra_span/pallas_call | solution.py:303
  18.8 0.1 collective-permute-done.refs_2_.rest_1_
  19.0 0.1 join_windows.3.refs_0_
  19.0 4.3 %collective-permute-start.3 = (f32[520,128]{1,0:T(8,128)S(1)}, f32[520,128]{1,0:T(8,128)S(1)}, u32[]{:S(2)}, u32[]{:S(2)}) collective-permute-start(f32[520,128]{1,0:T(8,128)S(1)} %join_windows.3.refs_0_), channel_id=1, source_target_pairs={{0,4},{2,6},{4,8},{6,10},{8,12},{10,14},{1,5},{3,7},{5,9},{7,11},{... | collective-permute-start | bytes 798728 | tf_op jit(solution)/shard_map/ppermute | solution.py:428
  23.3 0.0 collective-permute-done.4.odd_ref.rest_9_
  23.3 0.6 %collective-permute-start.5 = (f32[520,128]{1,0:T(8,128)S(1)}, f32[520,128]{1,0:T(8,128)S(1)}, u32[]{:S(2)}, u32[]{:S(2)}) collective-permute-start(f32[520,128]{1,0:T(8,128)S(1)} %pick_message.3.refs_0_), channel_id=1, source_target_pairs={{0,2},{2,0},{4,6},{6,4},{8,10},{10,8},{12,14},{14,12},{1,3},{3,1},... | collective-permute-start | bytes 798728 | tf_op jit(solution)/shard_map/ppermute | solution.py:426
  23.9 1.5 %intra_span.6 = (f32[512,512]{1,0:T(8,128)S(1)}, f32[512,512]{1,0:T(8,128)S(1)}, f32[512,512]{1,0:T(8,128)S(1)}) custom-call(f32[512,512]{1,0:T(8,128)S(1)} %get-tuple-element.45.mask_ref, f32[16,512]{1,0:T(8,128)S(1)} %get-tuple-element.42.a_ref, f32[1,2048]{1,0:T(1,128)S(1)} %bitcast.6, bf16[512,512]{1,0:T(8,128)(2,1)S(1)} %get-tuple-element.62.q_ref.rest_13_, ...), custom_call_target="tpu_custom_call" | custom-call | flops 1 | bytes 1 | tf_op jit(solution)/shard_map/intra_span/pallas_call | solution.py:303
  25.5 1.5 %intra_span.7 = (f32[512,512]{1,0:T(8,128)S(1)}, f32[512,512]{1,0:T(8,128)S(1)}, f32[512,512]{1,0:T(8,128)S(1)}) custom-call(f32[512,512]{1,0:T(8,128)S(1)} %get-tuple-element.45.mask_ref, f32[16,512]{1,0:T(8,128)S(1)} %get-tuple-element.42.a_ref, f32[1,2048]{1,0:T(1,128)S(1)} %bitcast.7, bf16[512,512]{1,0:T(8,128)(2,1)S(1)} %get-tuple-element.58.q_ref.rest_6_, ...), custom_call_target="tpu_custom_call" | custom-call | flops 1 | bytes 1 | tf_op jit(solution)/shard_map/intra_span/pallas_call | solution.py:303
  27.0 2.2 %finish.2 = (bf16[512,2048]{1,0:T(8,128)(2,1)}, f32[1,16,128,128]{3,2,1,0:T(8,128)}) custom-call(s32[1]{0:T(128)} %bitcast.order_ref.refs_0_, s32[1,512]{1,0:T(1,128)S(1)} %get-tuple-element.41.seg_ref, f32[520,128]{1,0:T(8,128)S(1)} %second_message.1.even_ref.rest_0_, f32[520,128]{1,0:T(8,128)S(1)} %collective-permute-done.6.rest_1_, ...), custom_call_target="tpu_custom_call" | custom-call | flops 1 | bytes 1 | tf_op jit(solution)/shard_map/finish/pallas_call | solution.py:396
  29.2 0.6 %collective-permute-done.3.rest_2_ = f32[520,128]{1,0:T(8,128)S(1)} collective-permute-done((f32[520,128]{1,0:T(8,128)S(1)}, f32[520,128]{1,0:T(8,128)S(1)}, u32[]{:S(2)}, u32[]{:S(2)}) %collective-permute-start.3) | collective-permute-done | bytes 266272 | tf_op jit(solution)/shard_map/ppermute | solution.py:428
  29.8 2.2 %finish.3 = (bf16[512,2048]{1,0:T(8,128)(2,1)}, f32[1,16,128,128]{3,2,1,0:T(8,128)}) custom-call(s32[1]{0:T(128)} %bitcast.order_ref.refs_0_, s32[1,512]{1,0:T(1,128)S(1)} %get-tuple-element.41.seg_ref, f32[520,128]{1,0:T(8,128)S(1)} %get-tuple-element.44.refs_1_.rest_0_, ...), custom_call_target="tpu_custom_call", output_to_operand_aliasing={{0}: (16, {}), {1}: (17, {})} | custom-call | flops 1 | bytes 1 | tf_op jit(solution)/shard_map/finish/pallas_call | solution.py:396
  (7 shorter events, 0.1 us)
Async XLA Ops:
  2.3 11.7 %collective-permute-start.2 = (f32[520,128]{1,0:T(8,128)S(1)}, f32[520,128]{1,0:T(8,128)S(1)}, u32[]{:S(2)}, u32[]{:S(2)}) collective-permute-start(f32[520,128]{1,0:T(8,128)S(1)} %get-tuple-element.52.refs_1_.rest_7_), channel_id=1, source_target_pairs={{0,2},{2,0},{4,6},{6,4},{8,10},{10,8},{12,14},{14,12},{1,3},{3,1},... | collective-permute-start | bytes 798728 | tf_op jit(solution)/shard_map/ppermute | solution.py:426
  5.7 6.8 %copy-start = (f32[2048]{0:T(1024)S(1)}, f32[2048]{0:T(1024)}, u32[]{:S(2)}) copy-start(f32[2048]{0:T(1024)} %param.15) | copy-start | bytes 24580
  5.7 10.9 %collective-permute-start.1 = (f32[520,128]{1,0:T(8,128)S(1)}, f32[520,128]{1,0:T(8,128)S(1)}, u32[]{:S(2)}, u32[]{:S(2)}) collective-permute-start(f32[520,128]{1,0:T(8,128)S(1)} %second_message.1.even_ref.rest_0_), channel_id=1, source_target_pairs={{0,4},{2,6},{4,8},{6,10},{8,12},{10,14},{12,0},{14,2},{1,5},{3,7},... | collective-permute-start | bytes 798728 | tf_op jit(solution)/shard_map/ppermute | solution.py:427
  10.3 8.6 %collective-permute-start = (f32[520,128]{1,0:T(8,128)S(1)}, f32[520,128]{1,0:T(8,128)S(1)}, u32[]{:S(2)}, u32[]{:S(2)}) collective-permute-start(f32[520,128]{1,0:T(8,128)S(1)} %get-tuple-element.44.refs_1_.rest_0_), channel_id=1, source_target_pairs={{0,2},{2,0},{4,6},{6,4},{8,10},{10,8},{12,14},{14,12},{1,3},{3,1},... | collective-permute-start | bytes 798728 | tf_op jit(solution)/shard_map/ppermute | solution.py:426
  10.9 12.4 %collective-permute-start.4 = (f32[520,128]{1,0:T(8,128)S(1)}, f32[520,128]{1,0:T(8,128)S(1)}, u32[]{:S(2)}, u32[]{:S(2)}) collective-permute-start(f32[520,128]{1,0:T(8,128)S(1)} %get-tuple-element.66.even_ref.rest_7_), channel_id=1, source_target_pairs={{0,4},{2,6},{4,8},{6,10},{8,12},{10,14},{12,0},{14,2},{1,5},{3,7},... | collective-permute-start | bytes 798728 | tf_op jit(solution)/shard_map/ppermute | solution.py:427
  16.6 10.4 %collective-permute-start.6 = (f32[520,128]{1,0:T(8,128)S(1)}, f32[520,128]{1,0:T(8,128)S(1)}, u32[]{:S(2)}, u32[]{:S(2)}) collective-permute-start(f32[520,128]{1,0:T(8,128)S(1)} %get-tuple-element.56.refs_0_), channel_id=1, source_target_pairs={{0,2},{2,0},{4,6},{6,4},{8,10},{10,8},{12,14},{14,12},{1,3},{3,1},... | collective-permute-start | bytes 798728 | tf_op jit(solution)/shard_map/ppermute | solution.py:426
  16.7 10.3 %collective-permute-start.7 = (f32[520,128]{1,0:T(8,128)S(1)}, f32[520,128]{1,0:T(8,128)S(1)}, u32[]{:S(2)}, u32[]{:S(2)}) collective-permute-start(f32[520,128]{1,0:T(8,128)S(1)} %get-tuple-element.75), channel_id=1, source_target_pairs={{0,4},{2,6},{4,8},{6,10},{8,12},{10,14},{12,0},{14,2},{1,5},{3,7},... | collective-permute-start | bytes 798728 | tf_op jit(solution)/shard_map/ppermute | solution.py:427
  19.0 10.8 %collective-permute-start.3 = (f32[520,128]{1,0:T(8,128)S(1)}, f32[520,128]{1,0:T(8,128)S(1)}, u32[]{:S(2)}, u32[]{:S(2)}) collective-permute-start(f32[520,128]{1,0:T(8,128)S(1)} %join_windows.3.refs_0_), channel_id=1, source_target_pairs={{0,4},{2,6},{4,8},{6,10},{8,12},{10,14},{1,5},{3,7},{5,9},{7,11},{... | collective-permute-start | bytes 798728 | tf_op jit(solution)/shard_map/ppermute | solution.py:428
  23.3 6.5 %collective-permute-start.5 = (f32[520,128]{1,0:T(8,128)S(1)}, f32[520,128]{1,0:T(8,128)S(1)}, u32[]{:S(2)}, u32[]{:S(2)}) collective-permute-start(f32[520,128]{1,0:T(8,128)S(1)} %pick_message.3.refs_0_), channel_id=1, source_target_pairs={{0,2},{2,0},{4,6},{6,4},{8,10},{10,8},{12,14},{14,12},{1,3},{3,1},... | collective-permute-start | bytes 798728 | tf_op jit(solution)/shard_map/ppermute | solution.py:426

commit v6 on v5

--- a/solution.py
+++ b/solution.py
@@ -55,30 +55,35 @@
     copies = [pltpu.make_async_copy(*pair, sems.at[i]) for i, pair in enumerate(pairs)]
     for copy in copies:
         copy.start()
-    earlier = lax.broadcasted_iota(jnp.int32, (tokens, tokens), 0)
-    later = lax.broadcasted_iota(jnp.int32, (tokens, tokens), 1)
+    part = min(tokens, 256)
+    earlier = lax.broadcasted_iota(jnp.int32, (part, part), 0)
+    later = lax.broadcasted_iota(jnp.int32, (part, part), 1)
     upper = jnp.where(earlier <= later, 1.0, 0.0).astype(BF16)
     across = lax.broadcasted_iota(jnp.int32, (heads, heads), 1)
     down = lax.broadcasted_iota(jnp.int32, (heads, heads), 0)
-    for copy in copies[:3]:
+    for copy in copies[:5]:
         copy.wait()
     spread = jnp.broadcast_to(exponent_ref[...], (heads, heads))
     exponent = jnp.sum(jnp.where(across == down, spread, 0).astype(F32), axis=1, keepdims=True)
     a = -jnp.exp2(-exponent) + jnp.log(keep_ref[...])
+    a = jnp.concatenate([a[:, i : i + part] for i in range(0, tokens, part)], axis=0)
     high = a.astype(BF16)
     rest = a - high.astype(F32)
     middle = rest.astype(BF16)
     low = (rest - middle.astype(F32)).astype(BF16)
-    parts = jnp.concatenate([high, middle, low], axis=0)
-    sums = lax.dot_general(parts, upper, NN, preferred_element_type=F32)
-    cumulative = sums[:heads] + (sums[heads : 2 * heads] + sums[2 * heads :])
+    pieces = jnp.concatenate([high, middle, low], axis=0)
+    sums = lax.dot_general(pieces, upper, NN, preferred_element_type=F32)
+    rows = a.shape[0]
+    sums = sums[:rows] + (sums[rows : 2 * rows] + sums[2 * rows :])
+    parts = [sums[i : i + heads] for i in range(0, rows, heads)]
+    for i in range(1, len(parts)):
+        parts[i] = parts[i] + parts[i - 1][:, part - 1 :]
+    cumulative = jnp.concatenate(parts, axis=1)
     a_ref[...] = cumulative
     final = cumulative[:, tokens - 1 :]
     seg = seg_ref[...]
     last = seg[:, tokens - 1 :]
     w_ref[...] = jnp.where(seg == last, jnp.exp(final - cumulative), 0.0)
-    for copy in copies[3:5]:
-        copy.wait()
     first, many = chunks[0]
     finals = final[first : first + many]
     put_message(msg_ref, first, many, size, w_ref, finals, last, k_refs[0], v_refs[0])
@@ -376,8 +381,9 @@
             square = jnp.sum(mixed * mixed, axis=1, keepdims=True)
             gated = mixed * lax.rsqrt(square + size * 1e-06) * gate_ref[here, columns]
             gated_ref[here, columns] = gated.astype(BF16)
-        if j % 2 == 1 or j == heads - 1:
-            begin = j - j % 2
+        alone = number + 2 >= len(work)
+        if alone or j % 2 == 1 or j == heads - 1:
+            begin = j if alone else j - j % 2
             width = (j + 1 - begin) * size
             there = pl.ds((first + begin) * size, width)
             send(gated_ref.at[:, pl.ds(begin * size, width)], gated_hbm.at[:, there])
@@ -476,11 +482,11 @@
     message, both = pair_last(0, (), (both,))
     past[1] = turn(both)
     look_inside(1, (), (message,))
-    both = joined(order, own[3], near[3], chunks[3][1], (inside[1][0],))
+    look_inside(2, (), (inside[1][0],))
+    both = joined(order, own[3], near[3], chunks[3][1], (inside[2][0],))
+    message, both = pair_last(2, (), (both,))
     past[3] = ahead(both)
-    (message,) = pair_last(2, (both,))
-    look_inside(2, (), (message,))
-    look_inside(3, (), (inside[2][0],))
+    look_inside(3, (), (message,))
 
     if reach > 2:
         for i, (_, many) in enumerate(chunks):
@@ -493,7 +499,7 @@
                 past[i] = widened(past[i], many, 2, 2)
 
     result = ()
-    for group in ((0, 1), (3, 2)):
+    for group in ((0, 1), (2, 3)):
         groups = [(*chunks[i], ("span", "pair")[i % 2]) for i in group]
         arrays = [x for i in group for x in (own[i], near[i], past[i], *inside[i])]
         result = finish(order, seg, heads, groups, arrays, result, (inside[3][0],))

time: 32.2 us -> 32.5 us (level)
  starting transfers between devices: 12.3 us -> 10.5 us
  waiting for transfers between devices: 3.22 us -> 4.96 us
  Pallas kernels: 15.7 us -> 16.1 us
    ppermute x1, starting transfers between devices: 4.26 us -> 2.29 us  [shards(): lax.ppermute(x, 'seq', [(c, c + 2) for c in range(count - 2)])]
    ppermute x3, waiting for transfers between devices: 2.48 us -> 4.25 us  [shards(): lax.ppermute(x, 'seq', [(c, (c + 2) % count) for c in range(count)])]
  transfers between devices with their start and end apart: 8 -> 8, of which waited for: 3 -> 4; matrix products, arithmetic and copies ran while one was open for 0% -> 0% of each run, Pallas kernels for 37% -> 37%
where the time goes in v6:
time: 32.5 us; the launch traced here: 32.3 us
  Pallas kernels  16.1 us (50%)
  starting transfers between devices  10.5 us (32%)
  waiting for transfers between devices  4.96 us (15%)
  between operations  0.77 us (2%)
    pallas_call x4, Pallas kernels, intra(): pl.pallas_call(functools.partial(intra_kernel, first, heads, len(through)...  6.2 us
    ppermute x4, starting transfers between devices, shards(): swap = lambda x: lax.ppermute(x, 'seq', [(c, c ^ 1) for c in range(count)])  4.4 us
    pallas_call x2, Pallas kernels, finish(): pl.pallas_call(functools.partial(final_kernel, groups, unread), in_specs=...  4.37 us
    ppermute x3, waiting for transfers between devices, shards(): lax.ppermute(x, 'seq', [(c, (c + 2) % count) for c in range(count)])  4.25 us
    ppermute x3, starting transfers between devices, shards(): lax.ppermute(x, 'seq', [(c, (c + 2) % count) for c in range(count)])  3.81 us
    pallas_call x1, Pallas kernels, rest_messages(): pl.pallas_call(functools.partial(rest_kernel, chunks, done), in_specs=[pl...  2.97 us
    ppermute x1, starting transfers between devices, shards(): lax.ppermute(x, 'seq', [(c, c + 2) for c in range(count - 2)])  2.29 us
    pallas_call x1, Pallas kernels, first_message(): pl.pallas_call(functools.partial(first_kernel, heads, chunks), in_specs=[...  2.01 us
  transfers between devices with their start and end apart: 8, of which 4 were waited for; matrix products, arithmetic and copies ran while one was open for 0% of the time, Pallas kernels for 37%

profile of v6, /device:TPU:0, one launch (start us, length us, event | category | flops | bytes accessed | tf_op | source)
XLA Modules:
  0.0 32.3 jit_solution(4529250981126466826)
XLA Ops:
  0.6 2.0 %first_message.1 = (f32[520,128]{1,0:T(8,128)S(1)}, f32[16,512]{1,0:T(8,128)S(1)}, f32[16,512]{1,0:T(8,128)S(1)}, s32[1,512]{1,0:T(1,128)S(1)}, bf16[512,512]{1,...) custom-call(s32[1]{0:T(128)} %bitcast.order_ref.refs_0_, ...), custom_call_target="tpu_custom_call" | custom-call | flops 1 | bytes 1 | tf_op jit(solution)/shard_map/first_message/pallas_call | solution.py:105
  2.7 3.0 %collective-permute-start.3 = (f32[520,128]{1,0:T(8,128)S(1)}, f32[520,128]{1,0:T(8,128)S(1)}, u32[]{:S(2)}, u32[]{:S(2)}) collective-permute-start(f32[520,128]{1,0:T(8,128)S(1)} %get-tuple-element.59.refs_1_.rest_7_), channel_id=1, source_target_pairs={{0,2},{2,0},{4,6},{6,4},{8,10},{10,8},{12,14},{14,12},{1,3},{3,1},... | collective-permute-start | bytes 798728 | tf_op jit(solution)/shard_map/ppermute | solution.py:432
  5.7 0.4 %second_message.1.even_ref.rest_0_ = f32[520,128]{1,0:T(8,128)S(1)} custom-call(s32[1,512]{1,0:T(1,128)S(1)} %get-tuple-element.43.seg_ref, f32[16,512]{1,0:T(8,128)S(1)} %get-tuple-element.44.a_ref, f32[16,512]{1,0:T(8,128)S(1)} %get-tuple-element.45.w_ref, bf16[512,512]{1,0:T(8,128)(2,1)S(1)} %get-tuple-element.57.k_ref, ...), custom_call_target="tpu_custom_call" | custom-call | flops 1 | bytes 1 | tf_op jit(solution)/shard_map/second_message/pallas_call | solution.py:132
  6.0 0.0 copy-start
  6.0 1.6 %collective-permute-start.2 = (f32[520,128]{1,0:T(8,128)S(1)}, f32[520,128]{1,0:T(8,128)S(1)}, u32[]{:S(2)}, u32[]{:S(2)}) collective-permute-start(f32[520,128]{1,0:T(8,128)S(1)} %second_message.1.even_ref.rest_0_), channel_id=1, source_target_pairs={{0,4},{2,6},{4,8},{6,10},{8,12},{10,14},{12,0},{14,2},{1,5},{3,7},... | collective-permute-start | bytes 798728 | tf_op jit(solution)/shard_map/ppermute | solution.py:433
  7.7 3.0 %rest_messages.1 = (f32[520,128]{1,0:T(8,128)S(1)}, f32[520,128]{1,0:T(8,128)S(1)}, f32[512,512]{1,0:T(8,128)S(1)}, bf16[512,512]{1,0:T(8,128)(2,1)S(1)}, bf16[5...) custom-call(s32[1,512]{1,0:T(1,128)S(1)} %get-tuple-element.43.seg_r, ...), custom_call_target="tpu_custom_call" | custom-call | flops 1 | bytes 1 | tf_op jit(solution)/shard_map/rest_messages/pallas_call | solution.py:179
  10.6 0.6 %collective-permute-start.1 = (f32[520,128]{1,0:T(8,128)S(1)}, f32[520,128]{1,0:T(8,128)S(1)}, u32[]{:S(2)}, u32[]{:S(2)}) collective-permute-start(f32[520,128]{1,0:T(8,128)S(1)} %get-tuple-element.47.refs_1_.rest_7_), channel_id=1, source_target_pairs={{0,2},{2,0},{4,6},{6,4},{8,10},{10,8},{12,14},{14,12},{1,3},{3,1},... | collective-permute-start | bytes 798728 | tf_op jit(solution)/shard_map/ppermute | solution.py:432
  11.2 1.6 %collective-permute-start = (f32[520,128]{1,0:T(8,128)S(1)}, f32[520,128]{1,0:T(8,128)S(1)}, u32[]{:S(2)}, u32[]{:S(2)}) collective-permute-start(f32[520,128]{1,0:T(8,128)S(1)} %get-tuple-element.46.even_ref.rest_0_), channel_id=1, source_target_pairs={{0,4},{2,6},{4,8},{6,10},{8,12},{10,14},{12,0},{14,2},{1,5},{3,7},... | collective-permute-start | bytes 798728 | tf_op jit(solution)/shard_map/ppermute | solution.py:433
  12.8 1.5 %intra_span.4 = (f32[512,512]{1,0:T(8,128)S(1)}, f32[512,512]{1,0:T(8,128)S(1)}, f32[512,512]{1,0:T(8,128)S(1)}) custom-call(f32[512,512]{1,0:T(8,128)S(1)} %get-tuple-element.48.mask_ref, f32[16,512]{1,0:T(8,128)S(1)} %get-tuple-element.44.a_ref, f32[1,2048]{1,0:T(1,128)S(1)} %bitcast.4, bf16[512,512]{1,0:T(8,128)(2,1)S(1)} %get-tuple-element.60.q_ref.rest_6_, ...), custom_call_target="tpu_custom_call" | custom-call | flops 1 | bytes 1 | tf_op jit(solution)/shard_map/intra_span/pallas_call | solution.py:308
  14.4 0.1 join_windows.2.refs_0_
  14.4 2.5 %collective-permute-done.2.odd_ref.rest_2_ = f32[520,128]{1,0:T(8,128)S(1)} collective-permute-done((f32[520,128]{1,0:T(8,128)S(1)}, f32[520,128]{1,0:T(8,128)S(1)}, u32[]{:S(2)}, u32[]{:S(2)}) %collective-permute-start.2) | collective-permute-done | bytes 266272 | tf_op jit(solution)/shard_map/ppermute | solution.py:433
  17.0 0.1 collective-permute-start.6
  17.0 0.6 %collective-permute-start.7 = (f32[520,128]{1,0:T(8,128)S(1)}, f32[520,128]{1,0:T(8,128)S(1)}, u32[]{:S(2)}, u32[]{:S(2)}) collective-permute-start(f32[520,128]{1,0:T(8,128)S(1)} %get-tuple-element.79), channel_id=1, source_target_pairs={{0,4},{2,6},{4,8},{6,10},{8,12},{10,14},{12,0},{14,2},{1,5},{3,7},... | collective-permute-start | bytes 798728 | tf_op jit(solution)/shard_map/ppermute | solution.py:433
  17.6 1.5 %intra_span.5 = (f32[512,512]{1,0:T(8,128)S(1)}, f32[512,512]{1,0:T(8,128)S(1)}, f32[512,512]{1,0:T(8,128)S(1)}) custom-call(f32[512,512]{1,0:T(8,128)S(1)} %get-tuple-element.48.mask_ref, f32[16,512]{1,0:T(8,128)S(1)} %get-tuple-element.44.a_ref, f32[1,2048]{1,0:T(1,128)S(1)} %bitcast.5, bf16[512,512]{1,0:T(8,128)(2,1)S(1)} %get-tuple-element.53.q_ref.rest_13_, ...), custom_call_target="tpu_custom_call" | custom-call | flops 1 | bytes 1 | tf_op jit(solution)/shard_map/intra_span/pallas_call | solution.py:308
  19.2 1.6 %intra_span.6 = (f32[512,512]{1,0:T(8,128)S(1)}, f32[512,512]{1,0:T(8,128)S(1)}, f32[512,512]{1,0:T(8,128)S(1)}) custom-call(f32[512,512]{1,0:T(8,128)S(1)} %get-tuple-element.48.mask_ref, f32[16,512]{1,0:T(8,128)S(1)} %get-tuple-element.44.a_ref, f32[1,2048]{1,0:T(1,128)S(1)} %bitcast.6, bf16[512,512]{1,0:T(8,128)(2,1)S(1)} %get-tuple-element.49.q_ref.rest_6_, ...), custom_call_target="tpu_custom_call" | custom-call | flops 1 | bytes 1 | tf_op jit(solution)/shard_map/intra_span/pallas_call | solution.py:308
  20.8 0.1 join_windows.3.refs_0_
  20.8 1.8 %collective-permute-done.odd_ref.rest_2_ = f32[520,128]{1,0:T(8,128)S(1)} collective-permute-done((f32[520,128]{1,0:T(8,128)S(1)}, f32[520,128]{1,0:T(8,128)S(1)}, u32[]{:S(2)}, u32[]{:S(2)}) %collective-permute-start) | collective-permute-done | bytes 266272 | tf_op jit(solution)/shard_map/ppermute | solution.py:433
  22.7 0.7 %collective-permute-start.4 = (f32[520,128]{1,0:T(8,128)S(1)}, f32[520,128]{1,0:T(8,128)S(1)}, u32[]{:S(2)}, u32[]{:S(2)}) collective-permute-start(f32[520,128]{1,0:T(8,128)S(1)} %get-tuple-element.66.refs_0_), channel_id=1, source_target_pairs={{0,2},{2,0},{4,6},{6,4},{8,10},{10,8},{12,14},{14,12},{1,3},{3,1},... | collective-permute-start | bytes 798728 | tf_op jit(solution)/shard_map/ppermute | solution.py:432
  23.4 2.3 %collective-permute-start.5 = (f32[520,128]{1,0:T(8,128)S(1)}, f32[520,128]{1,0:T(8,128)S(1)}, u32[]{:S(2)}, u32[]{:S(2)}) collective-permute-start(f32[520,128]{1,0:T(8,128)S(1)} %get-tuple-element.69), channel_id=1, source_target_pairs={{0,4},{2,6},{4,8},{6,10},{8,12},{10,14},{1,5},{3,7},{5,9},{7,11},{... | collective-permute-start | bytes 798728 | tf_op jit(solution)/shard_map/ppermute | solution.py:434
  25.7 1.6 %intra_span.7 = (f32[512,512]{1,0:T(8,128)S(1)}, f32[512,512]{1,0:T(8,128)S(1)}, f32[512,512]{1,0:T(8,128)S(1)}) custom-call(f32[512,512]{1,0:T(8,128)S(1)} %get-tuple-element.48.mask_ref, f32[16,512]{1,0:T(8,128)S(1)} %get-tuple-element.44.a_ref, f32[1,2048]{1,0:T(1,128)S(1)} %bitcast.7, bf16[512,512]{1,0:T(8,128)(2,1)S(1)} %get-tuple-element.70.q_ref.rest_13_, ...), custom_call_target="tpu_custom_call" | custom-call | flops 1 | bytes 1 | tf_op jit(solution)/shard_map/intra_span/pallas_call | solution.py:308
  27.3 2.2 %finish.2 = (bf16[512,2048]{1,0:T(8,128)(2,1)}, f32[1,16,128,128]{3,2,1,0:T(8,128)}) custom-call(s32[1]{0:T(128)} %bitcast.order_ref.refs_0_, s32[1,512]{1,0:T(1,128)S(1)} %get-tuple-element.43.seg_ref, f32[520,128]{1,0:T(8,128)S(1)} %second_message.1.even_ref.rest_0_, f32[520,128]{1,0:T(8,128)S(1)} %collective-permute-done.6.rest_1_, ...), custom_call_target="tpu_custom_call" | custom-call | flops 1 | bytes 1 | tf_op jit(solution)/shard_map/finish/pallas_call | solution.py:402
  29.4 0.2 collective-permute-done.4.rest_1_
  29.7 0.5 %collective-permute-done.5.rest_9_ = f32[520,128]{1,0:T(8,128)S(1)} collective-permute-done((f32[520,128]{1,0:T(8,128)S(1)}, f32[520,128]{1,0:T(8,128)S(1)}, u32[]{:S(2)}, u32[]{:S(2)}) %collective-permute-start.5) | collective-permute-done | bytes 266272 | tf_op jit(solution)/shard_map/ppermute | solution.py:434
  30.2 2.2 %finish.3 = (bf16[512,2048]{1,0:T(8,128)(2,1)}, f32[1,16,128,128]{3,2,1,0:T(8,128)}) custom-call(s32[1]{0:T(128)} %bitcast.order_ref.refs_0_, s32[1,512]{1,0:T(1,128)S(1)} %get-tuple-element.43.seg_ref, f32[520,128]{1,0:T(8,128)S(1)} %get-tuple-element.46.even_ref.rest_0_, ...), custom_call_target="tpu_custom_call", output_to_operand_aliasing={{0}: (16, {}), {1}: (17, {})} | custom-call | flops 1 | bytes 1 | tf_op jit(solution)/shard_map/finish/pallas_call | solution.py:402
  (7 shorter events, 0.1 us)
Async XLA Ops:
  2.7 11.7 %collective-permute-start.3 = (f32[520,128]{1,0:T(8,128)S(1)}, f32[520,128]{1,0:T(8,128)S(1)}, u32[]{:S(2)}, u32[]{:S(2)}) collective-permute-start(f32[520,128]{1,0:T(8,128)S(1)} %get-tuple-element.59.refs_1_.rest_7_), channel_id=1, source_target_pairs={{0,2},{2,0},{4,6},{6,4},{8,10},{10,8},{12,14},{14,12},{1,3},{3,1},... | collective-permute-start | bytes 798728 | tf_op jit(solution)/shard_map/ppermute | solution.py:432
  6.0 6.8 %copy-start = (f32[2048]{0:T(1024)S(1)}, f32[2048]{0:T(1024)}, u32[]{:S(2)}) copy-start(f32[2048]{0:T(1024)} %param.15) | copy-start | bytes 24580
  6.0 10.9 %collective-permute-start.2 = (f32[520,128]{1,0:T(8,128)S(1)}, f32[520,128]{1,0:T(8,128)S(1)}, u32[]{:S(2)}, u32[]{:S(2)}) collective-permute-start(f32[520,128]{1,0:T(8,128)S(1)} %second_message.1.even_ref.rest_0_), channel_id=1, source_target_pairs={{0,4},{2,6},{4,8},{6,10},{8,12},{10,14},{12,0},{14,2},{1,5},{3,7},... | collective-permute-start | bytes 798728 | tf_op jit(solution)/shard_map/ppermute | solution.py:433
  10.6 10.1 %collective-permute-start.1 = (f32[520,128]{1,0:T(8,128)S(1)}, f32[520,128]{1,0:T(8,128)S(1)}, u32[]{:S(2)}, u32[]{:S(2)}) collective-permute-start(f32[520,128]{1,0:T(8,128)S(1)} %get-tuple-element.47.refs_1_.rest_7_), channel_id=1, source_target_pairs={{0,2},{2,0},{4,6},{6,4},{8,10},{10,8},{12,14},{14,12},{1,3},{3,1},... | collective-permute-start | bytes 798728 | tf_op jit(solution)/shard_map/ppermute | solution.py:432
  11.2 11.4 %collective-permute-start = (f32[520,128]{1,0:T(8,128)S(1)}, f32[520,128]{1,0:T(8,128)S(1)}, u32[]{:S(2)}, u32[]{:S(2)}) collective-permute-start(f32[520,128]{1,0:T(8,128)S(1)} %get-tuple-element.46.even_ref.rest_0_), channel_id=1, source_target_pairs={{0,4},{2,6},{4,8},{6,10},{8,12},{10,14},{12,0},{14,2},{1,5},{3,7},... | collective-permute-start | bytes 798728 | tf_op jit(solution)/shard_map/ppermute | solution.py:433
  17.0 10.3 %collective-permute-start.6 = (f32[520,128]{1,0:T(8,128)S(1)}, f32[520,128]{1,0:T(8,128)S(1)}, u32[]{:S(2)}, u32[]{:S(2)}) collective-permute-start(f32[520,128]{1,0:T(8,128)S(1)} %get-tuple-element.63.refs_0_), channel_id=1, source_target_pairs={{0,2},{2,0},{4,6},{6,4},{8,10},{10,8},{12,14},{14,12},{1,3},{3,1},... | collective-permute-start | bytes 798728 | tf_op jit(solution)/shard_map/ppermute | solution.py:432
  17.0 10.2 %collective-permute-start.7 = (f32[520,128]{1,0:T(8,128)S(1)}, f32[520,128]{1,0:T(8,128)S(1)}, u32[]{:S(2)}, u32[]{:S(2)}) collective-permute-start(f32[520,128]{1,0:T(8,128)S(1)} %get-tuple-element.79), channel_id=1, source_target_pairs={{0,4},{2,6},{4,8},{6,10},{8,12},{10,14},{12,0},{14,2},{1,5},{3,7},... | collective-permute-start | bytes 798728 | tf_op jit(solution)/shard_map/ppermute | solution.py:433
  22.7 7.0 %collective-permute-start.4 = (f32[520,128]{1,0:T(8,128)S(1)}, f32[520,128]{1,0:T(8,128)S(1)}, u32[]{:S(2)}, u32[]{:S(2)}) collective-permute-start(f32[520,128]{1,0:T(8,128)S(1)} %get-tuple-element.66.refs_0_), channel_id=1, source_target_pairs={{0,2},{2,0},{4,6},{6,4},{8,10},{10,8},{12,14},{14,12},{1,3},{3,1},... | collective-permute-start | bytes 798728 | tf_op jit(solution)/shard_map/ppermute | solution.py:432
  23.4 6.8 %collective-permute-start.5 = (f32[520,128]{1,0:T(8,128)S(1)}, f32[520,128]{1,0:T(8,128)S(1)}, u32[]{:S(2)}, u32[]{:S(2)}) collective-permute-start(f32[520,128]{1,0:T(8,128)S(1)} %get-tuple-element.69), channel_id=1, source_target_pairs={{0,4},{2,6},{4,8},{6,10},{8,12},{10,14},{1,5},{3,7},{5,9},{7,11},{... | collective-permute-start | bytes 798728 | tf_op jit(solution)/shard_map/ppermute | solution.py:434

commit v7 on v5

--- a/solution.py
+++ b/solution.py
@@ -51,7 +51,10 @@
     pairs = [(keep_hbm, keep_ref), (exponent_hbm, exponent_ref), (seg_hbm, seg_ref)]
     for i, (first, many) in enumerate(chunks):
         wide = pl.ds(first * size, many * size)
-        pairs += [(k_hbm.at[:, wide], k_refs[i]), (v_hbm.at[:, wide], v_refs[i])]
+        for start in (0, tokens // 2):
+            rows = pl.ds(start, tokens // 2)
+            for source, target in ((k_hbm, k_refs[i]), (v_hbm, v_refs[i])):
+                pairs.append((source.at[rows, wide], target.at[rows, :]))
     copies = [pltpu.make_async_copy(*pair, sems.at[i]) for i, pair in enumerate(pairs)]
     for copy in copies:
         copy.start()
@@ -77,12 +80,12 @@
     seg = seg_ref[...]
     last = seg[:, tokens - 1 :]
     w_ref[...] = jnp.where(seg == last, jnp.exp(final - cumulative), 0.0)
-    for copy in copies[3:5]:
+    for copy in copies[3:7]:
         copy.wait()
     first, many = chunks[0]
     finals = final[first : first + many]
     put_message(msg_ref, first, many, size, w_ref, finals, last, k_refs[0], v_refs[0])
-    for copy in copies[5:]:
+    for copy in copies[7:]:
         copy.wait()
 
 
@@ -106,7 +109,7 @@
         scratch_shapes=[
             pltpu.VMEM((1, heads), jnp.int32),
             pltpu.VMEM((heads, tokens), F32),
-            pltpu.SemaphoreType.DMA((3 + 2 * number,)),
+            pltpu.SemaphoreType.DMA((3 + 4 * number,)),
         ],
         compiler_params=pltpu.CompilerParams(vmem_limit_bytes=8 * MIB),
         cost_estimate=SHORT,
@@ -376,8 +379,9 @@
             square = jnp.sum(mixed * mixed, axis=1, keepdims=True)
             gated = mixed * lax.rsqrt(square + size * 1e-06) * gate_ref[here, columns]
             gated_ref[here, columns] = gated.astype(BF16)
-        if j % 2 == 1 or j == heads - 1:
-            begin = j - j % 2
+        alone = number + 2 >= len(work)
+        if alone or j % 2 == 1 or j == heads - 1:
+            begin = j if alone else j - j % 2
             width = (j + 1 - begin) * size
             there = pl.ds((first + begin) * size, width)
             send(gated_ref.at[:, pl.ds(begin * size, width)], gated_hbm.at[:, there])
@@ -476,11 +480,11 @@
     message, both = pair_last(0, (), (both,))
     past[1] = turn(both)
     look_inside(1, (), (message,))
-    both = joined(order, own[3], near[3], chunks[3][1], (inside[1][0],))
+    look_inside(2, (), (inside[1][0],))
+    both = joined(order, own[3], near[3], chunks[3][1], (inside[2][0],))
+    message, both = pair_last(2, (), (both,))
     past[3] = ahead(both)
-    (message,) = pair_last(2, (both,))
-    look_inside(2, (), (message,))
-    look_inside(3, (), (inside[2][0],))
+    look_inside(3, (), (message,))
 
     if reach > 2:
         for i, (_, many) in enumerate(chunks):
@@ -493,7 +497,7 @@
                 past[i] = widened(past[i], many, 2, 2)
 
     result = ()
-    for group in ((0, 1), (3, 2)):
+    for group in ((0, 1), (2, 3)):
         groups = [(*chunks[i], ("span", "pair")[i % 2]) for i in group]
         arrays = [x for i in group for x in (own[i], near[i], past[i], *inside[i])]
         result = finish(order, seg, heads, groups, arrays, result, (inside[3][0],))

time: 32.2 us -> 32.2 us (level)
  starting transfers between devices: 12.3 us -> 10.5 us
  waiting for transfers between devices: 3.22 us -> 4.96 us
    ppermute x1, starting transfers between devices: 4.26 us -> 2.31 us  [shards(): lax.ppermute(x, 'seq', [(c, c + 2) for c in range(count - 2)])]
    ppermute x3, waiting for transfers between devices: 2.48 us -> 4.25 us  [shards(): lax.ppermute(x, 'seq', [(c, (c + 2) % count) for c in range(count)])]
  transfers between devices with their start and end apart: 8 -> 8, of which waited for: 3 -> 4; matrix products, arithmetic and copies ran while one was open for 0% -> 0% of each run, Pallas kernels for 37% -> 37%
where the time goes in v7:
time: 32.2 us; the launch traced here: 32 us
  Pallas kernels  15.8 us (49%)
  starting transfers between devices  10.5 us (33%)
  waiting for transfers between devices  4.96 us (15%)
  between operations  0.77 us (2%)
    pallas_call x4, Pallas kernels, intra(): pl.pallas_call(functools.partial(intra_kernel, first, heads, len(through)...  6.2 us
    ppermute x4, starting transfers between devices, shards(): swap = lambda x: lax.ppermute(x, 'seq', [(c, c ^ 1) for c in range(count)])  4.37 us
    pallas_call x2, Pallas kernels, finish(): pl.pallas_call(functools.partial(final_kernel, groups, unread), in_specs=...  4.37 us
    ppermute x3, waiting for transfers between devices, shards(): lax.ppermute(x, 'seq', [(c, (c + 2) % count) for c in range(count)])  4.25 us
    ppermute x3, starting transfers between devices, shards(): lax.ppermute(x, 'seq', [(c, (c + 2) % count) for c in range(count)])  3.81 us
    pallas_call x1, Pallas kernels, rest_messages(): pl.pallas_call(functools.partial(rest_kernel, chunks, done), in_specs=[pl...  2.97 us
    ppermute x1, starting transfers between devices, shards(): lax.ppermute(x, 'seq', [(c, c + 2) for c in range(count - 2)])  2.31 us
    pallas_call x1, Pallas kernels, first_message(): pl.pallas_call(functools.partial(first_kernel, heads, chunks), in_specs=[...  1.72 us
  transfers between devices with their start and end apart: 8, of which 4 were waited for; matrix products, arithmetic and copies ran while one was open for 0% of the time, Pallas kernels for 37%

profile of v7, /device:TPU:0, one launch (start us, length us, event | category | flops | bytes accessed | tf_op | source)
XLA Modules:
  0.0 32.0 jit_solution(5137238305480257541)
XLA Ops:
  0.6 1.7 %first_message.1 = (f32[520,128]{1,0:T(8,128)S(1)}, f32[16,512]{1,0:T(8,128)S(1)}, f32[16,512]{1,0:T(8,128)S(1)}, s32[1,512]{1,0:T(1,128)S(1)}, bf16[512,512]{1,...) custom-call(s32[1]{0:T(128)} %bitcast.order_ref.refs_0_, ...), custom_call_target="tpu_custom_call" | custom-call | flops 1 | bytes 1 | tf_op jit(solution)/shard_map/first_message/pallas_call | solution.py:103
  2.4 3.0 %collective-permute-start.3 = (f32[520,128]{1,0:T(8,128)S(1)}, f32[520,128]{1,0:T(8,128)S(1)}, u32[]{:S(2)}, u32[]{:S(2)}) collective-permute-start(f32[520,128]{1,0:T(8,128)S(1)} %get-tuple-element.59.refs_1_.rest_7_), channel_id=1, source_target_pairs={{0,2},{2,0},{4,6},{6,4},{8,10},{10,8},{12,14},{14,12},{1,3},{3,1},... | collective-permute-start | bytes 798728 | tf_op jit(solution)/shard_map/ppermute | solution.py:430
  5.4 0.4 %second_message.1.even_ref.rest_0_ = f32[520,128]{1,0:T(8,128)S(1)} custom-call(s32[1,512]{1,0:T(1,128)S(1)} %get-tuple-element.43.seg_ref, f32[16,512]{1,0:T(8,128)S(1)} %get-tuple-element.44.a_ref, f32[16,512]{1,0:T(8,128)S(1)} %get-tuple-element.45.w_ref, bf16[512,512]{1,0:T(8,128)(2,1)S(1)} %get-tuple-element.57.k_ref, ...), custom_call_target="tpu_custom_call" | custom-call | flops 1 | bytes 1 | tf_op jit(solution)/shard_map/second_message/pallas_call | solution.py:130
  5.7 0.0 copy-start
  5.7 1.6 %collective-permute-start.2 = (f32[520,128]{1,0:T(8,128)S(1)}, f32[520,128]{1,0:T(8,128)S(1)}, u32[]{:S(2)}, u32[]{:S(2)}) collective-permute-start(f32[520,128]{1,0:T(8,128)S(1)} %second_message.1.even_ref.rest_0_), channel_id=1, source_target_pairs={{0,4},{2,6},{4,8},{6,10},{8,12},{10,14},{12,0},{14,2},{1,5},{3,7},... | collective-permute-start | bytes 798728 | tf_op jit(solution)/shard_map/ppermute | solution.py:431
  7.4 3.0 %rest_messages.1 = (f32[520,128]{1,0:T(8,128)S(1)}, f32[520,128]{1,0:T(8,128)S(1)}, f32[512,512]{1,0:T(8,128)S(1)}, bf16[512,512]{1,0:T(8,128)(2,1)S(1)}, bf16[5...) custom-call(s32[1,512]{1,0:T(1,128)S(1)} %get-tuple-element.43.seg_r, ...), custom_call_target="tpu_custom_call" | custom-call | flops 1 | bytes 1 | tf_op jit(solution)/shard_map/rest_messages/pallas_call | solution.py:177
  10.3 0.6 %collective-permute-start.1 = (f32[520,128]{1,0:T(8,128)S(1)}, f32[520,128]{1,0:T(8,128)S(1)}, u32[]{:S(2)}, u32[]{:S(2)}) collective-permute-start(f32[520,128]{1,0:T(8,128)S(1)} %get-tuple-element.47.refs_1_.rest_7_), channel_id=1, source_target_pairs={{0,2},{2,0},{4,6},{6,4},{8,10},{10,8},{12,14},{14,12},{1,3},{3,1},... | collective-permute-start | bytes 798728 | tf_op jit(solution)/shard_map/ppermute | solution.py:430
  11.0 1.6 %collective-permute-start = (f32[520,128]{1,0:T(8,128)S(1)}, f32[520,128]{1,0:T(8,128)S(1)}, u32[]{:S(2)}, u32[]{:S(2)}) collective-permute-start(f32[520,128]{1,0:T(8,128)S(1)} %get-tuple-element.46.even_ref.rest_0_), channel_id=1, source_target_pairs={{0,4},{2,6},{4,8},{6,10},{8,12},{10,14},{12,0},{14,2},{1,5},{3,7},... | collective-permute-start | bytes 798728 | tf_op jit(solution)/shard_map/ppermute | solution.py:431
  12.5 1.5 %intra_span.4 = (f32[512,512]{1,0:T(8,128)S(1)}, f32[512,512]{1,0:T(8,128)S(1)}, f32[512,512]{1,0:T(8,128)S(1)}) custom-call(f32[512,512]{1,0:T(8,128)S(1)} %get-tuple-element.48.mask_ref, f32[16,512]{1,0:T(8,128)S(1)} %get-tuple-element.44.a_ref, f32[1,2048]{1,0:T(1,128)S(1)} %bitcast.4, bf16[512,512]{1,0:T(8,128)(2,1)S(1)} %get-tuple-element.60.q_ref.rest_6_, ...), custom_call_target="tpu_custom_call" | custom-call | flops 1 | bytes 1 | tf_op jit(solution)/shard_map/intra_span/pallas_call | solution.py:306
  14.1 0.1 join_windows.2.refs_0_
  14.1 2.5 %collective-permute-done.2.odd_ref.rest_2_ = f32[520,128]{1,0:T(8,128)S(1)} collective-permute-done((f32[520,128]{1,0:T(8,128)S(1)}, f32[520,128]{1,0:T(8,128)S(1)}, u32[]{:S(2)}, u32[]{:S(2)}) %collective-permute-start.2) | collective-permute-done | bytes 266272 | tf_op jit(solution)/shard_map/ppermute | solution.py:431
  16.7 0.1 collective-permute-start.6
  16.7 0.6 %collective-permute-start.7 = (f32[520,128]{1,0:T(8,128)S(1)}, f32[520,128]{1,0:T(8,128)S(1)}, u32[]{:S(2)}, u32[]{:S(2)}) collective-permute-start(f32[520,128]{1,0:T(8,128)S(1)} %get-tuple-element.79), channel_id=1, source_target_pairs={{0,4},{2,6},{4,8},{6,10},{8,12},{10,14},{12,0},{14,2},{1,5},{3,7},... | collective-permute-start | bytes 798728 | tf_op jit(solution)/shard_map/ppermute | solution.py:431
  17.3 1.6 %intra_span.5 = (f32[512,512]{1,0:T(8,128)S(1)}, f32[512,512]{1,0:T(8,128)S(1)}, f32[512,512]{1,0:T(8,128)S(1)}) custom-call(f32[512,512]{1,0:T(8,128)S(1)} %get-tuple-element.48.mask_ref, f32[16,512]{1,0:T(8,128)S(1)} %get-tuple-element.44.a_ref, f32[1,2048]{1,0:T(1,128)S(1)} %bitcast.5, bf16[512,512]{1,0:T(8,128)(2,1)S(1)} %get-tuple-element.53.q_ref.rest_13_, ...), custom_call_target="tpu_custom_call" | custom-call | flops 1 | bytes 1 | tf_op jit(solution)/shard_map/intra_span/pallas_call | solution.py:306
  18.9 1.6 %intra_span.6 = (f32[512,512]{1,0:T(8,128)S(1)}, f32[512,512]{1,0:T(8,128)S(1)}, f32[512,512]{1,0:T(8,128)S(1)}) custom-call(f32[512,512]{1,0:T(8,128)S(1)} %get-tuple-element.48.mask_ref, f32[16,512]{1,0:T(8,128)S(1)} %get-tuple-element.44.a_ref, f32[1,2048]{1,0:T(1,128)S(1)} %bitcast.6, bf16[512,512]{1,0:T(8,128)(2,1)S(1)} %get-tuple-element.49.q_ref.rest_6_, ...), custom_call_target="tpu_custom_call" | custom-call | flops 1 | bytes 1 | tf_op jit(solution)/shard_map/intra_span/pallas_call | solution.py:306
  20.5 0.1 join_windows.3.refs_0_
  20.5 1.8 %collective-permute-done.odd_ref.rest_2_ = f32[520,128]{1,0:T(8,128)S(1)} collective-permute-done((f32[520,128]{1,0:T(8,128)S(1)}, f32[520,128]{1,0:T(8,128)S(1)}, u32[]{:S(2)}, u32[]{:S(2)}) %collective-permute-start) | collective-permute-done | bytes 266272 | tf_op jit(solution)/shard_map/ppermute | solution.py:431
  22.4 0.7 %collective-permute-start.4 = (f32[520,128]{1,0:T(8,128)S(1)}, f32[520,128]{1,0:T(8,128)S(1)}, u32[]{:S(2)}, u32[]{:S(2)}) collective-permute-start(f32[520,128]{1,0:T(8,128)S(1)} %get-tuple-element.66.refs_0_), channel_id=1, source_target_pairs={{0,2},{2,0},{4,6},{6,4},{8,10},{10,8},{12,14},{14,12},{1,3},{3,1},... | collective-permute-start | bytes 798728 | tf_op jit(solution)/shard_map/ppermute | solution.py:430
  23.1 2.3 %collective-permute-start.5 = (f32[520,128]{1,0:T(8,128)S(1)}, f32[520,128]{1,0:T(8,128)S(1)}, u32[]{:S(2)}, u32[]{:S(2)}) collective-permute-start(f32[520,128]{1,0:T(8,128)S(1)} %get-tuple-element.69), channel_id=1, source_target_pairs={{0,4},{2,6},{4,8},{6,10},{8,12},{10,14},{1,5},{3,7},{5,9},{7,11},{... | collective-permute-start | bytes 798728 | tf_op jit(solution)/shard_map/ppermute | solution.py:432
  25.4 1.6 %intra_span.7 = (f32[512,512]{1,0:T(8,128)S(1)}, f32[512,512]{1,0:T(8,128)S(1)}, f32[512,512]{1,0:T(8,128)S(1)}) custom-call(f32[512,512]{1,0:T(8,128)S(1)} %get-tuple-element.48.mask_ref, f32[16,512]{1,0:T(8,128)S(1)} %get-tuple-element.44.a_ref, f32[1,2048]{1,0:T(1,128)S(1)} %bitcast.7, bf16[512,512]{1,0:T(8,128)(2,1)S(1)} %get-tuple-element.70.q_ref.rest_13_, ...), custom_call_target="tpu_custom_call" | custom-call | flops 1 | bytes 1 | tf_op jit(solution)/shard_map/intra_span/pallas_call | solution.py:306
  27.0 2.2 %finish.2 = (bf16[512,2048]{1,0:T(8,128)(2,1)}, f32[1,16,128,128]{3,2,1,0:T(8,128)}) custom-call(s32[1]{0:T(128)} %bitcast.order_ref.refs_0_, s32[1,512]{1,0:T(1,128)S(1)} %get-tuple-element.43.seg_ref, f32[520,128]{1,0:T(8,128)S(1)} %second_message.1.even_ref.rest_0_, f32[520,128]{1,0:T(8,128)S(1)} %collective-permute-done.6.rest_1_, ...), custom_call_target="tpu_custom_call" | custom-call | flops 1 | bytes 1 | tf_op jit(solution)/shard_map/finish/pallas_call | solution.py:400
  29.2 0.2 collective-permute-done.4.rest_1_
  29.4 0.5 %collective-permute-done.5.rest_9_ = f32[520,128]{1,0:T(8,128)S(1)} collective-permute-done((f32[520,128]{1,0:T(8,128)S(1)}, f32[520,128]{1,0:T(8,128)S(1)}, u32[]{:S(2)}, u32[]{:S(2)}) %collective-permute-start.5) | collective-permute-done | bytes 266272 | tf_op jit(solution)/shard_map/ppermute | solution.py:432
  29.9 2.2 %finish.3 = (bf16[512,2048]{1,0:T(8,128)(2,1)}, f32[1,16,128,128]{3,2,1,0:T(8,128)}) custom-call(s32[1]{0:T(128)} %bitcast.order_ref.refs_0_, s32[1,512]{1,0:T(1,128)S(1)} %get-tuple-element.43.seg_ref, f32[520,128]{1,0:T(8,128)S(1)} %get-tuple-element.46.even_ref.rest_0_, ...), custom_call_target="tpu_custom_call", output_to_operand_aliasing={{0}: (16, {}), {1}: (17, {})} | custom-call | flops 1 | bytes 1 | tf_op jit(solution)/shard_map/finish/pallas_call | solution.py:400
  (7 shorter events, 0.1 us)
Async XLA Ops:
  2.4 11.7 %collective-permute-start.3 = (f32[520,128]{1,0:T(8,128)S(1)}, f32[520,128]{1,0:T(8,128)S(1)}, u32[]{:S(2)}, u32[]{:S(2)}) collective-permute-start(f32[520,128]{1,0:T(8,128)S(1)} %get-tuple-element.59.refs_1_.rest_7_), channel_id=1, source_target_pairs={{0,2},{2,0},{4,6},{6,4},{8,10},{10,8},{12,14},{14,12},{1,3},{3,1},... | collective-permute-start | bytes 798728 | tf_op jit(solution)/shard_map/ppermute | solution.py:430
  5.7 6.8 %copy-start = (f32[2048]{0:T(1024)S(1)}, f32[2048]{0:T(1024)}, u32[]{:S(2)}) copy-start(f32[2048]{0:T(1024)} %param.15) | copy-start | bytes 24580
  5.7 10.9 %collective-permute-start.2 = (f32[520,128]{1,0:T(8,128)S(1)}, f32[520,128]{1,0:T(8,128)S(1)}, u32[]{:S(2)}, u32[]{:S(2)}) collective-permute-start(f32[520,128]{1,0:T(8,128)S(1)} %second_message.1.even_ref.rest_0_), channel_id=1, source_target_pairs={{0,4},{2,6},{4,8},{6,10},{8,12},{10,14},{12,0},{14,2},{1,5},{3,7},... | collective-permute-start | bytes 798728 | tf_op jit(solution)/shard_map/ppermute | solution.py:431
  10.3 10.1 %collective-permute-start.1 = (f32[520,128]{1,0:T(8,128)S(1)}, f32[520,128]{1,0:T(8,128)S(1)}, u32[]{:S(2)}, u32[]{:S(2)}) collective-permute-start(f32[520,128]{1,0:T(8,128)S(1)} %get-tuple-element.47.refs_1_.rest_7_), channel_id=1, source_target_pairs={{0,2},{2,0},{4,6},{6,4},{8,10},{10,8},{12,14},{14,12},{1,3},{3,1},... | collective-permute-start | bytes 798728 | tf_op jit(solution)/shard_map/ppermute | solution.py:430
  11.0 11.4 %collective-permute-start = (f32[520,128]{1,0:T(8,128)S(1)}, f32[520,128]{1,0:T(8,128)S(1)}, u32[]{:S(2)}, u32[]{:S(2)}) collective-permute-start(f32[520,128]{1,0:T(8,128)S(1)} %get-tuple-element.46.even_ref.rest_0_), channel_id=1, source_target_pairs={{0,4},{2,6},{4,8},{6,10},{8,12},{10,14},{12,0},{14,2},{1,5},{3,7},... | collective-permute-start | bytes 798728 | tf_op jit(solution)/shard_map/ppermute | solution.py:431
  16.7 10.3 %collective-permute-start.6 = (f32[520,128]{1,0:T(8,128)S(1)}, f32[520,128]{1,0:T(8,128)S(1)}, u32[]{:S(2)}, u32[]{:S(2)}) collective-permute-start(f32[520,128]{1,0:T(8,128)S(1)} %get-tuple-element.63.refs_0_), channel_id=1, source_target_pairs={{0,2},{2,0},{4,6},{6,4},{8,10},{10,8},{12,14},{14,12},{1,3},{3,1},... | collective-permute-start | bytes 798728 | tf_op jit(solution)/shard_map/ppermute | solution.py:430
  16.7 10.2 %collective-permute-start.7 = (f32[520,128]{1,0:T(8,128)S(1)}, f32[520,128]{1,0:T(8,128)S(1)}, u32[]{:S(2)}, u32[]{:S(2)}) collective-permute-start(f32[520,128]{1,0:T(8,128)S(1)} %get-tuple-element.79), channel_id=1, source_target_pairs={{0,4},{2,6},{4,8},{6,10},{8,12},{10,14},{12,0},{14,2},{1,5},{3,7},... | collective-permute-start | bytes 798728 | tf_op jit(solution)/shard_map/ppermute | solution.py:431
  22.4 7.0 %collective-permute-start.4 = (f32[520,128]{1,0:T(8,128)S(1)}, f32[520,128]{1,0:T(8,128)S(1)}, u32[]{:S(2)}, u32[]{:S(2)}) collective-permute-start(f32[520,128]{1,0:T(8,128)S(1)} %get-tuple-element.66.refs_0_), channel_id=1, source_target_pairs={{0,2},{2,0},{4,6},{6,4},{8,10},{10,8},{12,14},{14,12},{1,3},{3,1},... | collective-permute-start | bytes 798728 | tf_op jit(solution)/shard_map/ppermute | solution.py:430
  23.1 6.8 %collective-permute-start.5 = (f32[520,128]{1,0:T(8,128)S(1)}, f32[520,128]{1,0:T(8,128)S(1)}, u32[]{:S(2)}, u32[]{:S(2)}) collective-permute-start(f32[520,128]{1,0:T(8,128)S(1)} %get-tuple-element.69), channel_id=1, source_target_pairs={{0,4},{2,6},{4,8},{6,10},{8,12},{10,14},{1,5},{3,7},{5,9},{7,11},{... | collective-permute-start | bytes 798728 | tf_op jit(solution)/shard_map/ppermute | solution.py:432

commit v8 on v7

--- a/solution.py
+++ b/solution.py
@@ -330,7 +330,6 @@
 
     for i, (first, heads, kind) in enumerate(groups):
         own_ref, near_ref, past_ref = inputs[7 * i : 7 * i + 3]
-        gated_ref, snap_ref = scratch[2 * i : 2 * i + 2]
         size = own_ref.shape[1]
         top = heads * size
         ends = slice(top + heads, top + heads + 1)
@@ -351,40 +350,60 @@
         number_valid = jnp.sum(
             jnp.where(seg == previous[:, :1], 1.0, 0.0), axis=1, keepdims=True
         )
-        for j in range(heads):
-            rows = slice(j * size, (j + 1) * size)
-            state = scale_past[j : j + 1] * past_ref[rows, :] + scale_near * near_ref[rows, :]
-            snap_ref[j] = own_decay[j : j + 1] * state + own_ref[rows, :]
-            high = state.astype(BF16)
-            low = (state - high.astype(F32)).astype(BF16)
-            both = jnp.concatenate([high, low], axis=0)
-            work.append((i, j, first, heads, both, number_valid, inputs[7 * i + 3 : 7 * i + 7]))
-        send(snap_ref, snap_hbm.at[0, pl.ds(first, heads)])
-
-    rows = lax.broadcasted_iota(jnp.int32, (64, 128), 0).astype(F32)
-    for number, (i, j, first, heads, both, number_valid, arrays) in enumerate(work):
-        o_ref, gate_ref, decay_ref, q_ref = arrays
+        scales = scale_near, scale_past, own_decay, number_valid
+        work += [(i, j, first, heads, scales) for j in range(heads)]
+
+    tokens, size = seg.shape[1], inter_ref.shape[2]
+    count_rows = lax.broadcasted_iota(jnp.int32, (64, size), 0).astype(F32)
+    halves = {}
+
+    def state_of(n):
+        i, j, first, heads, (scale_near, scale_past, own_decay, _) = work[n]
+        own_ref, near_ref, past_ref = inputs[7 * i : 7 * i + 3]
+        snap_ref = scratch[2 * i + 1]
+        rows = slice(j * size, (j + 1) * size)
+        state = scale_past[j : j + 1] * past_ref[rows, :] + scale_near * near_ref[rows, :]
+        snap_ref[j] = own_decay[j : j + 1] * state + own_ref[rows, :]
+        high = state.astype(BF16)
+        low = (state - high.astype(F32)).astype(BF16)
+        halves[n] = jnp.concatenate([high, low], axis=0)
+        if j == heads - 1:
+            send(snap_ref, snap_hbm.at[0, pl.ds(first, heads)])
+
+    def product_of(n):
+        i, j = work[n][:2]
+        q = inputs[7 * i + 6][:, j * size : (j + 1) * size]
+        inter_ref[n % 4] = lax.dot_general(
+            jnp.concatenate([q, q], axis=1), halves.pop(n), NN, preferred_element_type=F32
+        )
+
+    def output_of(n):
+        i, j, first, heads, (*_, number_valid) = work[n]
+        o_ref, gate_ref, decay_ref = inputs[7 * i + 3 : 7 * i + 6]
         gated_ref = scratch[2 * i]
-        tokens, size = seg.shape[1], q_ref.shape[1] // heads
         columns = slice(j * size, (j + 1) * size)
-        q = q_ref[:, columns]
-        inter_ref[number % 4] = lax.dot_general(
-            jnp.concatenate([q, q], axis=1), both, NN, preferred_element_type=F32
-        )
         for start in range(0, tokens, 64):
             here = slice(start, start + 64)
-            inter = inter_ref[number % 4, here, :]
-            inter = jnp.where(rows < number_valid - start, inter * decay_ref[here, columns], 0.0)
+            inter = inter_ref[n % 4, here, :] * decay_ref[here, columns]
+            inter = jnp.where(count_rows < number_valid - start, inter, 0.0)
             mixed = o_ref[here, columns] + inter
             square = jnp.sum(mixed * mixed, axis=1, keepdims=True)
             gated = mixed * lax.rsqrt(square + size * 1e-06) * gate_ref[here, columns]
             gated_ref[here, columns] = gated.astype(BF16)
-        alone = number + 2 >= len(work)
+        alone = n + 2 >= len(work)
         if alone or j % 2 == 1 or j == heads - 1:
             begin = j if alone else j - j % 2
             width = (j + 1 - begin) * size
             there = pl.ds((first + begin) * size, width)
             send(gated_ref.at[:, pl.ds(begin * size, width)], gated_hbm.at[:, there])
+
+    for n in range(len(work) + 2):
+        if n < len(work):
+            state_of(n)
+        if 0 <= n - 1 < len(work):
+            product_of(n - 1)
+        if n >= 2:
+            output_of(n - 2)
     for copy in copies:
         copy.wait()
 

time: 32.2 us -> 32.2 us (level)
  no operation moved by 1% of the time
where the time goes in v8:
time: 32.2 us; the launch traced here: 32 us
  Pallas kernels  15.8 us (49%)
  starting transfers between devices  10.5 us (33%)
  waiting for transfers between devices  4.97 us (15%)
  between operations  0.77 us (2%)
    pallas_call x4, Pallas kernels, intra(): pl.pallas_call(functools.partial(intra_kernel, first, heads, len(through)...  6.2 us
    ppermute x4, starting transfers between devices, shards(): swap = lambda x: lax.ppermute(x, 'seq', [(c, c ^ 1) for c in range(count)])  4.37 us
    pallas_call x2, Pallas kernels, finish(): pl.pallas_call(functools.partial(final_kernel, groups, unread), in_specs=...  4.37 us
    ppermute x3, waiting for transfers between devices, shards(): lax.ppermute(x, 'seq', [(c, (c + 2) % count) for c in range(count)])  4.25 us
    ppermute x3, starting transfers between devices, shards(): lax.ppermute(x, 'seq', [(c, (c + 2) % count) for c in range(count)])  3.81 us
    pallas_call x1, Pallas kernels, rest_messages(): pl.pallas_call(functools.partial(rest_kernel, chunks, done), in_specs=[pl...  2.97 us
    ppermute x1, starting transfers between devices, shards(): lax.ppermute(x, 'seq', [(c, c + 2) for c in range(count - 2)])  2.31 us
    pallas_call x1, Pallas kernels, first_message(): pl.pallas_call(functools.partial(first_kernel, heads, chunks), in_specs=[...  1.72 us
  transfers between devices with their start and end apart: 8, of which 4 were waited for; matrix products, arithmetic and copies ran while one was open for 0% of the time, Pallas kernels for 37%

profile of v8, /device:TPU:0, one launch (start us, length us, event | category | flops | bytes accessed | tf_op | source)
XLA Modules:
  0.0 32.0 jit_solution(10775608487602481826)
XLA Ops:
  0.6 1.7 %first_message.1 = (f32[520,128]{1,0:T(8,128)S(1)}, f32[16,512]{1,0:T(8,128)S(1)}, f32[16,512]{1,0:T(8,128)S(1)}, s32[1,512]{1,0:T(1,128)S(1)}, bf16[512,512]{1,...) custom-call(s32[1]{0:T(128)} %bitcast.order_ref.refs_0_, ...), custom_call_target="tpu_custom_call" | custom-call | flops 1 | bytes 1 | tf_op jit(solution)/shard_map/first_message/pallas_call | solution.py:103
  2.4 3.0 %collective-permute-start.3 = (f32[520,128]{1,0:T(8,128)S(1)}, f32[520,128]{1,0:T(8,128)S(1)}, u32[]{:S(2)}, u32[]{:S(2)}) collective-permute-start(f32[520,128]{1,0:T(8,128)S(1)} %get-tuple-element.59.refs_1_.rest_7_), channel_id=1, source_target_pairs={{0,2},{2,0},{4,6},{6,4},{8,10},{10,8},{12,14},{14,12},{1,3},{3,1},... | collective-permute-start | bytes 798728 | tf_op jit(solution)/shard_map/ppermute | solution.py:449
  5.4 0.4 %second_message.1.even_ref.rest_0_ = f32[520,128]{1,0:T(8,128)S(1)} custom-call(s32[1,512]{1,0:T(1,128)S(1)} %get-tuple-element.43.seg_ref, f32[16,512]{1,0:T(8,128)S(1)} %get-tuple-element.44.a_ref, f32[16,512]{1,0:T(8,128)S(1)} %get-tuple-element.45.w_ref, bf16[512,512]{1,0:T(8,128)(2,1)S(1)} %get-tuple-element.57.k_ref, ...), custom_call_target="tpu_custom_call" | custom-call | flops 1 | bytes 1 | tf_op jit(solution)/shard_map/second_message/pallas_call | solution.py:130
  5.7 0.0 copy-start
  5.7 1.6 %collective-permute-start.2 = (f32[520,128]{1,0:T(8,128)S(1)}, f32[520,128]{1,0:T(8,128)S(1)}, u32[]{:S(2)}, u32[]{:S(2)}) collective-permute-start(f32[520,128]{1,0:T(8,128)S(1)} %second_message.1.even_ref.rest_0_), channel_id=1, source_target_pairs={{0,4},{2,6},{4,8},{6,10},{8,12},{10,14},{12,0},{14,2},{1,5},{3,7},... | collective-permute-start | bytes 798728 | tf_op jit(solution)/shard_map/ppermute | solution.py:450
  7.4 3.0 %rest_messages.1 = (f32[520,128]{1,0:T(8,128)S(1)}, f32[520,128]{1,0:T(8,128)S(1)}, f32[512,512]{1,0:T(8,128)S(1)}, bf16[512,512]{1,0:T(8,128)(2,1)S(1)}, bf16[5...) custom-call(s32[1,512]{1,0:T(1,128)S(1)} %get-tuple-element.43.seg_r, ...), custom_call_target="tpu_custom_call" | custom-call | flops 1 | bytes 1 | tf_op jit(solution)/shard_map/rest_messages/pallas_call | solution.py:177
  10.3 0.6 %collective-permute-start.1 = (f32[520,128]{1,0:T(8,128)S(1)}, f32[520,128]{1,0:T(8,128)S(1)}, u32[]{:S(2)}, u32[]{:S(2)}) collective-permute-start(f32[520,128]{1,0:T(8,128)S(1)} %get-tuple-element.47.refs_1_.rest_7_), channel_id=1, source_target_pairs={{0,2},{2,0},{4,6},{6,4},{8,10},{10,8},{12,14},{14,12},{1,3},{3,1},... | collective-permute-start | bytes 798728 | tf_op jit(solution)/shard_map/ppermute | solution.py:449
  11.0 1.6 %collective-permute-start = (f32[520,128]{1,0:T(8,128)S(1)}, f32[520,128]{1,0:T(8,128)S(1)}, u32[]{:S(2)}, u32[]{:S(2)}) collective-permute-start(f32[520,128]{1,0:T(8,128)S(1)} %get-tuple-element.46.even_ref.rest_0_), channel_id=1, source_target_pairs={{0,4},{2,6},{4,8},{6,10},{8,12},{10,14},{12,0},{14,2},{1,5},{3,7},... | collective-permute-start | bytes 798728 | tf_op jit(solution)/shard_map/ppermute | solution.py:450
  12.5 1.5 %intra_span.4 = (f32[512,512]{1,0:T(8,128)S(1)}, f32[512,512]{1,0:T(8,128)S(1)}, f32[512,512]{1,0:T(8,128)S(1)}) custom-call(f32[512,512]{1,0:T(8,128)S(1)} %get-tuple-element.48.mask_ref, f32[16,512]{1,0:T(8,128)S(1)} %get-tuple-element.44.a_ref, f32[1,2048]{1,0:T(1,128)S(1)} %bitcast.4, bf16[512,512]{1,0:T(8,128)(2,1)S(1)} %get-tuple-element.60.q_ref.rest_6_, ...), custom_call_target="tpu_custom_call" | custom-call | flops 1 | bytes 1 | tf_op jit(solution)/shard_map/intra_span/pallas_call | solution.py:306
  14.1 0.1 join_windows.2.refs_0_
  14.1 2.5 %collective-permute-done.2.odd_ref.rest_2_ = f32[520,128]{1,0:T(8,128)S(1)} collective-permute-done((f32[520,128]{1,0:T(8,128)S(1)}, f32[520,128]{1,0:T(8,128)S(1)}, u32[]{:S(2)}, u32[]{:S(2)}) %collective-permute-start.2) | collective-permute-done | bytes 266272 | tf_op jit(solution)/shard_map/ppermute | solution.py:450
  16.7 0.1 collective-permute-start.6
  16.7 0.6 %collective-permute-start.7 = (f32[520,128]{1,0:T(8,128)S(1)}, f32[520,128]{1,0:T(8,128)S(1)}, u32[]{:S(2)}, u32[]{:S(2)}) collective-permute-start(f32[520,128]{1,0:T(8,128)S(1)} %get-tuple-element.79), channel_id=1, source_target_pairs={{0,4},{2,6},{4,8},{6,10},{8,12},{10,14},{12,0},{14,2},{1,5},{3,7},... | collective-permute-start | bytes 798728 | tf_op jit(solution)/shard_map/ppermute | solution.py:450
  17.3 1.6 %intra_span.5 = (f32[512,512]{1,0:T(8,128)S(1)}, f32[512,512]{1,0:T(8,128)S(1)}, f32[512,512]{1,0:T(8,128)S(1)}) custom-call(f32[512,512]{1,0:T(8,128)S(1)} %get-tuple-element.48.mask_ref, f32[16,512]{1,0:T(8,128)S(1)} %get-tuple-element.44.a_ref, f32[1,2048]{1,0:T(1,128)S(1)} %bitcast.5, bf16[512,512]{1,0:T(8,128)(2,1)S(1)} %get-tuple-element.53.q_ref.rest_13_, ...), custom_call_target="tpu_custom_call" | custom-call | flops 1 | bytes 1 | tf_op jit(solution)/shard_map/intra_span/pallas_call | solution.py:306
  18.9 1.6 %intra_span.6 = (f32[512,512]{1,0:T(8,128)S(1)}, f32[512,512]{1,0:T(8,128)S(1)}, f32[512,512]{1,0:T(8,128)S(1)}) custom-call(f32[512,512]{1,0:T(8,128)S(1)} %get-tuple-element.48.mask_ref, f32[16,512]{1,0:T(8,128)S(1)} %get-tuple-element.44.a_ref, f32[1,2048]{1,0:T(1,128)S(1)} %bitcast.6, bf16[512,512]{1,0:T(8,128)(2,1)S(1)} %get-tuple-element.49.q_ref.rest_6_, ...), custom_call_target="tpu_custom_call" | custom-call | flops 1 | bytes 1 | tf_op jit(solution)/shard_map/intra_span/pallas_call | solution.py:306
  20.5 0.1 join_windows.3.refs_0_
  20.5 1.8 %collective-permute-done.odd_ref.rest_2_ = f32[520,128]{1,0:T(8,128)S(1)} collective-permute-done((f32[520,128]{1,0:T(8,128)S(1)}, f32[520,128]{1,0:T(8,128)S(1)}, u32[]{:S(2)}, u32[]{:S(2)}) %collective-permute-start) | collective-permute-done | bytes 266272 | tf_op jit(solution)/shard_map/ppermute | solution.py:450
  22.4 0.7 %collective-permute-start.4 = (f32[520,128]{1,0:T(8,128)S(1)}, f32[520,128]{1,0:T(8,128)S(1)}, u32[]{:S(2)}, u32[]{:S(2)}) collective-permute-start(f32[520,128]{1,0:T(8,128)S(1)} %get-tuple-element.66.refs_0_), channel_id=1, source_target_pairs={{0,2},{2,0},{4,6},{6,4},{8,10},{10,8},{12,14},{14,12},{1,3},{3,1},... | collective-permute-start | bytes 798728 | tf_op jit(solution)/shard_map/ppermute | solution.py:449
  23.1 2.3 %collective-permute-start.5 = (f32[520,128]{1,0:T(8,128)S(1)}, f32[520,128]{1,0:T(8,128)S(1)}, u32[]{:S(2)}, u32[]{:S(2)}) collective-permute-start(f32[520,128]{1,0:T(8,128)S(1)} %get-tuple-element.69), channel_id=1, source_target_pairs={{0,4},{2,6},{4,8},{6,10},{8,12},{10,14},{1,5},{3,7},{5,9},{7,11},{... | collective-permute-start | bytes 798728 | tf_op jit(solution)/shard_map/ppermute | solution.py:451
  25.4 1.6 %intra_span.7 = (f32[512,512]{1,0:T(8,128)S(1)}, f32[512,512]{1,0:T(8,128)S(1)}, f32[512,512]{1,0:T(8,128)S(1)}) custom-call(f32[512,512]{1,0:T(8,128)S(1)} %get-tuple-element.48.mask_ref, f32[16,512]{1,0:T(8,128)S(1)} %get-tuple-element.44.a_ref, f32[1,2048]{1,0:T(1,128)S(1)} %bitcast.7, bf16[512,512]{1,0:T(8,128)(2,1)S(1)} %get-tuple-element.70.q_ref.rest_13_, ...), custom_call_target="tpu_custom_call" | custom-call | flops 1 | bytes 1 | tf_op jit(solution)/shard_map/intra_span/pallas_call | solution.py:306
  27.0 2.2 %finish.2 = (bf16[512,2048]{1,0:T(8,128)(2,1)}, f32[1,16,128,128]{3,2,1,0:T(8,128)}) custom-call(s32[1]{0:T(128)} %bitcast.order_ref.refs_0_, s32[1,512]{1,0:T(1,128)S(1)} %get-tuple-element.43.seg_ref, f32[520,128]{1,0:T(8,128)S(1)} %second_message.1.even_ref.rest_0_, f32[520,128]{1,0:T(8,128)S(1)} %collective-permute-done.6.rest_1_, ...), custom_call_target="tpu_custom_call" | custom-call | flops 1 | bytes 1 | tf_op jit(solution)/shard_map/finish/pallas_call | solution.py:419
  29.1 0.3 collective-permute-done.4.rest_1_
  29.4 0.5 %collective-permute-done.5.rest_9_ = f32[520,128]{1,0:T(8,128)S(1)} collective-permute-done((f32[520,128]{1,0:T(8,128)S(1)}, f32[520,128]{1,0:T(8,128)S(1)}, u32[]{:S(2)}, u32[]{:S(2)}) %collective-permute-start.5) | collective-permute-done | bytes 266272 | tf_op jit(solution)/shard_map/ppermute | solution.py:451
  29.9 2.2 %finish.3 = (bf16[512,2048]{1,0:T(8,128)(2,1)}, f32[1,16,128,128]{3,2,1,0:T(8,128)}) custom-call(s32[1]{0:T(128)} %bitcast.order_ref.refs_0_, s32[1,512]{1,0:T(1,128)S(1)} %get-tuple-element.43.seg_ref, f32[520,128]{1,0:T(8,128)S(1)} %get-tuple-element.46.even_ref.rest_0_, ...), custom_call_target="tpu_custom_call", output_to_operand_aliasing={{0}: (16, {}), {1}: (17, {})} | custom-call | flops 1 | bytes 1 | tf_op jit(solution)/shard_map/finish/pallas_call | solution.py:419
  (7 shorter events, 0.1 us)
Async XLA Ops:
  2.4 11.7 %collective-permute-start.3 = (f32[520,128]{1,0:T(8,128)S(1)}, f32[520,128]{1,0:T(8,128)S(1)}, u32[]{:S(2)}, u32[]{:S(2)}) collective-permute-start(f32[520,128]{1,0:T(8,128)S(1)} %get-tuple-element.59.refs_1_.rest_7_), channel_id=1, source_target_pairs={{0,2},{2,0},{4,6},{6,4},{8,10},{10,8},{12,14},{14,12},{1,3},{3,1},... | collective-permute-start | bytes 798728 | tf_op jit(solution)/shard_map/ppermute | solution.py:449
  5.7 6.8 %copy-start = (f32[2048]{0:T(1024)S(1)}, f32[2048]{0:T(1024)}, u32[]{:S(2)}) copy-start(f32[2048]{0:T(1024)} %param.15) | copy-start | bytes 24580
  5.7 10.9 %collective-permute-start.2 = (f32[520,128]{1,0:T(8,128)S(1)}, f32[520,128]{1,0:T(8,128)S(1)}, u32[]{:S(2)}, u32[]{:S(2)}) collective-permute-start(f32[520,128]{1,0:T(8,128)S(1)} %second_message.1.even_ref.rest_0_), channel_id=1, source_target_pairs={{0,4},{2,6},{4,8},{6,10},{8,12},{10,14},{12,0},{14,2},{1,5},{3,7},... | collective-permute-start | bytes 798728 | tf_op jit(solution)/shard_map/ppermute | solution.py:450
  10.3 10.1 %collective-permute-start.1 = (f32[520,128]{1,0:T(8,128)S(1)}, f32[520,128]{1,0:T(8,128)S(1)}, u32[]{:S(2)}, u32[]{:S(2)}) collective-permute-start(f32[520,128]{1,0:T(8,128)S(1)} %get-tuple-element.47.refs_1_.rest_7_), channel_id=1, source_target_pairs={{0,2},{2,0},{4,6},{6,4},{8,10},{10,8},{12,14},{14,12},{1,3},{3,1},... | collective-permute-start | bytes 798728 | tf_op jit(solution)/shard_map/ppermute | solution.py:449
  11.0 11.4 %collective-permute-start = (f32[520,128]{1,0:T(8,128)S(1)}, f32[520,128]{1,0:T(8,128)S(1)}, u32[]{:S(2)}, u32[]{:S(2)}) collective-permute-start(f32[520,128]{1,0:T(8,128)S(1)} %get-tuple-element.46.even_ref.rest_0_), channel_id=1, source_target_pairs={{0,4},{2,6},{4,8},{6,10},{8,12},{10,14},{12,0},{14,2},{1,5},{3,7},... | collective-permute-start | bytes 798728 | tf_op jit(solution)/shard_map/ppermute | solution.py:450
  16.7 10.3 %collective-permute-start.6 = (f32[520,128]{1,0:T(8,128)S(1)}, f32[520,128]{1,0:T(8,128)S(1)}, u32[]{:S(2)}, u32[]{:S(2)}) collective-permute-start(f32[520,128]{1,0:T(8,128)S(1)} %get-tuple-element.63.refs_0_), channel_id=1, source_target_pairs={{0,2},{2,0},{4,6},{6,4},{8,10},{10,8},{12,14},{14,12},{1,3},{3,1},... | collective-permute-start | bytes 798728 | tf_op jit(solution)/shard_map/ppermute | solution.py:449
  16.7 10.2 %collective-permute-start.7 = (f32[520,128]{1,0:T(8,128)S(1)}, f32[520,128]{1,0:T(8,128)S(1)}, u32[]{:S(2)}, u32[]{:S(2)}) collective-permute-start(f32[520,128]{1,0:T(8,128)S(1)} %get-tuple-element.79), channel_id=1, source_target_pairs={{0,4},{2,6},{4,8},{6,10},{8,12},{10,14},{12,0},{14,2},{1,5},{3,7},... | collective-permute-start | bytes 798728 | tf_op jit(solution)/shard_map/ppermute | solution.py:450
  22.4 7.0 %collective-permute-start.4 = (f32[520,128]{1,0:T(8,128)S(1)}, f32[520,128]{1,0:T(8,128)S(1)}, u32[]{:S(2)}, u32[]{:S(2)}) collective-permute-start(f32[520,128]{1,0:T(8,128)S(1)} %get-tuple-element.66.refs_0_), channel_id=1, source_target_pairs={{0,2},{2,0},{4,6},{6,4},{8,10},{10,8},{12,14},{14,12},{1,3},{3,1},... | collective-permute-start | bytes 798728 | tf_op jit(solution)/shard_map/ppermute | solution.py:449
  23.1 6.8 %collective-permute-start.5 = (f32[520,128]{1,0:T(8,128)S(1)}, f32[520,128]{1,0:T(8,128)S(1)}, u32[]{:S(2)}, u32[]{:S(2)}) collective-permute-start(f32[520,128]{1,0:T(8,128)S(1)} %get-tuple-element.69), channel_id=1, source_target_pairs={{0,4},{2,6},{4,8},{6,10},{8,12},{10,14},{1,5},{3,7},{5,9},{7,11},{... | collective-permute-start | bytes 798728 | tf_op jit(solution)/shard_map/ppermute | solution.py:451

commit v9 on v7

--- a/solution.py
+++ b/solution.py
@@ -51,10 +51,7 @@
     pairs = [(keep_hbm, keep_ref), (exponent_hbm, exponent_ref), (seg_hbm, seg_ref)]
     for i, (first, many) in enumerate(chunks):
         wide = pl.ds(first * size, many * size)
-        for start in (0, tokens // 2):
-            rows = pl.ds(start, tokens // 2)
-            for source, target in ((k_hbm, k_refs[i]), (v_hbm, v_refs[i])):
-                pairs.append((source.at[rows, wide], target.at[rows, :]))
+        pairs += [(k_hbm.at[:, wide], k_refs[i]), (v_hbm.at[:, wide], v_refs[i])]
     copies = [pltpu.make_async_copy(*pair, sems.at[i]) for i, pair in enumerate(pairs)]
     for copy in copies:
         copy.start()
@@ -80,12 +77,12 @@
     seg = seg_ref[...]
     last = seg[:, tokens - 1 :]
     w_ref[...] = jnp.where(seg == last, jnp.exp(final - cumulative), 0.0)
-    for copy in copies[3:7]:
+    for copy in copies[3:5]:
         copy.wait()
     first, many = chunks[0]
     finals = final[first : first + many]
     put_message(msg_ref, first, many, size, w_ref, finals, last, k_refs[0], v_refs[0])
-    for copy in copies[7:]:
+    for copy in copies[5:]:
         copy.wait()
 
 
@@ -109,7 +106,7 @@
         scratch_shapes=[
             pltpu.VMEM((1, heads), jnp.int32),
             pltpu.VMEM((heads, tokens), F32),
-            pltpu.SemaphoreType.DMA((3 + 4 * number,)),
+            pltpu.SemaphoreType.DMA((3 + 2 * number,)),
         ],
         compiler_params=pltpu.CompilerParams(vmem_limit_bytes=8 * MIB),
         cost_estimate=SHORT,
@@ -377,9 +374,15 @@
             inter = jnp.where(rows < number_valid - start, inter * decay_ref[here, columns], 0.0)
             mixed = o_ref[here, columns] + inter
             square = jnp.sum(mixed * mixed, axis=1, keepdims=True)
-            gated = mixed * lax.rsqrt(square + size * 1e-06) * gate_ref[here, columns]
+            gated = mixed * gate_ref[here, columns] * lax.rsqrt(square + size * 1e-06)
             gated_ref[here, columns] = gated.astype(BF16)
-        alone = number + 2 >= len(work)
+            if number == len(work) - 1 and start % 128 == 64:
+                block = pl.ds(start - 64, 128)
+                there = pl.ds((first + j) * size, size)
+                send(gated_ref.at[block, pl.ds(j * size, size)], gated_hbm.at[block, there])
+        if number == len(work) - 1:
+            continue
+        alone = number + 2 == len(work) and j % 2 == 0
         if alone or j % 2 == 1 or j == heads - 1:
             begin = j if alone else j - j % 2
             width = (j + 1 - begin) * size

time: 32.2 us -> 32.1 us (level)
  no operation moved by 1% of the time
where the time goes in v9:
time: 32.1 us; the launch traced here: 32 us
  Pallas kernels  15.7 us (49%)
  starting transfers between devices  10.5 us (33%)
  waiting for transfers between devices  5.01 us (16%)
  between operations  0.77 us (2%)
    pallas_call x4, Pallas kernels, intra(): pl.pallas_call(functools.partial(intra_kernel, first, heads, len(through)...  6.2 us
    ppermute x4, starting transfers between devices, shards(): swap = lambda x: lax.ppermute(x, 'seq', [(c, c ^ 1) for c in range(count)])  4.39 us
    pallas_call x2, Pallas kernels, finish(): pl.pallas_call(functools.partial(final_kernel, groups, unread), in_specs=...  4.29 us
    ppermute x3, waiting for transfers between devices, shards(): lax.ppermute(x, 'seq', [(c, (c + 2) % count) for c in range(count)])  4.25 us
    ppermute x3, starting transfers between devices, shards(): lax.ppermute(x, 'seq', [(c, (c + 2) % count) for c in range(count)])  3.81 us
    pallas_call x1, Pallas kernels, rest_messages(): pl.pallas_call(functools.partial(rest_kernel, chunks, done), in_specs=[pl...  2.97 us
    ppermute x1, starting transfers between devices, shards(): lax.ppermute(x, 'seq', [(c, c + 2) for c in range(count - 2)])  2.29 us
    pallas_call x1, Pallas kernels, first_message(): pl.pallas_call(functools.partial(first_kernel, heads, chunks), in_specs=[...  1.69 us
  transfers between devices with their start and end apart: 8, of which 4 were waited for; matrix products, arithmetic and copies ran while one was open for 0% of the time, Pallas kernels for 37%

profile of v9, /device:TPU:0, one launch (start us, length us, event | category | flops | bytes accessed | tf_op | source)
XLA Modules:
  0.0 32.0 jit_solution(11604509994303372231)
XLA Ops:
  0.6 1.7 %first_message.1 = (f32[520,128]{1,0:T(8,128)S(1)}, f32[16,512]{1,0:T(8,128)S(1)}, f32[16,512]{1,0:T(8,128)S(1)}, s32[1,512]{1,0:T(1,128)S(1)}, bf16[512,512]{1,...) custom-call(s32[1]{0:T(128)} %bitcast.order_ref.refs_0_, ...), custom_call_target="tpu_custom_call" | custom-call | flops 1 | bytes 1 | tf_op jit(solution)/shard_map/first_message/pallas_call | solution.py:100
  2.3 3.0 %collective-permute-start.3 = (f32[520,128]{1,0:T(8,128)S(1)}, f32[520,128]{1,0:T(8,128)S(1)}, u32[]{:S(2)}, u32[]{:S(2)}) collective-permute-start(f32[520,128]{1,0:T(8,128)S(1)} %get-tuple-element.59.refs_1_.rest_7_), channel_id=1, source_target_pairs={{0,2},{2,0},{4,6},{6,4},{8,10},{10,8},{12,14},{14,12},{1,3},{3,1},... | collective-permute-start | bytes 798728 | tf_op jit(solution)/shard_map/ppermute | solution.py:433
  5.3 0.4 %second_message.1.even_ref.rest_0_ = f32[520,128]{1,0:T(8,128)S(1)} custom-call(s32[1,512]{1,0:T(1,128)S(1)} %get-tuple-element.43.seg_ref, f32[16,512]{1,0:T(8,128)S(1)} %get-tuple-element.44.a_ref, f32[16,512]{1,0:T(8,128)S(1)} %get-tuple-element.45.w_ref, bf16[512,512]{1,0:T(8,128)(2,1)S(1)} %get-tuple-element.57.k_ref, ...), custom_call_target="tpu_custom_call" | custom-call | flops 1 | bytes 1 | tf_op jit(solution)/shard_map/second_message/pallas_call | solution.py:127
  5.7 0.0 copy-start
  5.7 1.6 %collective-permute-start.2 = (f32[520,128]{1,0:T(8,128)S(1)}, f32[520,128]{1,0:T(8,128)S(1)}, u32[]{:S(2)}, u32[]{:S(2)}) collective-permute-start(f32[520,128]{1,0:T(8,128)S(1)} %second_message.1.even_ref.rest_0_), channel_id=1, source_target_pairs={{0,4},{2,6},{4,8},{6,10},{8,12},{10,14},{12,0},{14,2},{1,5},{3,7},... | collective-permute-start | bytes 798728 | tf_op jit(solution)/shard_map/ppermute | solution.py:434
  7.3 3.0 %rest_messages.1 = (f32[520,128]{1,0:T(8,128)S(1)}, f32[520,128]{1,0:T(8,128)S(1)}, f32[512,512]{1,0:T(8,128)S(1)}, bf16[512,512]{1,0:T(8,128)(2,1)S(1)}, bf16[5...) custom-call(s32[1,512]{1,0:T(1,128)S(1)} %get-tuple-element.43.seg_r, ...), custom_call_target="tpu_custom_call" | custom-call | flops 1 | bytes 1 | tf_op jit(solution)/shard_map/rest_messages/pallas_call | solution.py:174
  10.3 0.6 %collective-permute-start.1 = (f32[520,128]{1,0:T(8,128)S(1)}, f32[520,128]{1,0:T(8,128)S(1)}, u32[]{:S(2)}, u32[]{:S(2)}) collective-permute-start(f32[520,128]{1,0:T(8,128)S(1)} %get-tuple-element.47.refs_1_.rest_7_), channel_id=1, source_target_pairs={{0,2},{2,0},{4,6},{6,4},{8,10},{10,8},{12,14},{14,12},{1,3},{3,1},... | collective-permute-start | bytes 798728 | tf_op jit(solution)/shard_map/ppermute | solution.py:433
  10.9 1.6 %collective-permute-start = (f32[520,128]{1,0:T(8,128)S(1)}, f32[520,128]{1,0:T(8,128)S(1)}, u32[]{:S(2)}, u32[]{:S(2)}) collective-permute-start(f32[520,128]{1,0:T(8,128)S(1)} %get-tuple-element.46.even_ref.rest_0_), channel_id=1, source_target_pairs={{0,4},{2,6},{4,8},{6,10},{8,12},{10,14},{12,0},{14,2},{1,5},{3,7},... | collective-permute-start | bytes 798728 | tf_op jit(solution)/shard_map/ppermute | solution.py:434
  12.5 1.5 %intra_span.4 = (f32[512,512]{1,0:T(8,128)S(1)}, f32[512,512]{1,0:T(8,128)S(1)}, f32[512,512]{1,0:T(8,128)S(1)}) custom-call(f32[512,512]{1,0:T(8,128)S(1)} %get-tuple-element.48.mask_ref, f32[16,512]{1,0:T(8,128)S(1)} %get-tuple-element.44.a_ref, f32[1,2048]{1,0:T(1,128)S(1)} %bitcast.4, bf16[512,512]{1,0:T(8,128)(2,1)S(1)} %get-tuple-element.60.q_ref.rest_6_, ...), custom_call_target="tpu_custom_call" | custom-call | flops 1 | bytes 1 | tf_op jit(solution)/shard_map/intra_span/pallas_call | solution.py:303
  14.1 0.1 join_windows.2.refs_0_
  14.1 2.5 %collective-permute-done.2.odd_ref.rest_2_ = f32[520,128]{1,0:T(8,128)S(1)} collective-permute-done((f32[520,128]{1,0:T(8,128)S(1)}, f32[520,128]{1,0:T(8,128)S(1)}, u32[]{:S(2)}, u32[]{:S(2)}) %collective-permute-start.2) | collective-permute-done | bytes 266272 | tf_op jit(solution)/shard_map/ppermute | solution.py:434
  16.6 0.1 collective-permute-start.6
  16.7 0.6 %collective-permute-start.7 = (f32[520,128]{1,0:T(8,128)S(1)}, f32[520,128]{1,0:T(8,128)S(1)}, u32[]{:S(2)}, u32[]{:S(2)}) collective-permute-start(f32[520,128]{1,0:T(8,128)S(1)} %get-tuple-element.79), channel_id=1, source_target_pairs={{0,4},{2,6},{4,8},{6,10},{8,12},{10,14},{12,0},{14,2},{1,5},{3,7},... | collective-permute-start | bytes 798728 | tf_op jit(solution)/shard_map/ppermute | solution.py:434
  17.3 1.6 %intra_span.5 = (f32[512,512]{1,0:T(8,128)S(1)}, f32[512,512]{1,0:T(8,128)S(1)}, f32[512,512]{1,0:T(8,128)S(1)}) custom-call(f32[512,512]{1,0:T(8,128)S(1)} %get-tuple-element.48.mask_ref, f32[16,512]{1,0:T(8,128)S(1)} %get-tuple-element.44.a_ref, f32[1,2048]{1,0:T(1,128)S(1)} %bitcast.5, bf16[512,512]{1,0:T(8,128)(2,1)S(1)} %get-tuple-element.53.q_ref.rest_13_, ...), custom_call_target="tpu_custom_call" | custom-call | flops 1 | bytes 1 | tf_op jit(solution)/shard_map/intra_span/pallas_call | solution.py:303
  18.9 1.6 %intra_span.6 = (f32[512,512]{1,0:T(8,128)S(1)}, f32[512,512]{1,0:T(8,128)S(1)}, f32[512,512]{1,0:T(8,128)S(1)}) custom-call(f32[512,512]{1,0:T(8,128)S(1)} %get-tuple-element.48.mask_ref, f32[16,512]{1,0:T(8,128)S(1)} %get-tuple-element.44.a_ref, f32[1,2048]{1,0:T(1,128)S(1)} %bitcast.6, bf16[512,512]{1,0:T(8,128)(2,1)S(1)} %get-tuple-element.49.q_ref.rest_6_, ...), custom_call_target="tpu_custom_call" | custom-call | flops 1 | bytes 1 | tf_op jit(solution)/shard_map/intra_span/pallas_call | solution.py:303
  20.4 0.1 join_windows.3.refs_0_
  20.5 1.8 %collective-permute-done.odd_ref.rest_2_ = f32[520,128]{1,0:T(8,128)S(1)} collective-permute-done((f32[520,128]{1,0:T(8,128)S(1)}, f32[520,128]{1,0:T(8,128)S(1)}, u32[]{:S(2)}, u32[]{:S(2)}) %collective-permute-start) | collective-permute-done | bytes 266272 | tf_op jit(solution)/shard_map/ppermute | solution.py:434
  22.3 0.7 %collective-permute-start.4 = (f32[520,128]{1,0:T(8,128)S(1)}, f32[520,128]{1,0:T(8,128)S(1)}, u32[]{:S(2)}, u32[]{:S(2)}) collective-permute-start(f32[520,128]{1,0:T(8,128)S(1)} %get-tuple-element.66.refs_0_), channel_id=1, source_target_pairs={{0,2},{2,0},{4,6},{6,4},{8,10},{10,8},{12,14},{14,12},{1,3},{3,1},... | collective-permute-start | bytes 798728 | tf_op jit(solution)/shard_map/ppermute | solution.py:433
  23.1 2.3 %collective-permute-start.5 = (f32[520,128]{1,0:T(8,128)S(1)}, f32[520,128]{1,0:T(8,128)S(1)}, u32[]{:S(2)}, u32[]{:S(2)}) collective-permute-start(f32[520,128]{1,0:T(8,128)S(1)} %get-tuple-element.69), channel_id=1, source_target_pairs={{0,4},{2,6},{4,8},{6,10},{8,12},{10,14},{1,5},{3,7},{5,9},{7,11},{... | collective-permute-start | bytes 798728 | tf_op jit(solution)/shard_map/ppermute | solution.py:435
  25.3 1.5 %intra_span.7 = (f32[512,512]{1,0:T(8,128)S(1)}, f32[512,512]{1,0:T(8,128)S(1)}, f32[512,512]{1,0:T(8,128)S(1)}) custom-call(f32[512,512]{1,0:T(8,128)S(1)} %get-tuple-element.48.mask_ref, f32[16,512]{1,0:T(8,128)S(1)} %get-tuple-element.44.a_ref, f32[1,2048]{1,0:T(1,128)S(1)} %bitcast.7, bf16[512,512]{1,0:T(8,128)(2,1)S(1)} %get-tuple-element.70.q_ref.rest_13_, ...), custom_call_target="tpu_custom_call" | custom-call | flops 1 | bytes 1 | tf_op jit(solution)/shard_map/intra_span/pallas_call | solution.py:303
  26.9 2.1 %finish.2 = (bf16[512,2048]{1,0:T(8,128)(2,1)}, f32[1,16,128,128]{3,2,1,0:T(8,128)}) custom-call(s32[1]{0:T(128)} %bitcast.order_ref.refs_0_, s32[1,512]{1,0:T(1,128)S(1)} %get-tuple-element.43.seg_ref, f32[520,128]{1,0:T(8,128)S(1)} %second_message.1.even_ref.rest_0_, f32[520,128]{1,0:T(8,128)S(1)} %collective-permute-done.6.rest_1_, ...), custom_call_target="tpu_custom_call" | custom-call | flops 1 | bytes 1 | tf_op jit(solution)/shard_map/finish/pallas_call | solution.py:403
  29.1 0.3 collective-permute-done.4.rest_1_
  29.4 0.5 %collective-permute-done.5.rest_9_ = f32[520,128]{1,0:T(8,128)S(1)} collective-permute-done((f32[520,128]{1,0:T(8,128)S(1)}, f32[520,128]{1,0:T(8,128)S(1)}, u32[]{:S(2)}, u32[]{:S(2)}) %collective-permute-start.5) | collective-permute-done | bytes 266272 | tf_op jit(solution)/shard_map/ppermute | solution.py:435
  29.8 2.1 %finish.3 = (bf16[512,2048]{1,0:T(8,128)(2,1)}, f32[1,16,128,128]{3,2,1,0:T(8,128)}) custom-call(s32[1]{0:T(128)} %bitcast.order_ref.refs_0_, s32[1,512]{1,0:T(1,128)S(1)} %get-tuple-element.43.seg_ref, f32[520,128]{1,0:T(8,128)S(1)} %get-tuple-element.46.even_ref.rest_0_, ...), custom_call_target="tpu_custom_call", output_to_operand_aliasing={{0}: (16, {}), {1}: (17, {})} | custom-call | flops 1 | bytes 1 | tf_op jit(solution)/shard_map/finish/pallas_call | solution.py:403
  (7 shorter events, 0.1 us)
Async XLA Ops:
  2.3 11.7 %collective-permute-start.3 = (f32[520,128]{1,0:T(8,128)S(1)}, f32[520,128]{1,0:T(8,128)S(1)}, u32[]{:S(2)}, u32[]{:S(2)}) collective-permute-start(f32[520,128]{1,0:T(8,128)S(1)} %get-tuple-element.59.refs_1_.rest_7_), channel_id=1, source_target_pairs={{0,2},{2,0},{4,6},{6,4},{8,10},{10,8},{12,14},{14,12},{1,3},{3,1},... | collective-permute-start | bytes 798728 | tf_op jit(solution)/shard_map/ppermute | solution.py:433
  5.7 6.8 %copy-start = (f32[2048]{0:T(1024)S(1)}, f32[2048]{0:T(1024)}, u32[]{:S(2)}) copy-start(f32[2048]{0:T(1024)} %param.15) | copy-start | bytes 24580
  5.7 10.9 %collective-permute-start.2 = (f32[520,128]{1,0:T(8,128)S(1)}, f32[520,128]{1,0:T(8,128)S(1)}, u32[]{:S(2)}, u32[]{:S(2)}) collective-permute-start(f32[520,128]{1,0:T(8,128)S(1)} %second_message.1.even_ref.rest_0_), channel_id=1, source_target_pairs={{0,4},{2,6},{4,8},{6,10},{8,12},{10,14},{12,0},{14,2},{1,5},{3,7},... | collective-permute-start | bytes 798728 | tf_op jit(solution)/shard_map/ppermute | solution.py:434
  10.3 10.1 %collective-permute-start.1 = (f32[520,128]{1,0:T(8,128)S(1)}, f32[520,128]{1,0:T(8,128)S(1)}, u32[]{:S(2)}, u32[]{:S(2)}) collective-permute-start(f32[520,128]{1,0:T(8,128)S(1)} %get-tuple-element.47.refs_1_.rest_7_), channel_id=1, source_target_pairs={{0,2},{2,0},{4,6},{6,4},{8,10},{10,8},{12,14},{14,12},{1,3},{3,1},... | collective-permute-start | bytes 798728 | tf_op jit(solution)/shard_map/ppermute | solution.py:433
  10.9 11.4 %collective-permute-start = (f32[520,128]{1,0:T(8,128)S(1)}, f32[520,128]{1,0:T(8,128)S(1)}, u32[]{:S(2)}, u32[]{:S(2)}) collective-permute-start(f32[520,128]{1,0:T(8,128)S(1)} %get-tuple-element.46.even_ref.rest_0_), channel_id=1, source_target_pairs={{0,4},{2,6},{4,8},{6,10},{8,12},{10,14},{12,0},{14,2},{1,5},{3,7},... | collective-permute-start | bytes 798728 | tf_op jit(solution)/shard_map/ppermute | solution.py:434
  16.6 10.3 %collective-permute-start.6 = (f32[520,128]{1,0:T(8,128)S(1)}, f32[520,128]{1,0:T(8,128)S(1)}, u32[]{:S(2)}, u32[]{:S(2)}) collective-permute-start(f32[520,128]{1,0:T(8,128)S(1)} %get-tuple-element.63.refs_0_), channel_id=1, source_target_pairs={{0,2},{2,0},{4,6},{6,4},{8,10},{10,8},{12,14},{14,12},{1,3},{3,1},... | collective-permute-start | bytes 798728 | tf_op jit(solution)/shard_map/ppermute | solution.py:433
  16.7 10.2 %collective-permute-start.7 = (f32[520,128]{1,0:T(8,128)S(1)}, f32[520,128]{1,0:T(8,128)S(1)}, u32[]{:S(2)}, u32[]{:S(2)}) collective-permute-start(f32[520,128]{1,0:T(8,128)S(1)} %get-tuple-element.79), channel_id=1, source_target_pairs={{0,4},{2,6},{4,8},{6,10},{8,12},{10,14},{12,0},{14,2},{1,5},{3,7},... | collective-permute-start | bytes 798728 | tf_op jit(solution)/shard_map/ppermute | solution.py:434
  22.3 7.0 %collective-permute-start.4 = (f32[520,128]{1,0:T(8,128)S(1)}, f32[520,128]{1,0:T(8,128)S(1)}, u32[]{:S(2)}, u32[]{:S(2)}) collective-permute-start(f32[520,128]{1,0:T(8,128)S(1)} %get-tuple-element.66.refs_0_), channel_id=1, source_target_pairs={{0,2},{2,0},{4,6},{6,4},{8,10},{10,8},{12,14},{14,12},{1,3},{3,1},... | collective-permute-start | bytes 798728 | tf_op jit(solution)/shard_map/ppermute | solution.py:433
  23.1 6.8 %collective-permute-start.5 = (f32[520,128]{1,0:T(8,128)S(1)}, f32[520,128]{1,0:T(8,128)S(1)}, u32[]{:S(2)}, u32[]{:S(2)}) collective-permute-start(f32[520,128]{1,0:T(8,128)S(1)} %get-tuple-element.69), channel_id=1, source_target_pairs={{0,4},{2,6},{4,8},{6,10},{8,12},{10,14},{1,5},{3,7},{5,9},{7,11},{... | collective-permute-start | bytes 798728 | tf_op jit(solution)/shard_map/ppermute | solution.py:435

commit v10 on v9

--- a/solution.py
+++ b/solution.py
@@ -323,7 +323,7 @@
 
     def send(source, target):
         copies.append(pltpu.make_async_copy(source, target, sems.at[len(copies)]))
-        copies[-1].start()
+        copies[-1].start(priority=len(copies) % 2)
 
     for i, (first, heads, kind) in enumerate(groups):
         own_ref, near_ref, past_ref = inputs[7 * i : 7 * i + 3]

time: 32.1 us -> 32.2 us (level)
  no operation moved by 1% of the time
where the time goes in v10:
time: 32.2 us; the launch traced here: 32 us
  Pallas kernels  15.7 us (49%)
  starting transfers between devices  10.5 us (33%)
  waiting for transfers between devices  4.98 us (15%)
  between operations  0.77 us (2%)
    pallas_call x4, Pallas kernels, intra(): pl.pallas_call(functools.partial(intra_kernel, first, heads, len(through)...  6.2 us
    ppermute x4, starting transfers between devices, shards(): swap = lambda x: lax.ppermute(x, 'seq', [(c, c ^ 1) for c in range(count)])  4.39 us
    pallas_call x2, Pallas kernels, finish(): pl.pallas_call(functools.partial(final_kernel, groups, unread), in_specs=...  4.33 us
    ppermute x3, waiting for transfers between devices, shards(): lax.ppermute(x, 'seq', [(c, (c + 2) % count) for c in range(count)])  4.25 us
    ppermute x3, starting transfers between devices, shards(): lax.ppermute(x, 'seq', [(c, (c + 2) % count) for c in range(count)])  3.81 us
    pallas_call x1, Pallas kernels, rest_messages(): pl.pallas_call(functools.partial(rest_kernel, chunks, done), in_specs=[pl...  2.97 us
    ppermute x1, starting transfers between devices, shards(): lax.ppermute(x, 'seq', [(c, c + 2) for c in range(count - 2)])  2.29 us
    pallas_call x1, Pallas kernels, first_message(): pl.pallas_call(functools.partial(first_kernel, heads, chunks), in_specs=[...  1.69 us
  transfers between devices with their start and end apart: 8, of which 4 were waited for; matrix products, arithmetic and copies ran while one was open for 0% of the time, Pallas kernels for 37%

profile of v10, /device:TPU:0, one launch (start us, length us, event | category | flops | bytes accessed | tf_op | source)
XLA Modules:
  0.0 32.0 jit_solution(10235137438881658566)
XLA Ops:
  0.6 1.7 %first_message.1 = (f32[520,128]{1,0:T(8,128)S(1)}, f32[16,512]{1,0:T(8,128)S(1)}, f32[16,512]{1,0:T(8,128)S(1)}, s32[1,512]{1,0:T(1,128)S(1)}, bf16[512,512]{1,...) custom-call(s32[1]{0:T(128)} %bitcast.order_ref.refs_0_, ...), custom_call_target="tpu_custom_call" | custom-call | flops 1 | bytes 1 | tf_op jit(solution)/shard_map/first_message/pallas_call | solution.py:100
  2.3 3.0 %collective-permute-start.3 = (f32[520,128]{1,0:T(8,128)S(1)}, f32[520,128]{1,0:T(8,128)S(1)}, u32[]{:S(2)}, u32[]{:S(2)}) collective-permute-start(f32[520,128]{1,0:T(8,128)S(1)} %get-tuple-element.59.refs_1_.rest_7_), channel_id=1, source_target_pairs={{0,2},{2,0},{4,6},{6,4},{8,10},{10,8},{12,14},{14,12},{1,3},{3,1},... | collective-permute-start | bytes 798728 | tf_op jit(solution)/shard_map/ppermute | solution.py:433
  5.3 0.4 %second_message.1.even_ref.rest_0_ = f32[520,128]{1,0:T(8,128)S(1)} custom-call(s32[1,512]{1,0:T(1,128)S(1)} %get-tuple-element.43.seg_ref, f32[16,512]{1,0:T(8,128)S(1)} %get-tuple-element.44.a_ref, f32[16,512]{1,0:T(8,128)S(1)} %get-tuple-element.45.w_ref, bf16[512,512]{1,0:T(8,128)(2,1)S(1)} %get-tuple-element.57.k_ref, ...), custom_call_target="tpu_custom_call" | custom-call | flops 1 | bytes 1 | tf_op jit(solution)/shard_map/second_message/pallas_call | solution.py:127
  5.7 0.0 copy-start
  5.7 1.6 %collective-permute-start.2 = (f32[520,128]{1,0:T(8,128)S(1)}, f32[520,128]{1,0:T(8,128)S(1)}, u32[]{:S(2)}, u32[]{:S(2)}) collective-permute-start(f32[520,128]{1,0:T(8,128)S(1)} %second_message.1.even_ref.rest_0_), channel_id=1, source_target_pairs={{0,4},{2,6},{4,8},{6,10},{8,12},{10,14},{12,0},{14,2},{1,5},{3,7},... | collective-permute-start | bytes 798728 | tf_op jit(solution)/shard_map/ppermute | solution.py:434
  7.3 3.0 %rest_messages.1 = (f32[520,128]{1,0:T(8,128)S(1)}, f32[520,128]{1,0:T(8,128)S(1)}, f32[512,512]{1,0:T(8,128)S(1)}, bf16[512,512]{1,0:T(8,128)(2,1)S(1)}, bf16[5...) custom-call(s32[1,512]{1,0:T(1,128)S(1)} %get-tuple-element.43.seg_r, ...), custom_call_target="tpu_custom_call" | custom-call | flops 1 | bytes 1 | tf_op jit(solution)/shard_map/rest_messages/pallas_call | solution.py:174
  10.3 0.6 %collective-permute-start.1 = (f32[520,128]{1,0:T(8,128)S(1)}, f32[520,128]{1,0:T(8,128)S(1)}, u32[]{:S(2)}, u32[]{:S(2)}) collective-permute-start(f32[520,128]{1,0:T(8,128)S(1)} %get-tuple-element.47.refs_1_.rest_7_), channel_id=1, source_target_pairs={{0,2},{2,0},{4,6},{6,4},{8,10},{10,8},{12,14},{14,12},{1,3},{3,1},... | collective-permute-start | bytes 798728 | tf_op jit(solution)/shard_map/ppermute | solution.py:433
  10.9 1.6 %collective-permute-start = (f32[520,128]{1,0:T(8,128)S(1)}, f32[520,128]{1,0:T(8,128)S(1)}, u32[]{:S(2)}, u32[]{:S(2)}) collective-permute-start(f32[520,128]{1,0:T(8,128)S(1)} %get-tuple-element.46.even_ref.rest_0_), channel_id=1, source_target_pairs={{0,4},{2,6},{4,8},{6,10},{8,12},{10,14},{12,0},{14,2},{1,5},{3,7},... | collective-permute-start | bytes 798728 | tf_op jit(solution)/shard_map/ppermute | solution.py:434
  12.5 1.5 %intra_span.4 = (f32[512,512]{1,0:T(8,128)S(1)}, f32[512,512]{1,0:T(8,128)S(1)}, f32[512,512]{1,0:T(8,128)S(1)}) custom-call(f32[512,512]{1,0:T(8,128)S(1)} %get-tuple-element.48.mask_ref, f32[16,512]{1,0:T(8,128)S(1)} %get-tuple-element.44.a_ref, f32[1,2048]{1,0:T(1,128)S(1)} %bitcast.4, bf16[512,512]{1,0:T(8,128)(2,1)S(1)} %get-tuple-element.60.q_ref.rest_6_, ...), custom_call_target="tpu_custom_call" | custom-call | flops 1 | bytes 1 | tf_op jit(solution)/shard_map/intra_span/pallas_call | solution.py:303
  14.1 0.1 join_windows.2.refs_0_
  14.1 2.5 %collective-permute-done.2.odd_ref.rest_2_ = f32[520,128]{1,0:T(8,128)S(1)} collective-permute-done((f32[520,128]{1,0:T(8,128)S(1)}, f32[520,128]{1,0:T(8,128)S(1)}, u32[]{:S(2)}, u32[]{:S(2)}) %collective-permute-start.2) | collective-permute-done | bytes 266272 | tf_op jit(solution)/shard_map/ppermute | solution.py:434
  16.6 0.1 collective-permute-start.6
  16.7 0.6 %collective-permute-start.7 = (f32[520,128]{1,0:T(8,128)S(1)}, f32[520,128]{1,0:T(8,128)S(1)}, u32[]{:S(2)}, u32[]{:S(2)}) collective-permute-start(f32[520,128]{1,0:T(8,128)S(1)} %get-tuple-element.79), channel_id=1, source_target_pairs={{0,4},{2,6},{4,8},{6,10},{8,12},{10,14},{12,0},{14,2},{1,5},{3,7},... | collective-permute-start | bytes 798728 | tf_op jit(solution)/shard_map/ppermute | solution.py:434
  17.3 1.6 %intra_span.5 = (f32[512,512]{1,0:T(8,128)S(1)}, f32[512,512]{1,0:T(8,128)S(1)}, f32[512,512]{1,0:T(8,128)S(1)}) custom-call(f32[512,512]{1,0:T(8,128)S(1)} %get-tuple-element.48.mask_ref, f32[16,512]{1,0:T(8,128)S(1)} %get-tuple-element.44.a_ref, f32[1,2048]{1,0:T(1,128)S(1)} %bitcast.5, bf16[512,512]{1,0:T(8,128)(2,1)S(1)} %get-tuple-element.53.q_ref.rest_13_, ...), custom_call_target="tpu_custom_call" | custom-call | flops 1 | bytes 1 | tf_op jit(solution)/shard_map/intra_span/pallas_call | solution.py:303
  18.9 1.6 %intra_span.6 = (f32[512,512]{1,0:T(8,128)S(1)}, f32[512,512]{1,0:T(8,128)S(1)}, f32[512,512]{1,0:T(8,128)S(1)}) custom-call(f32[512,512]{1,0:T(8,128)S(1)} %get-tuple-element.48.mask_ref, f32[16,512]{1,0:T(8,128)S(1)} %get-tuple-element.44.a_ref, f32[1,2048]{1,0:T(1,128)S(1)} %bitcast.6, bf16[512,512]{1,0:T(8,128)(2,1)S(1)} %get-tuple-element.49.q_ref.rest_6_, ...), custom_call_target="tpu_custom_call" | custom-call | flops 1 | bytes 1 | tf_op jit(solution)/shard_map/intra_span/pallas_call | solution.py:303
  20.4 0.1 join_windows.3.refs_0_
  20.5 1.8 %collective-permute-done.odd_ref.rest_2_ = f32[520,128]{1,0:T(8,128)S(1)} collective-permute-done((f32[520,128]{1,0:T(8,128)S(1)}, f32[520,128]{1,0:T(8,128)S(1)}, u32[]{:S(2)}, u32[]{:S(2)}) %collective-permute-start) | collective-permute-done | bytes 266272 | tf_op jit(solution)/shard_map/ppermute | solution.py:434
  22.3 0.7 %collective-permute-start.4 = (f32[520,128]{1,0:T(8,128)S(1)}, f32[520,128]{1,0:T(8,128)S(1)}, u32[]{:S(2)}, u32[]{:S(2)}) collective-permute-start(f32[520,128]{1,0:T(8,128)S(1)} %get-tuple-element.66.refs_0_), channel_id=1, source_target_pairs={{0,2},{2,0},{4,6},{6,4},{8,10},{10,8},{12,14},{14,12},{1,3},{3,1},... | collective-permute-start | bytes 798728 | tf_op jit(solution)/shard_map/ppermute | solution.py:433
  23.1 2.3 %collective-permute-start.5 = (f32[520,128]{1,0:T(8,128)S(1)}, f32[520,128]{1,0:T(8,128)S(1)}, u32[]{:S(2)}, u32[]{:S(2)}) collective-permute-start(f32[520,128]{1,0:T(8,128)S(1)} %get-tuple-element.69), channel_id=1, source_target_pairs={{0,4},{2,6},{4,8},{6,10},{8,12},{10,14},{1,5},{3,7},{5,9},{7,11},{... | collective-permute-start | bytes 798728 | tf_op jit(solution)/shard_map/ppermute | solution.py:435
  25.3 1.5 %intra_span.7 = (f32[512,512]{1,0:T(8,128)S(1)}, f32[512,512]{1,0:T(8,128)S(1)}, f32[512,512]{1,0:T(8,128)S(1)}) custom-call(f32[512,512]{1,0:T(8,128)S(1)} %get-tuple-element.48.mask_ref, f32[16,512]{1,0:T(8,128)S(1)} %get-tuple-element.44.a_ref, f32[1,2048]{1,0:T(1,128)S(1)} %bitcast.7, bf16[512,512]{1,0:T(8,128)(2,1)S(1)} %get-tuple-element.70.q_ref.rest_13_, ...), custom_call_target="tpu_custom_call" | custom-call | flops 1 | bytes 1 | tf_op jit(solution)/shard_map/intra_span/pallas_call | solution.py:303
  26.9 2.2 %finish.2 = (bf16[512,2048]{1,0:T(8,128)(2,1)}, f32[1,16,128,128]{3,2,1,0:T(8,128)}) custom-call(s32[1]{0:T(128)} %bitcast.order_ref.refs_0_, s32[1,512]{1,0:T(1,128)S(1)} %get-tuple-element.43.seg_ref, f32[520,128]{1,0:T(8,128)S(1)} %second_message.1.even_ref.rest_0_, f32[520,128]{1,0:T(8,128)S(1)} %collective-permute-done.6.rest_1_, ...), custom_call_target="tpu_custom_call" | custom-call | flops 1 | bytes 1 | tf_op jit(solution)/shard_map/finish/pallas_call | solution.py:403
  29.1 0.3 collective-permute-done.4.rest_1_
  29.4 0.5 %collective-permute-done.5.rest_9_ = f32[520,128]{1,0:T(8,128)S(1)} collective-permute-done((f32[520,128]{1,0:T(8,128)S(1)}, f32[520,128]{1,0:T(8,128)S(1)}, u32[]{:S(2)}, u32[]{:S(2)}) %collective-permute-start.5) | collective-permute-done | bytes 266272 | tf_op jit(solution)/shard_map/ppermute | solution.py:435
  29.8 2.2 %finish.3 = (bf16[512,2048]{1,0:T(8,128)(2,1)}, f32[1,16,128,128]{3,2,1,0:T(8,128)}) custom-call(s32[1]{0:T(128)} %bitcast.order_ref.refs_0_, s32[1,512]{1,0:T(1,128)S(1)} %get-tuple-element.43.seg_ref, f32[520,128]{1,0:T(8,128)S(1)} %get-tuple-element.46.even_ref.rest_0_, ...), custom_call_target="tpu_custom_call", output_to_operand_aliasing={{0}: (16, {}), {1}: (17, {})} | custom-call | flops 1 | bytes 1 | tf_op jit(solution)/shard_map/finish/pallas_call | solution.py:403
  (7 shorter events, 0.1 us)
Async XLA Ops:
  2.3 11.7 %collective-permute-start.3 = (f32[520,128]{1,0:T(8,128)S(1)}, f32[520,128]{1,0:T(8,128)S(1)}, u32[]{:S(2)}, u32[]{:S(2)}) collective-permute-start(f32[520,128]{1,0:T(8,128)S(1)} %get-tuple-element.59.refs_1_.rest_7_), channel_id=1, source_target_pairs={{0,2},{2,0},{4,6},{6,4},{8,10},{10,8},{12,14},{14,12},{1,3},{3,1},... | collective-permute-start | bytes 798728 | tf_op jit(solution)/shard_map/ppermute | solution.py:433
  5.7 6.8 %copy-start = (f32[2048]{0:T(1024)S(1)}, f32[2048]{0:T(1024)}, u32[]{:S(2)}) copy-start(f32[2048]{0:T(1024)} %param.15) | copy-start | bytes 24580
  5.7 10.9 %collective-permute-start.2 = (f32[520,128]{1,0:T(8,128)S(1)}, f32[520,128]{1,0:T(8,128)S(1)}, u32[]{:S(2)}, u32[]{:S(2)}) collective-permute-start(f32[520,128]{1,0:T(8,128)S(1)} %second_message.1.even_ref.rest_0_), channel_id=1, source_target_pairs={{0,4},{2,6},{4,8},{6,10},{8,12},{10,14},{12,0},{14,2},{1,5},{3,7},... | collective-permute-start | bytes 798728 | tf_op jit(solution)/shard_map/ppermute | solution.py:434
  10.3 10.1 %collective-permute-start.1 = (f32[520,128]{1,0:T(8,128)S(1)}, f32[520,128]{1,0:T(8,128)S(1)}, u32[]{:S(2)}, u32[]{:S(2)}) collective-permute-start(f32[520,128]{1,0:T(8,128)S(1)} %get-tuple-element.47.refs_1_.rest_7_), channel_id=1, source_target_pairs={{0,2},{2,0},{4,6},{6,4},{8,10},{10,8},{12,14},{14,12},{1,3},{3,1},... | collective-permute-start | bytes 798728 | tf_op jit(solution)/shard_map/ppermute | solution.py:433
  10.9 11.4 %collective-permute-start = (f32[520,128]{1,0:T(8,128)S(1)}, f32[520,128]{1,0:T(8,128)S(1)}, u32[]{:S(2)}, u32[]{:S(2)}) collective-permute-start(f32[520,128]{1,0:T(8,128)S(1)} %get-tuple-element.46.even_ref.rest_0_), channel_id=1, source_target_pairs={{0,4},{2,6},{4,8},{6,10},{8,12},{10,14},{12,0},{14,2},{1,5},{3,7},... | collective-permute-start | bytes 798728 | tf_op jit(solution)/shard_map/ppermute | solution.py:434
  16.6 10.3 %collective-permute-start.6 = (f32[520,128]{1,0:T(8,128)S(1)}, f32[520,128]{1,0:T(8,128)S(1)}, u32[]{:S(2)}, u32[]{:S(2)}) collective-permute-start(f32[520,128]{1,0:T(8,128)S(1)} %get-tuple-element.63.refs_0_), channel_id=1, source_target_pairs={{0,2},{2,0},{4,6},{6,4},{8,10},{10,8},{12,14},{14,12},{1,3},{3,1},... | collective-permute-start | bytes 798728 | tf_op jit(solution)/shard_map/ppermute | solution.py:433
  16.7 10.2 %collective-permute-start.7 = (f32[520,128]{1,0:T(8,128)S(1)}, f32[520,128]{1,0:T(8,128)S(1)}, u32[]{:S(2)}, u32[]{:S(2)}) collective-permute-start(f32[520,128]{1,0:T(8,128)S(1)} %get-tuple-element.79), channel_id=1, source_target_pairs={{0,4},{2,6},{4,8},{6,10},{8,12},{10,14},{12,0},{14,2},{1,5},{3,7},... | collective-permute-start | bytes 798728 | tf_op jit(solution)/shard_map/ppermute | solution.py:434
  22.3 7.0 %collective-permute-start.4 = (f32[520,128]{1,0:T(8,128)S(1)}, f32[520,128]{1,0:T(8,128)S(1)}, u32[]{:S(2)}, u32[]{:S(2)}) collective-permute-start(f32[520,128]{1,0:T(8,128)S(1)} %get-tuple-element.66.refs_0_), channel_id=1, source_target_pairs={{0,2},{2,0},{4,6},{6,4},{8,10},{10,8},{12,14},{14,12},{1,3},{3,1},... | collective-permute-start | bytes 798728 | tf_op jit(solution)/shard_map/ppermute | solution.py:433
  23.1 6.8 %collective-permute-start.5 = (f32[520,128]{1,0:T(8,128)S(1)}, f32[520,128]{1,0:T(8,128)S(1)}, u32[]{:S(2)}, u32[]{:S(2)}) collective-permute-start(f32[520,128]{1,0:T(8,128)S(1)} %get-tuple-element.69), channel_id=1, source_target_pairs={{0,4},{2,6},{4,8},{6,10},{8,12},{10,14},{1,5},{3,7},{5,9},{7,11},{... | collective-permute-start | bytes 798728 | tf_op jit(solution)/shard_map/ppermute | solution.py:435

commit v11 on v9

--- a/solution.py
+++ b/solution.py
@@ -358,7 +358,7 @@
             work.append((i, j, first, heads, both, number_valid, inputs[7 * i + 3 : 7 * i + 7]))
         send(snap_ref, snap_hbm.at[0, pl.ds(first, heads)])
 
-    rows = lax.broadcasted_iota(jnp.int32, (64, 128), 0).astype(F32)
+    rows = lax.broadcasted_iota(jnp.int32, (32, 128), 0).astype(F32)
     for number, (i, j, first, heads, both, number_valid, arrays) in enumerate(work):
         o_ref, gate_ref, decay_ref, q_ref = arrays
         gated_ref = scratch[2 * i]
@@ -368,16 +368,16 @@
         inter_ref[number % 4] = lax.dot_general(
             jnp.concatenate([q, q], axis=1), both, NN, preferred_element_type=F32
         )
-        for start in range(0, tokens, 64):
-            here = slice(start, start + 64)
+        for start in range(0, tokens, 32):
+            here = slice(start, start + 32)
             inter = inter_ref[number % 4, here, :]
             inter = jnp.where(rows < number_valid - start, inter * decay_ref[here, columns], 0.0)
             mixed = o_ref[here, columns] + inter
             square = jnp.sum(mixed * mixed, axis=1, keepdims=True)
             gated = mixed * gate_ref[here, columns] * lax.rsqrt(square + size * 1e-06)
             gated_ref[here, columns] = gated.astype(BF16)
-            if number == len(work) - 1 and start % 128 == 64:
-                block = pl.ds(start - 64, 128)
+            if number == len(work) - 1 and start % 128 == 96:
+                block = pl.ds(start - 96, 128)
                 there = pl.ds((first + j) * size, size)
                 send(gated_ref.at[block, pl.ds(j * size, size)], gated_hbm.at[block, there])
         if number == len(work) - 1:

time: 32.1 us -> 32.2 us (level)
  no operation moved by 1% of the time
where the time goes in v11:
time: 32.2 us; the launch traced here: 32 us
  Pallas kernels  15.7 us (49%)
  starting transfers between devices  10.5 us (33%)
  waiting for transfers between devices  5.01 us (16%)
  between operations  0.77 us (2%)
    pallas_call x4, Pallas kernels, intra(): pl.pallas_call(functools.partial(intra_kernel, first, heads, len(through)...  6.2 us
    ppermute x4, starting transfers between devices, shards(): swap = lambda x: lax.ppermute(x, 'seq', [(c, c ^ 1) for c in range(count)])  4.39 us
    pallas_call x2, Pallas kernels, finish(): pl.pallas_call(functools.partial(final_kernel, groups, unread), in_specs=...  4.3 us
    ppermute x3, waiting for transfers between devices, shards(): lax.ppermute(x, 'seq', [(c, (c + 2) % count) for c in range(count)])  4.25 us
    ppermute x3, starting transfers between devices, shards(): lax.ppermute(x, 'seq', [(c, (c + 2) % count) for c in range(count)])  3.81 us
    pallas_call x1, Pallas kernels, rest_messages(): pl.pallas_call(functools.partial(rest_kernel, chunks, done), in_specs=[pl...  2.97 us
    ppermute x1, starting transfers between devices, shards(): lax.ppermute(x, 'seq', [(c, c + 2) for c in range(count - 2)])  2.29 us
    pallas_call x1, Pallas kernels, first_message(): pl.pallas_call(functools.partial(first_kernel, heads, chunks), in_specs=[...  1.69 us
  transfers between devices with their start and end apart: 8, of which 4 were waited for; matrix products, arithmetic and copies ran while one was open for 0% of the time, Pallas kernels for 37%

profile of v11, /device:TPU:0, one launch (start us, length us, event | category | flops | bytes accessed | tf_op | source)
XLA Modules:
  0.0 32.0 jit_solution(97541102445804001)
XLA Ops:
  0.6 1.7 %first_message.1 = (f32[520,128]{1,0:T(8,128)S(1)}, f32[16,512]{1,0:T(8,128)S(1)}, f32[16,512]{1,0:T(8,128)S(1)}, s32[1,512]{1,0:T(1,128)S(1)}, bf16[512,512]{1,...) custom-call(s32[1]{0:T(128)} %bitcast.order_ref.refs_0_, ...), custom_call_target="tpu_custom_call" | custom-call | flops 1 | bytes 1 | tf_op jit(solution)/shard_map/first_message/pallas_call | solution.py:100
  2.3 3.0 %collective-permute-start.3 = (f32[520,128]{1,0:T(8,128)S(1)}, f32[520,128]{1,0:T(8,128)S(1)}, u32[]{:S(2)}, u32[]{:S(2)}) collective-permute-start(f32[520,128]{1,0:T(8,128)S(1)} %get-tuple-element.59.refs_1_.rest_7_), channel_id=1, source_target_pairs={{0,2},{2,0},{4,6},{6,4},{8,10},{10,8},{12,14},{14,12},{1,3},{3,1},... | collective-permute-start | bytes 798728 | tf_op jit(solution)/shard_map/ppermute | solution.py:433
  5.3 0.4 %second_message.1.even_ref.rest_0_ = f32[520,128]{1,0:T(8,128)S(1)} custom-call(s32[1,512]{1,0:T(1,128)S(1)} %get-tuple-element.43.seg_ref, f32[16,512]{1,0:T(8,128)S(1)} %get-tuple-element.44.a_ref, f32[16,512]{1,0:T(8,128)S(1)} %get-tuple-element.45.w_ref, bf16[512,512]{1,0:T(8,128)(2,1)S(1)} %get-tuple-element.57.k_ref, ...), custom_call_target="tpu_custom_call" | custom-call | flops 1 | bytes 1 | tf_op jit(solution)/shard_map/second_message/pallas_call | solution.py:127
  5.7 0.0 copy-start
  5.7 1.6 %collective-permute-start.2 = (f32[520,128]{1,0:T(8,128)S(1)}, f32[520,128]{1,0:T(8,128)S(1)}, u32[]{:S(2)}, u32[]{:S(2)}) collective-permute-start(f32[520,128]{1,0:T(8,128)S(1)} %second_message.1.even_ref.rest_0_), channel_id=1, source_target_pairs={{0,4},{2,6},{4,8},{6,10},{8,12},{10,14},{12,0},{14,2},{1,5},{3,7},... | collective-permute-start | bytes 798728 | tf_op jit(solution)/shard_map/ppermute | solution.py:434
  7.3 3.0 %rest_messages.1 = (f32[520,128]{1,0:T(8,128)S(1)}, f32[520,128]{1,0:T(8,128)S(1)}, f32[512,512]{1,0:T(8,128)S(1)}, bf16[512,512]{1,0:T(8,128)(2,1)S(1)}, bf16[5...) custom-call(s32[1,512]{1,0:T(1,128)S(1)} %get-tuple-element.43.seg_r, ...), custom_call_target="tpu_custom_call" | custom-call | flops 1 | bytes 1 | tf_op jit(solution)/shard_map/rest_messages/pallas_call | solution.py:174
  10.3 0.6 %collective-permute-start.1 = (f32[520,128]{1,0:T(8,128)S(1)}, f32[520,128]{1,0:T(8,128)S(1)}, u32[]{:S(2)}, u32[]{:S(2)}) collective-permute-start(f32[520,128]{1,0:T(8,128)S(1)} %get-tuple-element.47.refs_1_.rest_7_), channel_id=1, source_target_pairs={{0,2},{2,0},{4,6},{6,4},{8,10},{10,8},{12,14},{14,12},{1,3},{3,1},... | collective-permute-start | bytes 798728 | tf_op jit(solution)/shard_map/ppermute | solution.py:433
  10.9 1.6 %collective-permute-start = (f32[520,128]{1,0:T(8,128)S(1)}, f32[520,128]{1,0:T(8,128)S(1)}, u32[]{:S(2)}, u32[]{:S(2)}) collective-permute-start(f32[520,128]{1,0:T(8,128)S(1)} %get-tuple-element.46.even_ref.rest_0_), channel_id=1, source_target_pairs={{0,4},{2,6},{4,8},{6,10},{8,12},{10,14},{12,0},{14,2},{1,5},{3,7},... | collective-permute-start | bytes 798728 | tf_op jit(solution)/shard_map/ppermute | solution.py:434
  12.5 1.5 %intra_span.4 = (f32[512,512]{1,0:T(8,128)S(1)}, f32[512,512]{1,0:T(8,128)S(1)}, f32[512,512]{1,0:T(8,128)S(1)}) custom-call(f32[512,512]{1,0:T(8,128)S(1)} %get-tuple-element.48.mask_ref, f32[16,512]{1,0:T(8,128)S(1)} %get-tuple-element.44.a_ref, f32[1,2048]{1,0:T(1,128)S(1)} %bitcast.4, bf16[512,512]{1,0:T(8,128)(2,1)S(1)} %get-tuple-element.60.q_ref.rest_6_, ...), custom_call_target="tpu_custom_call" | custom-call | flops 1 | bytes 1 | tf_op jit(solution)/shard_map/intra_span/pallas_call | solution.py:303
  14.1 0.1 join_windows.2.refs_0_
  14.1 2.5 %collective-permute-done.2.odd_ref.rest_2_ = f32[520,128]{1,0:T(8,128)S(1)} collective-permute-done((f32[520,128]{1,0:T(8,128)S(1)}, f32[520,128]{1,0:T(8,128)S(1)}, u32[]{:S(2)}, u32[]{:S(2)}) %collective-permute-start.2) | collective-permute-done | bytes 266272 | tf_op jit(solution)/shard_map/ppermute | solution.py:434
  16.6 0.1 collective-permute-start.6
  16.7 0.6 %collective-permute-start.7 = (f32[520,128]{1,0:T(8,128)S(1)}, f32[520,128]{1,0:T(8,128)S(1)}, u32[]{:S(2)}, u32[]{:S(2)}) collective-permute-start(f32[520,128]{1,0:T(8,128)S(1)} %get-tuple-element.79), channel_id=1, source_target_pairs={{0,4},{2,6},{4,8},{6,10},{8,12},{10,14},{12,0},{14,2},{1,5},{3,7},... | collective-permute-start | bytes 798728 | tf_op jit(solution)/shard_map/ppermute | solution.py:434
  17.3 1.6 %intra_span.5 = (f32[512,512]{1,0:T(8,128)S(1)}, f32[512,512]{1,0:T(8,128)S(1)}, f32[512,512]{1,0:T(8,128)S(1)}) custom-call(f32[512,512]{1,0:T(8,128)S(1)} %get-tuple-element.48.mask_ref, f32[16,512]{1,0:T(8,128)S(1)} %get-tuple-element.44.a_ref, f32[1,2048]{1,0:T(1,128)S(1)} %bitcast.5, bf16[512,512]{1,0:T(8,128)(2,1)S(1)} %get-tuple-element.53.q_ref.rest_13_, ...), custom_call_target="tpu_custom_call" | custom-call | flops 1 | bytes 1 | tf_op jit(solution)/shard_map/intra_span/pallas_call | solution.py:303
  18.9 1.6 %intra_span.6 = (f32[512,512]{1,0:T(8,128)S(1)}, f32[512,512]{1,0:T(8,128)S(1)}, f32[512,512]{1,0:T(8,128)S(1)}) custom-call(f32[512,512]{1,0:T(8,128)S(1)} %get-tuple-element.48.mask_ref, f32[16,512]{1,0:T(8,128)S(1)} %get-tuple-element.44.a_ref, f32[1,2048]{1,0:T(1,128)S(1)} %bitcast.6, bf16[512,512]{1,0:T(8,128)(2,1)S(1)} %get-tuple-element.49.q_ref.rest_6_, ...), custom_call_target="tpu_custom_call" | custom-call | flops 1 | bytes 1 | tf_op jit(solution)/shard_map/intra_span/pallas_call | solution.py:303
  20.4 0.1 join_windows.3.refs_0_
  20.5 1.8 %collective-permute-done.odd_ref.rest_2_ = f32[520,128]{1,0:T(8,128)S(1)} collective-permute-done((f32[520,128]{1,0:T(8,128)S(1)}, f32[520,128]{1,0:T(8,128)S(1)}, u32[]{:S(2)}, u32[]{:S(2)}) %collective-permute-start) | collective-permute-done | bytes 266272 | tf_op jit(solution)/shard_map/ppermute | solution.py:434
  22.3 0.7 %collective-permute-start.4 = (f32[520,128]{1,0:T(8,128)S(1)}, f32[520,128]{1,0:T(8,128)S(1)}, u32[]{:S(2)}, u32[]{:S(2)}) collective-permute-start(f32[520,128]{1,0:T(8,128)S(1)} %get-tuple-element.66.refs_0_), channel_id=1, source_target_pairs={{0,2},{2,0},{4,6},{6,4},{8,10},{10,8},{12,14},{14,12},{1,3},{3,1},... | collective-permute-start | bytes 798728 | tf_op jit(solution)/shard_map/ppermute | solution.py:433
  23.1 2.3 %collective-permute-start.5 = (f32[520,128]{1,0:T(8,128)S(1)}, f32[520,128]{1,0:T(8,128)S(1)}, u32[]{:S(2)}, u32[]{:S(2)}) collective-permute-start(f32[520,128]{1,0:T(8,128)S(1)} %get-tuple-element.69), channel_id=1, source_target_pairs={{0,4},{2,6},{4,8},{6,10},{8,12},{10,14},{1,5},{3,7},{5,9},{7,11},{... | collective-permute-start | bytes 798728 | tf_op jit(solution)/shard_map/ppermute | solution.py:435
  25.3 1.5 %intra_span.7 = (f32[512,512]{1,0:T(8,128)S(1)}, f32[512,512]{1,0:T(8,128)S(1)}, f32[512,512]{1,0:T(8,128)S(1)}) custom-call(f32[512,512]{1,0:T(8,128)S(1)} %get-tuple-element.48.mask_ref, f32[16,512]{1,0:T(8,128)S(1)} %get-tuple-element.44.a_ref, f32[1,2048]{1,0:T(1,128)S(1)} %bitcast.7, bf16[512,512]{1,0:T(8,128)(2,1)S(1)} %get-tuple-element.70.q_ref.rest_13_, ...), custom_call_target="tpu_custom_call" | custom-call | flops 1 | bytes 1 | tf_op jit(solution)/shard_map/intra_span/pallas_call | solution.py:303
  26.9 2.1 %finish.2 = (bf16[512,2048]{1,0:T(8,128)(2,1)}, f32[1,16,128,128]{3,2,1,0:T(8,128)}) custom-call(s32[1]{0:T(128)} %bitcast.order_ref.refs_0_, s32[1,512]{1,0:T(1,128)S(1)} %get-tuple-element.43.seg_ref, f32[520,128]{1,0:T(8,128)S(1)} %second_message.1.even_ref.rest_0_, f32[520,128]{1,0:T(8,128)S(1)} %collective-permute-done.6.rest_1_, ...), custom_call_target="tpu_custom_call" | custom-call | flops 1 | bytes 1 | tf_op jit(solution)/shard_map/finish/pallas_call | solution.py:403
  29.1 0.3 collective-permute-done.4.rest_1_
  29.4 0.5 %collective-permute-done.5.rest_9_ = f32[520,128]{1,0:T(8,128)S(1)} collective-permute-done((f32[520,128]{1,0:T(8,128)S(1)}, f32[520,128]{1,0:T(8,128)S(1)}, u32[]{:S(2)}, u32[]{:S(2)}) %collective-permute-start.5) | collective-permute-done | bytes 266272 | tf_op jit(solution)/shard_map/ppermute | solution.py:435
  29.8 2.1 %finish.3 = (bf16[512,2048]{1,0:T(8,128)(2,1)}, f32[1,16,128,128]{3,2,1,0:T(8,128)}) custom-call(s32[1]{0:T(128)} %bitcast.order_ref.refs_0_, s32[1,512]{1,0:T(1,128)S(1)} %get-tuple-element.43.seg_ref, f32[520,128]{1,0:T(8,128)S(1)} %get-tuple-element.46.even_ref.rest_0_, ...), custom_call_target="tpu_custom_call", output_to_operand_aliasing={{0}: (16, {}), {1}: (17, {})} | custom-call | flops 1 | bytes 1 | tf_op jit(solution)/shard_map/finish/pallas_call | solution.py:403
  (7 shorter events, 0.1 us)
Async XLA Ops:
  2.3 11.7 %collective-permute-start.3 = (f32[520,128]{1,0:T(8,128)S(1)}, f32[520,128]{1,0:T(8,128)S(1)}, u32[]{:S(2)}, u32[]{:S(2)}) collective-permute-start(f32[520,128]{1,0:T(8,128)S(1)} %get-tuple-element.59.refs_1_.rest_7_), channel_id=1, source_target_pairs={{0,2},{2,0},{4,6},{6,4},{8,10},{10,8},{12,14},{14,12},{1,3},{3,1},... | collective-permute-start | bytes 798728 | tf_op jit(solution)/shard_map/ppermute | solution.py:433
  5.7 6.8 %copy-start = (f32[2048]{0:T(1024)S(1)}, f32[2048]{0:T(1024)}, u32[]{:S(2)}) copy-start(f32[2048]{0:T(1024)} %param.15) | copy-start | bytes 24580
  5.7 10.9 %collective-permute-start.2 = (f32[520,128]{1,0:T(8,128)S(1)}, f32[520,128]{1,0:T(8,128)S(1)}, u32[]{:S(2)}, u32[]{:S(2)}) collective-permute-start(f32[520,128]{1,0:T(8,128)S(1)} %second_message.1.even_ref.rest_0_), channel_id=1, source_target_pairs={{0,4},{2,6},{4,8},{6,10},{8,12},{10,14},{12,0},{14,2},{1,5},{3,7},... | collective-permute-start | bytes 798728 | tf_op jit(solution)/shard_map/ppermute | solution.py:434
  10.3 10.1 %collective-permute-start.1 = (f32[520,128]{1,0:T(8,128)S(1)}, f32[520,128]{1,0:T(8,128)S(1)}, u32[]{:S(2)}, u32[]{:S(2)}) collective-permute-start(f32[520,128]{1,0:T(8,128)S(1)} %get-tuple-element.47.refs_1_.rest_7_), channel_id=1, source_target_pairs={{0,2},{2,0},{4,6},{6,4},{8,10},{10,8},{12,14},{14,12},{1,3},{3,1},... | collective-permute-start | bytes 798728 | tf_op jit(solution)/shard_map/ppermute | solution.py:433
  10.9 11.4 %collective-permute-start = (f32[520,128]{1,0:T(8,128)S(1)}, f32[520,128]{1,0:T(8,128)S(1)}, u32[]{:S(2)}, u32[]{:S(2)}) collective-permute-start(f32[520,128]{1,0:T(8,128)S(1)} %get-tuple-element.46.even_ref.rest_0_), channel_id=1, source_target_pairs={{0,4},{2,6},{4,8},{6,10},{8,12},{10,14},{12,0},{14,2},{1,5},{3,7},... | collective-permute-start | bytes 798728 | tf_op jit(solution)/shard_map/ppermute | solution.py:434
  16.6 10.3 %collective-permute-start.6 = (f32[520,128]{1,0:T(8,128)S(1)}, f32[520,128]{1,0:T(8,128)S(1)}, u32[]{:S(2)}, u32[]{:S(2)}) collective-permute-start(f32[520,128]{1,0:T(8,128)S(1)} %get-tuple-element.63.refs_0_), channel_id=1, source_target_pairs={{0,2},{2,0},{4,6},{6,4},{8,10},{10,8},{12,14},{14,12},{1,3},{3,1},... | collective-permute-start | bytes 798728 | tf_op jit(solution)/shard_map/ppermute | solution.py:433
  16.7 10.2 %collective-permute-start.7 = (f32[520,128]{1,0:T(8,128)S(1)}, f32[520,128]{1,0:T(8,128)S(1)}, u32[]{:S(2)}, u32[]{:S(2)}) collective-permute-start(f32[520,128]{1,0:T(8,128)S(1)} %get-tuple-element.79), channel_id=1, source_target_pairs={{0,4},{2,6},{4,8},{6,10},{8,12},{10,14},{12,0},{14,2},{1,5},{3,7},... | collective-permute-start | bytes 798728 | tf_op jit(solution)/shard_map/ppermute | solution.py:434
  22.3 7.0 %collective-permute-start.4 = (f32[520,128]{1,0:T(8,128)S(1)}, f32[520,128]{1,0:T(8,128)S(1)}, u32[]{:S(2)}, u32[]{:S(2)}) collective-permute-start(f32[520,128]{1,0:T(8,128)S(1)} %get-tuple-element.66.refs_0_), channel_id=1, source_target_pairs={{0,2},{2,0},{4,6},{6,4},{8,10},{10,8},{12,14},{14,12},{1,3},{3,1},... | collective-permute-start | bytes 798728 | tf_op jit(solution)/shard_map/ppermute | solution.py:433
  23.1 6.8 %collective-permute-start.5 = (f32[520,128]{1,0:T(8,128)S(1)}, f32[520,128]{1,0:T(8,128)S(1)}, u32[]{:S(2)}, u32[]{:S(2)}) collective-permute-start(f32[520,128]{1,0:T(8,128)S(1)} %get-tuple-element.69), channel_id=1, source_target_pairs={{0,4},{2,6},{4,8},{6,10},{8,12},{10,14},{1,5},{3,7},{5,9},{7,11},{... | collective-permute-start | bytes 798728 | tf_op jit(solution)/shard_map/ppermute | solution.py:435

commit v12 on v9

--- a/solution.py
+++ b/solution.py
@@ -359,35 +359,30 @@
         send(snap_ref, snap_hbm.at[0, pl.ds(first, heads)])
 
     rows = lax.broadcasted_iota(jnp.int32, (64, 128), 0).astype(F32)
+    tokens, size = seg.shape[1], inter_ref.shape[2]
     for number, (i, j, first, heads, both, number_valid, arrays) in enumerate(work):
-        o_ref, gate_ref, decay_ref, q_ref = arrays
-        gated_ref = scratch[2 * i]
-        tokens, size = seg.shape[1], q_ref.shape[1] // heads
-        columns = slice(j * size, (j + 1) * size)
-        q = q_ref[:, columns]
-        inter_ref[number % 4] = lax.dot_general(
+        q = arrays[3][:, j * size : (j + 1) * size]
+        inter_ref[number] = lax.dot_general(
             jnp.concatenate([q, q], axis=1), both, NN, preferred_element_type=F32
         )
+    for i, (first, heads, _) in enumerate(groups):
+        gated_ref = scratch[2 * i]
         for start in range(0, tokens, 64):
             here = slice(start, start + 64)
-            inter = inter_ref[number % 4, here, :]
-            inter = jnp.where(rows < number_valid - start, inter * decay_ref[here, columns], 0.0)
-            mixed = o_ref[here, columns] + inter
-            square = jnp.sum(mixed * mixed, axis=1, keepdims=True)
-            gated = mixed * gate_ref[here, columns] * lax.rsqrt(square + size * 1e-06)
-            gated_ref[here, columns] = gated.astype(BF16)
-            if number == len(work) - 1 and start % 128 == 64:
-                block = pl.ds(start - 64, 128)
-                there = pl.ds((first + j) * size, size)
-                send(gated_ref.at[block, pl.ds(j * size, size)], gated_hbm.at[block, there])
-        if number == len(work) - 1:
-            continue
-        alone = number + 2 == len(work) and j % 2 == 0
-        if alone or j % 2 == 1 or j == heads - 1:
-            begin = j if alone else j - j % 2
-            width = (j + 1 - begin) * size
-            there = pl.ds((first + begin) * size, width)
-            send(gated_ref.at[:, pl.ds(begin * size, width)], gated_hbm.at[:, there])
+            for number, (i_of, j, _, _, _, number_valid, arrays) in enumerate(work):
+                if i_of != i:
+                    continue
+                o_ref, gate_ref, decay_ref, _ = arrays
+                columns = slice(j * size, (j + 1) * size)
+                inter = inter_ref[number, here, :] * decay_ref[here, columns]
+                inter = jnp.where(rows < number_valid - start, inter, 0.0)
+                mixed = o_ref[here, columns] + inter
+                square = jnp.sum(mixed * mixed, axis=1, keepdims=True)
+                gated = mixed * gate_ref[here, columns] * lax.rsqrt(square + size * 1e-06)
+                gated_ref[here, columns] = gated.astype(BF16)
+            if start % 128 == 64:
+                block, there = pl.ds(start - 64, 128), pl.ds(first * size, heads * size)
+                send(gated_ref.at[block, :], gated_hbm.at[block, there])
     for copy in copies:
         copy.wait()
 
@@ -411,7 +406,10 @@
             jax.ShapeDtypeStruct((1, total, size, size), F32),
         ],
         scratch_shapes=scratch
-        + [pltpu.VMEM((4, tokens, size), F32), pltpu.SemaphoreType.DMA((2 * total,))],
+        + [
+            pltpu.VMEM((sum(many for _, many, _ in groups), tokens, size), F32),
+            pltpu.SemaphoreType.DMA((2 * total,)),
+        ],
         input_output_aliases={2 + len(arrays) + i: i for i in range(len(so_far))},
         compiler_params=pltpu.CompilerParams(vmem_limit_bytes=12 * MIB),
         cost_estimate=SHORT,

time: 32.1 us -> 32.2 us (level)
  no operation moved by 1% of the time
where the time goes in v12:
time: 32.2 us; the launch traced here: 32.1 us
  Pallas kernels  15.9 us (49%)
  starting transfers between devices  10.5 us (33%)
  waiting for transfers between devices  4.91 us (15%)
  between operations  0.77 us (2%)
    pallas_call x4, Pallas kernels, intra(): pl.pallas_call(functools.partial(intra_kernel, first, heads, len(through)...  6.2 us
    pallas_call x2, Pallas kernels, finish(): pl.pallas_call(functools.partial(final_kernel, groups, unread), in_specs=...  4.49 us
    ppermute x4, starting transfers between devices, shards(): swap = lambda x: lax.ppermute(x, 'seq', [(c, c ^ 1) for c in range(count)])  4.39 us
    ppermute x3, waiting for transfers between devices, shards(): lax.ppermute(x, 'seq', [(c, (c + 2) % count) for c in range(count)])  4.25 us
    ppermute x3, starting transfers between devices, shards(): lax.ppermute(x, 'seq', [(c, (c + 2) % count) for c in range(count)])  3.81 us
    pallas_call x1, Pallas kernels, rest_messages(): pl.pallas_call(functools.partial(rest_kernel, chunks, done), in_specs=[pl...  2.97 us
    ppermute x1, starting transfers between devices, shards(): lax.ppermute(x, 'seq', [(c, c + 2) for c in range(count - 2)])  2.29 us
    pallas_call x1, Pallas kernels, first_message(): pl.pallas_call(functools.partial(first_kernel, heads, chunks), in_specs=[...  1.69 us
  transfers between devices with their start and end apart: 8, of which 4 were waited for; matrix products, arithmetic and copies ran while one was open for 0% of the time, Pallas kernels for 37%

profile of v12, /device:TPU:0, one launch (start us, length us, event | category | flops | bytes accessed | tf_op | source)
XLA Modules:
  0.0 32.1 jit_solution(2450365517108277059)
XLA Ops:
  0.6 1.7 %first_message.1 = (f32[520,128]{1,0:T(8,128)S(1)}, f32[16,512]{1,0:T(8,128)S(1)}, f32[16,512]{1,0:T(8,128)S(1)}, s32[1,512]{1,0:T(1,128)S(1)}, bf16[512,512]{1,...) custom-call(s32[1]{0:T(128)} %bitcast.order_ref.refs_0_, ...), custom_call_target="tpu_custom_call" | custom-call | flops 1 | bytes 1 | tf_op jit(solution)/shard_map/first_message/pallas_call | solution.py:100
  2.3 3.0 %collective-permute-start.3 = (f32[520,128]{1,0:T(8,128)S(1)}, f32[520,128]{1,0:T(8,128)S(1)}, u32[]{:S(2)}, u32[]{:S(2)}) collective-permute-start(f32[520,128]{1,0:T(8,128)S(1)} %get-tuple-element.59.refs_1_.rest_7_), channel_id=1, source_target_pairs={{0,2},{2,0},{4,6},{6,4},{8,10},{10,8},{12,14},{14,12},{1,3},{3,1},... | collective-permute-start | bytes 798728 | tf_op jit(solution)/shard_map/ppermute | solution.py:431
  5.3 0.4 %second_message.1.even_ref.rest_0_ = f32[520,128]{1,0:T(8,128)S(1)} custom-call(s32[1,512]{1,0:T(1,128)S(1)} %get-tuple-element.43.seg_ref, f32[16,512]{1,0:T(8,128)S(1)} %get-tuple-element.44.a_ref, f32[16,512]{1,0:T(8,128)S(1)} %get-tuple-element.45.w_ref, bf16[512,512]{1,0:T(8,128)(2,1)S(1)} %get-tuple-element.57.k_ref, ...), custom_call_target="tpu_custom_call" | custom-call | flops 1 | bytes 1 | tf_op jit(solution)/shard_map/second_message/pallas_call | solution.py:127
  5.7 0.0 copy-start
  5.7 1.6 %collective-permute-start.2 = (f32[520,128]{1,0:T(8,128)S(1)}, f32[520,128]{1,0:T(8,128)S(1)}, u32[]{:S(2)}, u32[]{:S(2)}) collective-permute-start(f32[520,128]{1,0:T(8,128)S(1)} %second_message.1.even_ref.rest_0_), channel_id=1, source_target_pairs={{0,4},{2,6},{4,8},{6,10},{8,12},{10,14},{12,0},{14,2},{1,5},{3,7},... | collective-permute-start | bytes 798728 | tf_op jit(solution)/shard_map/ppermute | solution.py:432
  7.3 3.0 %rest_messages.1 = (f32[520,128]{1,0:T(8,128)S(1)}, f32[520,128]{1,0:T(8,128)S(1)}, f32[512,512]{1,0:T(8,128)S(1)}, bf16[512,512]{1,0:T(8,128)(2,1)S(1)}, bf16[5...) custom-call(s32[1,512]{1,0:T(1,128)S(1)} %get-tuple-element.43.seg_r, ...), custom_call_target="tpu_custom_call" | custom-call | flops 1 | bytes 1 | tf_op jit(solution)/shard_map/rest_messages/pallas_call | solution.py:174
  10.3 0.6 %collective-permute-start.1 = (f32[520,128]{1,0:T(8,128)S(1)}, f32[520,128]{1,0:T(8,128)S(1)}, u32[]{:S(2)}, u32[]{:S(2)}) collective-permute-start(f32[520,128]{1,0:T(8,128)S(1)} %get-tuple-element.47.refs_1_.rest_7_), channel_id=1, source_target_pairs={{0,2},{2,0},{4,6},{6,4},{8,10},{10,8},{12,14},{14,12},{1,3},{3,1},... | collective-permute-start | bytes 798728 | tf_op jit(solution)/shard_map/ppermute | solution.py:431
  10.9 1.6 %collective-permute-start = (f32[520,128]{1,0:T(8,128)S(1)}, f32[520,128]{1,0:T(8,128)S(1)}, u32[]{:S(2)}, u32[]{:S(2)}) collective-permute-start(f32[520,128]{1,0:T(8,128)S(1)} %get-tuple-element.46.even_ref.rest_0_), channel_id=1, source_target_pairs={{0,4},{2,6},{4,8},{6,10},{8,12},{10,14},{12,0},{14,2},{1,5},{3,7},... | collective-permute-start | bytes 798728 | tf_op jit(solution)/shard_map/ppermute | solution.py:432
  12.5 1.5 %intra_span.4 = (f32[512,512]{1,0:T(8,128)S(1)}, f32[512,512]{1,0:T(8,128)S(1)}, f32[512,512]{1,0:T(8,128)S(1)}) custom-call(f32[512,512]{1,0:T(8,128)S(1)} %get-tuple-element.48.mask_ref, f32[16,512]{1,0:T(8,128)S(1)} %get-tuple-element.44.a_ref, f32[1,2048]{1,0:T(1,128)S(1)} %bitcast.4, bf16[512,512]{1,0:T(8,128)(2,1)S(1)} %get-tuple-element.60.q_ref.rest_6_, ...), custom_call_target="tpu_custom_call" | custom-call | flops 1 | bytes 1 | tf_op jit(solution)/shard_map/intra_span/pallas_call | solution.py:303
  14.1 0.1 join_windows.2.refs_0_
  14.1 2.5 %collective-permute-done.2.odd_ref.rest_2_ = f32[520,128]{1,0:T(8,128)S(1)} collective-permute-done((f32[520,128]{1,0:T(8,128)S(1)}, f32[520,128]{1,0:T(8,128)S(1)}, u32[]{:S(2)}, u32[]{:S(2)}) %collective-permute-start.2) | collective-permute-done | bytes 266272 | tf_op jit(solution)/shard_map/ppermute | solution.py:432
  16.6 0.1 collective-permute-start.6
  16.7 0.6 %collective-permute-start.7 = (f32[520,128]{1,0:T(8,128)S(1)}, f32[520,128]{1,0:T(8,128)S(1)}, u32[]{:S(2)}, u32[]{:S(2)}) collective-permute-start(f32[520,128]{1,0:T(8,128)S(1)} %get-tuple-element.79), channel_id=1, source_target_pairs={{0,4},{2,6},{4,8},{6,10},{8,12},{10,14},{12,0},{14,2},{1,5},{3,7},... | collective-permute-start | bytes 798728 | tf_op jit(solution)/shard_map/ppermute | solution.py:432
  17.3 1.6 %intra_span.5 = (f32[512,512]{1,0:T(8,128)S(1)}, f32[512,512]{1,0:T(8,128)S(1)}, f32[512,512]{1,0:T(8,128)S(1)}) custom-call(f32[512,512]{1,0:T(8,128)S(1)} %get-tuple-element.48.mask_ref, f32[16,512]{1,0:T(8,128)S(1)} %get-tuple-element.44.a_ref, f32[1,2048]{1,0:T(1,128)S(1)} %bitcast.5, bf16[512,512]{1,0:T(8,128)(2,1)S(1)} %get-tuple-element.53.q_ref.rest_13_, ...), custom_call_target="tpu_custom_call" | custom-call | flops 1 | bytes 1 | tf_op jit(solution)/shard_map/intra_span/pallas_call | solution.py:303
  18.9 1.6 %intra_span.6 = (f32[512,512]{1,0:T(8,128)S(1)}, f32[512,512]{1,0:T(8,128)S(1)}, f32[512,512]{1,0:T(8,128)S(1)}) custom-call(f32[512,512]{1,0:T(8,128)S(1)} %get-tuple-element.48.mask_ref, f32[16,512]{1,0:T(8,128)S(1)} %get-tuple-element.44.a_ref, f32[1,2048]{1,0:T(1,128)S(1)} %bitcast.6, bf16[512,512]{1,0:T(8,128)(2,1)S(1)} %get-tuple-element.49.q_ref.rest_6_, ...), custom_call_target="tpu_custom_call" | custom-call | flops 1 | bytes 1 | tf_op jit(solution)/shard_map/intra_span/pallas_call | solution.py:303
  20.4 0.1 join_windows.3.refs_0_
  20.5 1.8 %collective-permute-done.odd_ref.rest_2_ = f32[520,128]{1,0:T(8,128)S(1)} collective-permute-done((f32[520,128]{1,0:T(8,128)S(1)}, f32[520,128]{1,0:T(8,128)S(1)}, u32[]{:S(2)}, u32[]{:S(2)}) %collective-permute-start) | collective-permute-done | bytes 266272 | tf_op jit(solution)/shard_map/ppermute | solution.py:432
  22.3 0.7 %collective-permute-start.4 = (f32[520,128]{1,0:T(8,128)S(1)}, f32[520,128]{1,0:T(8,128)S(1)}, u32[]{:S(2)}, u32[]{:S(2)}) collective-permute-start(f32[520,128]{1,0:T(8,128)S(1)} %get-tuple-element.66.refs_0_), channel_id=1, source_target_pairs={{0,2},{2,0},{4,6},{6,4},{8,10},{10,8},{12,14},{14,12},{1,3},{3,1},... | collective-permute-start | bytes 798728 | tf_op jit(solution)/shard_map/ppermute | solution.py:431
  23.1 2.3 %collective-permute-start.5 = (f32[520,128]{1,0:T(8,128)S(1)}, f32[520,128]{1,0:T(8,128)S(1)}, u32[]{:S(2)}, u32[]{:S(2)}) collective-permute-start(f32[520,128]{1,0:T(8,128)S(1)} %get-tuple-element.69), channel_id=1, source_target_pairs={{0,4},{2,6},{4,8},{6,10},{8,12},{10,14},{1,5},{3,7},{5,9},{7,11},{... | collective-permute-start | bytes 798728 | tf_op jit(solution)/shard_map/ppermute | solution.py:433
  25.3 1.5 %intra_span.7 = (f32[512,512]{1,0:T(8,128)S(1)}, f32[512,512]{1,0:T(8,128)S(1)}, f32[512,512]{1,0:T(8,128)S(1)}) custom-call(f32[512,512]{1,0:T(8,128)S(1)} %get-tuple-element.48.mask_ref, f32[16,512]{1,0:T(8,128)S(1)} %get-tuple-element.44.a_ref, f32[1,2048]{1,0:T(1,128)S(1)} %bitcast.7, bf16[512,512]{1,0:T(8,128)(2,1)S(1)} %get-tuple-element.70.q_ref.rest_13_, ...), custom_call_target="tpu_custom_call" | custom-call | flops 1 | bytes 1 | tf_op jit(solution)/shard_map/intra_span/pallas_call | solution.py:303
  26.9 2.2 %finish.2 = (bf16[512,2048]{1,0:T(8,128)(2,1)}, f32[1,16,128,128]{3,2,1,0:T(8,128)}) custom-call(s32[1]{0:T(128)} %bitcast.order_ref.refs_0_, s32[1,512]{1,0:T(1,128)S(1)} %get-tuple-element.43.seg_ref, f32[520,128]{1,0:T(8,128)S(1)} %second_message.1.even_ref.rest_0_, f32[520,128]{1,0:T(8,128)S(1)} %collective-permute-done.6.rest_1_, ...), custom_call_target="tpu_custom_call" | custom-call | flops 1 | bytes 1 | tf_op jit(solution)/shard_map/finish/pallas_call | solution.py:398
  29.2 0.2 collective-permute-done.4.rest_1_
  29.4 0.5 %collective-permute-done.5.rest_9_ = f32[520,128]{1,0:T(8,128)S(1)} collective-permute-done((f32[520,128]{1,0:T(8,128)S(1)}, f32[520,128]{1,0:T(8,128)S(1)}, u32[]{:S(2)}, u32[]{:S(2)}) %collective-permute-start.5) | collective-permute-done | bytes 266272 | tf_op jit(solution)/shard_map/ppermute | solution.py:433
  29.8 2.2 %finish.3 = (bf16[512,2048]{1,0:T(8,128)(2,1)}, f32[1,16,128,128]{3,2,1,0:T(8,128)}) custom-call(s32[1]{0:T(128)} %bitcast.order_ref.refs_0_, s32[1,512]{1,0:T(1,128)S(1)} %get-tuple-element.43.seg_ref, f32[520,128]{1,0:T(8,128)S(1)} %get-tuple-element.46.even_ref.rest_0_, ...), custom_call_target="tpu_custom_call", output_to_operand_aliasing={{0}: (16, {}), {1}: (17, {})} | custom-call | flops 1 | bytes 1 | tf_op jit(solution)/shard_map/finish/pallas_call | solution.py:398
  (7 shorter events, 0.1 us)
Async XLA Ops:
  2.3 11.7 %collective-permute-start.3 = (f32[520,128]{1,0:T(8,128)S(1)}, f32[520,128]{1,0:T(8,128)S(1)}, u32[]{:S(2)}, u32[]{:S(2)}) collective-permute-start(f32[520,128]{1,0:T(8,128)S(1)} %get-tuple-element.59.refs_1_.rest_7_), channel_id=1, source_target_pairs={{0,2},{2,0},{4,6},{6,4},{8,10},{10,8},{12,14},{14,12},{1,3},{3,1},... | collective-permute-start | bytes 798728 | tf_op jit(solution)/shard_map/ppermute | solution.py:431
  5.7 6.8 %copy-start = (f32[2048]{0:T(1024)S(1)}, f32[2048]{0:T(1024)}, u32[]{:S(2)}) copy-start(f32[2048]{0:T(1024)} %param.15) | copy-start | bytes 24580
  5.7 10.9 %collective-permute-start.2 = (f32[520,128]{1,0:T(8,128)S(1)}, f32[520,128]{1,0:T(8,128)S(1)}, u32[]{:S(2)}, u32[]{:S(2)}) collective-permute-start(f32[520,128]{1,0:T(8,128)S(1)} %second_message.1.even_ref.rest_0_), channel_id=1, source_target_pairs={{0,4},{2,6},{4,8},{6,10},{8,12},{10,14},{12,0},{14,2},{1,5},{3,7},... | collective-permute-start | bytes 798728 | tf_op jit(solution)/shard_map/ppermute | solution.py:432
  10.3 10.1 %collective-permute-start.1 = (f32[520,128]{1,0:T(8,128)S(1)}, f32[520,128]{1,0:T(8,128)S(1)}, u32[]{:S(2)}, u32[]{:S(2)}) collective-permute-start(f32[520,128]{1,0:T(8,128)S(1)} %get-tuple-element.47.refs_1_.rest_7_), channel_id=1, source_target_pairs={{0,2},{2,0},{4,6},{6,4},{8,10},{10,8},{12,14},{14,12},{1,3},{3,1},... | collective-permute-start | bytes 798728 | tf_op jit(solution)/shard_map/ppermute | solution.py:431
  10.9 11.4 %collective-permute-start = (f32[520,128]{1,0:T(8,128)S(1)}, f32[520,128]{1,0:T(8,128)S(1)}, u32[]{:S(2)}, u32[]{:S(2)}) collective-permute-start(f32[520,128]{1,0:T(8,128)S(1)} %get-tuple-element.46.even_ref.rest_0_), channel_id=1, source_target_pairs={{0,4},{2,6},{4,8},{6,10},{8,12},{10,14},{12,0},{14,2},{1,5},{3,7},... | collective-permute-start | bytes 798728 | tf_op jit(solution)/shard_map/ppermute | solution.py:432
  16.6 10.3 %collective-permute-start.6 = (f32[520,128]{1,0:T(8,128)S(1)}, f32[520,128]{1,0:T(8,128)S(1)}, u32[]{:S(2)}, u32[]{:S(2)}) collective-permute-start(f32[520,128]{1,0:T(8,128)S(1)} %get-tuple-element.63.refs_0_), channel_id=1, source_target_pairs={{0,2},{2,0},{4,6},{6,4},{8,10},{10,8},{12,14},{14,12},{1,3},{3,1},... | collective-permute-start | bytes 798728 | tf_op jit(solution)/shard_map/ppermute | solution.py:431
  16.7 10.2 %collective-permute-start.7 = (f32[520,128]{1,0:T(8,128)S(1)}, f32[520,128]{1,0:T(8,128)S(1)}, u32[]{:S(2)}, u32[]{:S(2)}) collective-permute-start(f32[520,128]{1,0:T(8,128)S(1)} %get-tuple-element.79), channel_id=1, source_target_pairs={{0,4},{2,6},{4,8},{6,10},{8,12},{10,14},{12,0},{14,2},{1,5},{3,7},... | collective-permute-start | bytes 798728 | tf_op jit(solution)/shard_map/ppermute | solution.py:432
  22.3 7.0 %collective-permute-start.4 = (f32[520,128]{1,0:T(8,128)S(1)}, f32[520,128]{1,0:T(8,128)S(1)}, u32[]{:S(2)}, u32[]{:S(2)}) collective-permute-start(f32[520,128]{1,0:T(8,128)S(1)} %get-tuple-element.66.refs_0_), channel_id=1, source_target_pairs={{0,2},{2,0},{4,6},{6,4},{8,10},{10,8},{12,14},{14,12},{1,3},{3,1},... | collective-permute-start | bytes 798728 | tf_op jit(solution)/shard_map/ppermute | solution.py:431
  23.1 6.8 %collective-permute-start.5 = (f32[520,128]{1,0:T(8,128)S(1)}, f32[520,128]{1,0:T(8,128)S(1)}, u32[]{:S(2)}, u32[]{:S(2)}) collective-permute-start(f32[520,128]{1,0:T(8,128)S(1)} %get-tuple-element.69), channel_id=1, source_target_pairs={{0,4},{2,6},{4,8},{6,10},{8,12},{10,14},{1,5},{3,7},{5,9},{7,11},{... | collective-permute-start | bytes 798728 | tf_op jit(solution)/shard_map/ppermute | solution.py:433

commit v13 on v9

--- a/solution.py
+++ b/solution.py
@@ -435,7 +435,7 @@
     ahead = lambda x: lax.ppermute(x, "seq", [(c, c + 2) for c in range(count - 2)])
 
     half = heads // 2
-    even, odd = half // 2, half // 2
+    even = odd = half - half * 3 // 8
     chunks = [(0, half - even), (half, half - odd), (half - even, even), (heads - odd, odd)]
 
     def widened(x, many, shift, window):

time: 32.1 us -> 44.3 us (1.38)
  waiting for transfers between devices: 5.01 us -> 15.7 us
  starting transfers between devices: 10.5 us -> 12.1 us
    ppermute x4, waiting for transfers between devices: 0.3 us -> 12.4 us  [shards(): swap = lambda x: lax.ppermute(x, 'seq', [(c, c ^ 1) for c in range(count)])]
    ppermute x4, starting transfers between devices: 4.39 us -> 5.69 us  [shards(): swap = lambda x: lax.ppermute(x, 'seq', [(c, c ^ 1) for c in range(count)])]
    ppermute x3, waiting for transfers between devices: 4.25 us -> 3.28 us  [shards(): lax.ppermute(x, 'seq', [(c, (c + 2) % count) for c in range(count)])]
    ppermute x3, starting transfers between devices: 3.81 us -> 4.77 us  [shards(): lax.ppermute(x, 'seq', [(c, (c + 2) % count) for c in range(count)])]
    ppermute x1, starting transfers between devices: 2.29 us -> 1.63 us  [shards(): lax.ppermute(x, 'seq', [(c, c + 2) for c in range(count - 2)])]
    ppermute x1, waiting for transfers between devices: 0.46 us -> 0.01 us  [shards(): lax.ppermute(x, 'seq', [(c, c + 2) for c in range(count - 2)])]
  transfers between devices with their start and end apart: 8 -> 8, of which waited for: 4 -> 3; matrix products, arithmetic and copies ran while one was open for 0% -> 0% of each run, Pallas kernels for 37% -> 19%
where the time goes in v13:
time: 44.3 us; the launch traced here: 44.2 us
  waiting for transfers between devices  15.7 us (35%)
  Pallas kernels  15.6 us (35%)
  starting transfers between devices  12.1 us (27%)
  between operations  0.77 us (2%)
    ppermute x4, waiting for transfers between devices, shards(): swap = lambda x: lax.ppermute(x, 'seq', [(c, c ^ 1) for c in range(count)])  12.4 us
    pallas_call x4, Pallas kernels, intra(): pl.pallas_call(functools.partial(intra_kernel, first, heads, len(through)...  6.11 us
    ppermute x4, starting transfers between devices, shards(): swap = lambda x: lax.ppermute(x, 'seq', [(c, c ^ 1) for c in range(count)])  5.69 us
    ppermute x3, starting transfers between devices, shards(): lax.ppermute(x, 'seq', [(c, (c + 2) % count) for c in range(count)])  4.77 us
    pallas_call x2, Pallas kernels, finish(): pl.pallas_call(functools.partial(final_kernel, groups, unread), in_specs=...  4.28 us
    ppermute x3, waiting for transfers between devices, shards(): lax.ppermute(x, 'seq', [(c, (c + 2) % count) for c in range(count)])  3.28 us
    pallas_call x1, Pallas kernels, rest_messages(): pl.pallas_call(functools.partial(rest_kernel, chunks, done), in_specs=[pl...  3.14 us
    ppermute x1, starting transfers between devices, shards(): lax.ppermute(x, 'seq', [(c, c + 2) for c in range(count - 2)])  1.63 us
  transfers between devices with their start and end apart: 8, of which 3 were waited for; matrix products, arithmetic and copies ran while one was open for 0% of the time, Pallas kernels for 19%

profile of v13, /device:TPU:0, one launch (start us, length us, event | category | flops | bytes accessed | tf_op | source)
XLA Modules:
  0.0 44.2 jit_solution(10881925175493197249)
XLA Ops:
  0.6 1.6 %first_message.1 = (f32[392,128]{1,0:T(8,128)S(1)}, f32[16,512]{1,0:T(8,128)S(1)}, f32[16,512]{1,0:T(8,128)S(1)}, s32[1,512]{1,0:T(1,128)S(1)}, bf16[512,384]{1,...) custom-call(s32[1]{0:T(128)} %bitcast.order_ref.refs_0_, ...), custom_call_target="tpu_custom_call" | custom-call | flops 1 | bytes 1 | tf_op jit(solution)/shard_map/first_message/pallas_call | solution.py:100
  2.2 0.0 copy-start
  2.2 3.1 %rest_messages.1 = (f32[648,128]{1,0:T(8,128)S(1)}, f32[648,128]{1,0:T(8,128)S(1)}, f32[512,512]{1,0:T(8,128)S(1)}, bf16[512,640]{1,0:T(8,128)(2,1)S(1)}, bf16[5...) custom-call(s32[1,512]{1,0:T(1,128)S(1)} %get-tuple-element.43.seg_r, ...), custom_call_target="tpu_custom_call" | custom-call | flops 1 | bytes 1 | tf_op jit(solution)/shard_map/rest_messages/pallas_call | solution.py:174
  5.4 3.0 %collective-permute-start.1 = (f32[648,128]{1,0:T(8,128)S(1)}, f32[648,128]{1,0:T(8,128)S(1)}, u32[]{:S(2)}, u32[]{:S(2)}) collective-permute-start(f32[648,128]{1,0:T(8,128)S(1)} %get-tuple-element.47.refs_1_.rest_7_), channel_id=1, source_target_pairs={{0,2},{2,0},{4,6},{6,4},{8,10},{10,8},{12,14},{14,12},{1,3},{3,1},... | collective-permute-start | bytes 995336 | tf_op jit(solution)/shard_map/ppermute | solution.py:433
  8.4 1.6 %collective-permute-start = (f32[648,128]{1,0:T(8,128)S(1)}, f32[648,128]{1,0:T(8,128)S(1)}, u32[]{:S(2)}, u32[]{:S(2)}) collective-permute-start(f32[648,128]{1,0:T(8,128)S(1)} %get-tuple-element.46.even_ref.rest_0_), channel_id=1, source_target_pairs={{0,4},{2,6},{4,8},{6,10},{8,12},{10,14},{12,0},{14,2},{1,5},{3,7},... | collective-permute-start | bytes 995336 | tf_op jit(solution)/shard_map/ppermute | solution.py:434
  10.0 0.5 %collective-permute-start.3 = (f32[392,128]{1,0:T(8,128)S(1)}, f32[392,128]{1,0:T(8,128)S(1)}, u32[]{:S(2)}, u32[]{:S(2)}) collective-permute-start(f32[392,128]{1,0:T(8,128)S(1)} %get-tuple-element.59.refs_1_.rest_7_), channel_id=1, source_target_pairs={{0,2},{2,0},{4,6},{6,4},{8,10},{10,8},{12,14},{14,12},{1,3},{3,1},... | collective-permute-start | bytes 602120 | tf_op jit(solution)/shard_map/ppermute | solution.py:433
  10.5 0.3 second_message.1.even_ref.rest_0_
  10.8 1.6 %collective-permute-start.2 = (f32[392,128]{1,0:T(8,128)S(1)}, f32[392,128]{1,0:T(8,128)S(1)}, u32[]{:S(2)}, u32[]{:S(2)}) collective-permute-start(f32[392,128]{1,0:T(8,128)S(1)} %second_message.1.even_ref.rest_0_), channel_id=1, source_target_pairs={{0,4},{2,6},{4,8},{6,10},{8,12},{10,14},{12,0},{14,2},{1,5},{3,7},... | collective-permute-start | bytes 602120 | tf_op jit(solution)/shard_map/ppermute | solution.py:434
  12.5 1.2 %intra_span.4 = (f32[512,384]{1,0:T(8,128)S(1)}, f32[512,384]{1,0:T(8,128)S(1)}, f32[512,384]{1,0:T(8,128)S(1)}) custom-call(f32[512,512]{1,0:T(8,128)S(1)} %get-tuple-element.48.mask_ref, f32[16,512]{1,0:T(8,128)S(1)} %get-tuple-element.44.a_ref, f32[1,2048]{1,0:T(1,128)S(1)} %bitcast.4, bf16[512,384]{1,0:T(8,128)(2,1)S(1)} %get-tuple-element.60.q_ref.rest_6_, ...), custom_call_target="tpu_custom_call" | custom-call | flops 1 | bytes 1 | tf_op jit(solution)/shard_map/intra_span/pallas_call | solution.py:303
  13.7 6.8 %collective-permute-done.3.refs_2_.rest_8_ = f32[392,128]{1,0:T(8,128)S(1)} collective-permute-done((f32[392,128]{1,0:T(8,128)S(1)}, f32[392,128]{1,0:T(8,128)S(1)}, u32[]{:S(2)}, u32[]{:S(2)}) %collective-permute-start.3) | collective-permute-done | bytes 200736 | tf_op jit(solution)/shard_map/ppermute | solution.py:433
  20.5 3.3 %collective-permute-done.2.odd_ref.rest_2_ = f32[392,128]{1,0:T(8,128)S(1)} collective-permute-done((f32[392,128]{1,0:T(8,128)S(1)}, f32[392,128]{1,0:T(8,128)S(1)}, u32[]{:S(2)}, u32[]{:S(2)}) %collective-permute-start.2) | collective-permute-done | bytes 200736 | tf_op jit(solution)/shard_map/ppermute | solution.py:434
  23.8 1.2 %intra_span.5 = (f32[512,384]{1,0:T(8,128)S(1)}, f32[512,384]{1,0:T(8,128)S(1)}, f32[512,384]{1,0:T(8,128)S(1)}) custom-call(f32[512,512]{1,0:T(8,128)S(1)} %get-tuple-element.48.mask_ref, f32[16,512]{1,0:T(8,128)S(1)} %get-tuple-element.44.a_ref, f32[1,2048]{1,0:T(1,128)S(1)} %bitcast.5, bf16[512,384]{1,0:T(8,128)(2,1)S(1)} %get-tuple-element.53.q_ref.rest_13_, ...), custom_call_target="tpu_custom_call" | custom-call | flops 1 | bytes 1 | tf_op jit(solution)/shard_map/intra_span/pallas_call | solution.py:303
  25.1 1.8 %intra_span.6 = (f32[512,640]{1,0:T(8,128)S(1)}, f32[512,640]{1,0:T(8,128)S(1)}, f32[512,640]{1,0:T(8,128)S(1)}) custom-call(f32[512,512]{1,0:T(8,128)S(1)} %get-tuple-element.48.mask_ref, f32[16,512]{1,0:T(8,128)S(1)} %get-tuple-element.44.a_ref, f32[1,2048]{1,0:T(1,128)S(1)} %bitcast.6, bf16[512,640]{1,0:T(8,128)(2,1)S(1)} %get-tuple-element.49.q_ref.rest_6_, ...), custom_call_target="tpu_custom_call" | custom-call | flops 1 | bytes 1 | tf_op jit(solution)/shard_map/intra_span/pallas_call | solution.py:303
  26.9 0.0 collective-permute-done.1.refs_2_.rest_8_
  26.9 0.1 join_windows.3.refs_0_
  27.0 0.1 pick_message.3
  27.1 0.6 %collective-permute-start.4 = (f32[648,128]{1,0:T(8,128)S(1)}, f32[648,128]{1,0:T(8,128)S(1)}, u32[]{:S(2)}, u32[]{:S(2)}) collective-permute-start(f32[648,128]{1,0:T(8,128)S(1)} %get-tuple-element.66.refs_0_), channel_id=1, source_target_pairs={{0,2},{2,0},{4,6},{6,4},{8,10},{10,8},{12,14},{14,12},{1,3},{3,1},... | collective-permute-start | bytes 995336 | tf_op jit(solution)/shard_map/ppermute | solution.py:433
  27.7 1.6 %collective-permute-start.5 = (f32[648,128]{1,0:T(8,128)S(1)}, f32[648,128]{1,0:T(8,128)S(1)}, u32[]{:S(2)}, u32[]{:S(2)}) collective-permute-start(f32[648,128]{1,0:T(8,128)S(1)} %get-tuple-element.69), channel_id=1, source_target_pairs={{0,4},{2,6},{4,8},{6,10},{8,12},{10,14},{1,5},{3,7},{5,9},{7,11},{... | collective-permute-start | bytes 995336 | tf_op jit(solution)/shard_map/ppermute | solution.py:435
  29.3 1.6 %collective-permute-start.6 = (f32[392,128]{1,0:T(8,128)S(1)}, f32[392,128]{1,0:T(8,128)S(1)}, u32[]{:S(2)}, u32[]{:S(2)}) collective-permute-start(f32[392,128]{1,0:T(8,128)S(1)} %get-tuple-element.63.refs_0_), channel_id=1, source_target_pairs={{0,2},{2,0},{4,6},{6,4},{8,10},{10,8},{12,14},{14,12},{1,3},{3,1},... | collective-permute-start | bytes 602120 | tf_op jit(solution)/shard_map/ppermute | solution.py:433
  30.9 1.6 %collective-permute-start.7 = (f32[392,128]{1,0:T(8,128)S(1)}, f32[392,128]{1,0:T(8,128)S(1)}, u32[]{:S(2)}, u32[]{:S(2)}) collective-permute-start(f32[392,128]{1,0:T(8,128)S(1)} %get-tuple-element.79), channel_id=1, source_target_pairs={{0,4},{2,6},{4,8},{6,10},{8,12},{10,14},{12,0},{14,2},{1,5},{3,7},... | collective-permute-start | bytes 602120 | tf_op jit(solution)/shard_map/ppermute | solution.py:434
  32.4 1.8 %intra_span.7 = (f32[512,640]{1,0:T(8,128)S(1)}, f32[512,640]{1,0:T(8,128)S(1)}, f32[512,640]{1,0:T(8,128)S(1)}) custom-call(f32[512,512]{1,0:T(8,128)S(1)} %get-tuple-element.48.mask_ref, f32[16,512]{1,0:T(8,128)S(1)} %get-tuple-element.44.a_ref, f32[1,2048]{1,0:T(1,128)S(1)} %bitcast.7, bf16[512,640]{1,0:T(8,128)(2,1)S(1)} %get-tuple-element.70.q_ref.rest_13_, ...), custom_call_target="tpu_custom_call" | custom-call | flops 1 | bytes 1 | tf_op jit(solution)/shard_map/intra_span/pallas_call | solution.py:303
  34.2 5.6 %collective-permute-done.6.rest_1_ = f32[392,128]{1,0:T(8,128)S(1)} collective-permute-done((f32[392,128]{1,0:T(8,128)S(1)}, f32[392,128]{1,0:T(8,128)S(1)}, u32[]{:S(2)}, u32[]{:S(2)}) %collective-permute-start.6) | collective-permute-done | bytes 200736 | tf_op jit(solution)/shard_map/ppermute | solution.py:433
  39.8 1.9 %finish.2 = (bf16[512,2048]{1,0:T(8,128)(2,1)}, f32[1,16,128,128]{3,2,1,0:T(8,128)}) custom-call(s32[1]{0:T(128)} %bitcast.order_ref.refs_0_, s32[1,512]{1,0:T(1,128)S(1)} %get-tuple-element.43.seg_ref, f32[392,128]{1,0:T(8,128)S(1)} %second_message.1.even_ref.rest_0_, f32[392,128]{1,0:T(8,128)S(1)} %collective-permute-done.6.rest_1_, ...), custom_call_target="tpu_custom_call" | custom-call | flops 1 | bytes 1 | tf_op jit(solution)/shard_map/finish/pallas_call | solution.py:403
  41.8 2.4 %finish.3 = (bf16[512,2048]{1,0:T(8,128)(2,1)}, f32[1,16,128,128]{3,2,1,0:T(8,128)}) custom-call(s32[1]{0:T(128)} %bitcast.order_ref.refs_0_, s32[1,512]{1,0:T(1,128)S(1)} %get-tuple-element.43.seg_ref, f32[648,128]{1,0:T(8,128)S(1)} %get-tuple-element.46.even_ref.rest_0_, ...), custom_call_target="tpu_custom_call", output_to_operand_aliasing={{0}: (16, {}), {1}: (17, {})} | custom-call | flops 1 | bytes 1 | tf_op jit(solution)/shard_map/finish/pallas_call | solution.py:403
  (7 shorter events, 0.1 us)
Async XLA Ops:
  2.2 10.2 %copy-start = (f32[2048]{0:T(1024)S(1)}, f32[2048]{0:T(1024)}, u32[]{:S(2)}) copy-start(f32[2048]{0:T(1024)} %param.15) | copy-start | bytes 24580
  5.4 21.5 %collective-permute-start.1 = (f32[648,128]{1,0:T(8,128)S(1)}, f32[648,128]{1,0:T(8,128)S(1)}, u32[]{:S(2)}, u32[]{:S(2)}) collective-permute-start(f32[648,128]{1,0:T(8,128)S(1)} %get-tuple-element.47.refs_1_.rest_7_), channel_id=1, source_target_pairs={{0,2},{2,0},{4,6},{6,4},{8,10},{10,8},{12,14},{14,12},{1,3},{3,1},... | collective-permute-start | bytes 995336 | tf_op jit(solution)/shard_map/ppermute | solution.py:433
  8.4 18.6 %collective-permute-start = (f32[648,128]{1,0:T(8,128)S(1)}, f32[648,128]{1,0:T(8,128)S(1)}, u32[]{:S(2)}, u32[]{:S(2)}) collective-permute-start(f32[648,128]{1,0:T(8,128)S(1)} %get-tuple-element.46.even_ref.rest_0_), channel_id=1, source_target_pairs={{0,4},{2,6},{4,8},{6,10},{8,12},{10,14},{12,0},{14,2},{1,5},{3,7},... | collective-permute-start | bytes 995336 | tf_op jit(solution)/shard_map/ppermute | solution.py:434
  10.0 10.5 %collective-permute-start.3 = (f32[392,128]{1,0:T(8,128)S(1)}, f32[392,128]{1,0:T(8,128)S(1)}, u32[]{:S(2)}, u32[]{:S(2)}) collective-permute-start(f32[392,128]{1,0:T(8,128)S(1)} %get-tuple-element.59.refs_1_.rest_7_), channel_id=1, source_target_pairs={{0,2},{2,0},{4,6},{6,4},{8,10},{10,8},{12,14},{14,12},{1,3},{3,1},... | collective-permute-start | bytes 602120 | tf_op jit(solution)/shard_map/ppermute | solution.py:433
  10.8 13.0 %collective-permute-start.2 = (f32[392,128]{1,0:T(8,128)S(1)}, f32[392,128]{1,0:T(8,128)S(1)}, u32[]{:S(2)}, u32[]{:S(2)}) collective-permute-start(f32[392,128]{1,0:T(8,128)S(1)} %second_message.1.even_ref.rest_0_), channel_id=1, source_target_pairs={{0,4},{2,6},{4,8},{6,10},{8,12},{10,14},{12,0},{14,2},{1,5},{3,7},... | collective-permute-start | bytes 602120 | tf_op jit(solution)/shard_map/ppermute | solution.py:434
  27.1 14.7 %collective-permute-start.4 = (f32[648,128]{1,0:T(8,128)S(1)}, f32[648,128]{1,0:T(8,128)S(1)}, u32[]{:S(2)}, u32[]{:S(2)}) collective-permute-start(f32[648,128]{1,0:T(8,128)S(1)} %get-tuple-element.66.refs_0_), channel_id=1, source_target_pairs={{0,2},{2,0},{4,6},{6,4},{8,10},{10,8},{12,14},{14,12},{1,3},{3,1},... | collective-permute-start | bytes 995336 | tf_op jit(solution)/shard_map/ppermute | solution.py:433
  27.7 14.1 %collective-permute-start.5 = (f32[648,128]{1,0:T(8,128)S(1)}, f32[648,128]{1,0:T(8,128)S(1)}, u32[]{:S(2)}, u32[]{:S(2)}) collective-permute-start(f32[648,128]{1,0:T(8,128)S(1)} %get-tuple-element.69), channel_id=1, source_target_pairs={{0,4},{2,6},{4,8},{6,10},{8,12},{10,14},{1,5},{3,7},{5,9},{7,11},{... | collective-permute-start | bytes 995336 | tf_op jit(solution)/shard_map/ppermute | solution.py:435
  29.3 10.5 %collective-permute-start.6 = (f32[392,128]{1,0:T(8,128)S(1)}, f32[392,128]{1,0:T(8,128)S(1)}, u32[]{:S(2)}, u32[]{:S(2)}) collective-permute-start(f32[392,128]{1,0:T(8,128)S(1)} %get-tuple-element.63.refs_0_), channel_id=1, source_target_pairs={{0,2},{2,0},{4,6},{6,4},{8,10},{10,8},{12,14},{14,12},{1,3},{3,1},... | collective-permute-start | bytes 602120 | tf_op jit(solution)/shard_map/ppermute | solution.py:433
  30.9 9.0 %collective-permute-start.7 = (f32[392,128]{1,0:T(8,128)S(1)}, f32[392,128]{1,0:T(8,128)S(1)}, u32[]{:S(2)}, u32[]{:S(2)}) collective-permute-start(f32[392,128]{1,0:T(8,128)S(1)} %get-tuple-element.79), channel_id=1, source_target_pairs={{0,4},{2,6},{4,8},{6,10},{8,12},{10,14},{12,0},{14,2},{1,5},{3,7},... | collective-permute-start | bytes 602120 | tf_op jit(solution)/shard_map/ppermute | solution.py:434

commit v14 on v9

--- a/solution.py
+++ b/solution.py
@@ -53,7 +53,7 @@
         wide = pl.ds(first * size, many * size)
         pairs += [(k_hbm.at[:, wide], k_refs[i]), (v_hbm.at[:, wide], v_refs[i])]
     copies = [pltpu.make_async_copy(*pair, sems.at[i]) for i, pair in enumerate(pairs)]
-    for copy in copies:
+    for copy in copies[:5]:
         copy.start()
     earlier = lax.broadcasted_iota(jnp.int32, (tokens, tokens), 0)
     later = lax.broadcasted_iota(jnp.int32, (tokens, tokens), 1)
@@ -62,6 +62,8 @@
     down = lax.broadcasted_iota(jnp.int32, (heads, heads), 0)
     for copy in copies[:3]:
         copy.wait()
+    for copy in copies[5:]:
+        copy.start()
     spread = jnp.broadcast_to(exponent_ref[...], (heads, heads))
     exponent = jnp.sum(jnp.where(across == down, spread, 0).astype(F32), axis=1, keepdims=True)
     a = -jnp.exp2(-exponent) + jnp.log(keep_ref[...])

time: 32.1 us -> 32.6 us (1.016)
  Pallas kernels: 15.7 us -> 16.1 us
    pallas_call x1, Pallas kernels: 1.69 us -> 2.11 us  [first_message(): pl.pallas_call(functools.partial(first_kernel, heads, chunks), in_specs=[...]
where the time goes in v14:
time: 32.6 us; the launch traced here: 32.4 us
  Pallas kernels  16.1 us (49%)
  starting transfers between devices  10.5 us (32%)
  waiting for transfers between devices  5 us (15%)
  between operations  0.77 us (2%)
    pallas_call x4, Pallas kernels, intra(): pl.pallas_call(functools.partial(intra_kernel, first, heads, len(through)...  6.21 us
    ppermute x4, starting transfers between devices, shards(): swap = lambda x: lax.ppermute(x, 'seq', [(c, c ^ 1) for c in range(count)])  4.4 us
    pallas_call x2, Pallas kernels, finish(): pl.pallas_call(functools.partial(final_kernel, groups, unread), in_specs=...  4.29 us
    ppermute x3, waiting for transfers between devices, shards(): lax.ppermute(x, 'seq', [(c, (c + 2) % count) for c in range(count)])  4.25 us
    ppermute x3, starting transfers between devices, shards(): lax.ppermute(x, 'seq', [(c, (c + 2) % count) for c in range(count)])  3.81 us
    pallas_call x1, Pallas kernels, rest_messages(): pl.pallas_call(functools.partial(rest_kernel, chunks, done), in_specs=[pl...  2.97 us
    ppermute x1, starting transfers between devices, shards(): lax.ppermute(x, 'seq', [(c, c + 2) for c in range(count - 2)])  2.28 us
    pallas_call x1, Pallas kernels, first_message(): pl.pallas_call(functools.partial(first_kernel, heads, chunks), in_specs=[...  2.11 us
  transfers between devices with their start and end apart: 8, of which 4 were waited for; matrix products, arithmetic and copies ran while one was open for 0% of the time, Pallas kernels for 37%

profile of v14, /device:TPU:0, one launch (start us, length us, event | category | flops | bytes accessed | tf_op | source)
XLA Modules:
  0.0 32.4 jit_solution(4937829167027510423)
XLA Ops:
  0.6 2.1 %first_message.1 = (f32[520,128]{1,0:T(8,128)S(1)}, f32[16,512]{1,0:T(8,128)S(1)}, f32[16,512]{1,0:T(8,128)S(1)}, s32[1,512]{1,0:T(1,128)S(1)}, bf16[512,512]{1,...) custom-call(s32[1]{0:T(128)} %bitcast.order_ref.refs_0_, ...), custom_call_target="tpu_custom_call" | custom-call | flops 1 | bytes 1 | tf_op jit(solution)/shard_map/first_message/pallas_call | solution.py:102
  2.8 3.0 %collective-permute-start.3 = (f32[520,128]{1,0:T(8,128)S(1)}, f32[520,128]{1,0:T(8,128)S(1)}, u32[]{:S(2)}, u32[]{:S(2)}) collective-permute-start(f32[520,128]{1,0:T(8,128)S(1)} %get-tuple-element.59.refs_1_.rest_7_), channel_id=1, source_target_pairs={{0,2},{2,0},{4,6},{6,4},{8,10},{10,8},{12,14},{14,12},{1,3},{3,1},... | collective-permute-start | bytes 798728 | tf_op jit(solution)/shard_map/ppermute | solution.py:435
  5.8 0.4 %second_message.1.even_ref.rest_0_ = f32[520,128]{1,0:T(8,128)S(1)} custom-call(s32[1,512]{1,0:T(1,128)S(1)} %get-tuple-element.43.seg_ref, f32[16,512]{1,0:T(8,128)S(1)} %get-tuple-element.44.a_ref, f32[16,512]{1,0:T(8,128)S(1)} %get-tuple-element.45.w_ref, bf16[512,512]{1,0:T(8,128)(2,1)S(1)} %get-tuple-element.57.k_ref, ...), custom_call_target="tpu_custom_call" | custom-call | flops 1 | bytes 1 | tf_op jit(solution)/shard_map/second_message/pallas_call | solution.py:129
  6.1 0.0 copy-start
  6.1 1.6 %collective-permute-start.2 = (f32[520,128]{1,0:T(8,128)S(1)}, f32[520,128]{1,0:T(8,128)S(1)}, u32[]{:S(2)}, u32[]{:S(2)}) collective-permute-start(f32[520,128]{1,0:T(8,128)S(1)} %second_message.1.even_ref.rest_0_), channel_id=1, source_target_pairs={{0,4},{2,6},{4,8},{6,10},{8,12},{10,14},{12,0},{14,2},{1,5},{3,7},... | collective-permute-start | bytes 798728 | tf_op jit(solution)/shard_map/ppermute | solution.py:436
  7.8 3.0 %rest_messages.1 = (f32[520,128]{1,0:T(8,128)S(1)}, f32[520,128]{1,0:T(8,128)S(1)}, f32[512,512]{1,0:T(8,128)S(1)}, bf16[512,512]{1,0:T(8,128)(2,1)S(1)}, bf16[5...) custom-call(s32[1,512]{1,0:T(1,128)S(1)} %get-tuple-element.43.seg_r, ...), custom_call_target="tpu_custom_call" | custom-call | flops 1 | bytes 1 | tf_op jit(solution)/shard_map/rest_messages/pallas_call | solution.py:176
  10.7 0.6 %collective-permute-start.1 = (f32[520,128]{1,0:T(8,128)S(1)}, f32[520,128]{1,0:T(8,128)S(1)}, u32[]{:S(2)}, u32[]{:S(2)}) collective-permute-start(f32[520,128]{1,0:T(8,128)S(1)} %get-tuple-element.47.refs_1_.rest_7_), channel_id=1, source_target_pairs={{0,2},{2,0},{4,6},{6,4},{8,10},{10,8},{12,14},{14,12},{1,3},{3,1},... | collective-permute-start | bytes 798728 | tf_op jit(solution)/shard_map/ppermute | solution.py:435
  11.3 1.6 %collective-permute-start = (f32[520,128]{1,0:T(8,128)S(1)}, f32[520,128]{1,0:T(8,128)S(1)}, u32[]{:S(2)}, u32[]{:S(2)}) collective-permute-start(f32[520,128]{1,0:T(8,128)S(1)} %get-tuple-element.46.even_ref.rest_0_), channel_id=1, source_target_pairs={{0,4},{2,6},{4,8},{6,10},{8,12},{10,14},{12,0},{14,2},{1,5},{3,7},... | collective-permute-start | bytes 798728 | tf_op jit(solution)/shard_map/ppermute | solution.py:436
  12.9 1.5 %intra_span.4 = (f32[512,512]{1,0:T(8,128)S(1)}, f32[512,512]{1,0:T(8,128)S(1)}, f32[512,512]{1,0:T(8,128)S(1)}) custom-call(f32[512,512]{1,0:T(8,128)S(1)} %get-tuple-element.48.mask_ref, f32[16,512]{1,0:T(8,128)S(1)} %get-tuple-element.44.a_ref, f32[1,2048]{1,0:T(1,128)S(1)} %bitcast.4, bf16[512,512]{1,0:T(8,128)(2,1)S(1)} %get-tuple-element.60.q_ref.rest_6_, ...), custom_call_target="tpu_custom_call" | custom-call | flops 1 | bytes 1 | tf_op jit(solution)/shard_map/intra_span/pallas_call | solution.py:305
  14.5 0.1 join_windows.2.refs_0_
  14.5 2.5 %collective-permute-done.2.odd_ref.rest_2_ = f32[520,128]{1,0:T(8,128)S(1)} collective-permute-done((f32[520,128]{1,0:T(8,128)S(1)}, f32[520,128]{1,0:T(8,128)S(1)}, u32[]{:S(2)}, u32[]{:S(2)}) %collective-permute-start.2) | collective-permute-done | bytes 266272 | tf_op jit(solution)/shard_map/ppermute | solution.py:436
  17.0 0.1 collective-permute-start.6
  17.1 0.6 %collective-permute-start.7 = (f32[520,128]{1,0:T(8,128)S(1)}, f32[520,128]{1,0:T(8,128)S(1)}, u32[]{:S(2)}, u32[]{:S(2)}) collective-permute-start(f32[520,128]{1,0:T(8,128)S(1)} %get-tuple-element.79), channel_id=1, source_target_pairs={{0,4},{2,6},{4,8},{6,10},{8,12},{10,14},{12,0},{14,2},{1,5},{3,7},... | collective-permute-start | bytes 798728 | tf_op jit(solution)/shard_map/ppermute | solution.py:436
  17.7 1.5 %intra_span.5 = (f32[512,512]{1,0:T(8,128)S(1)}, f32[512,512]{1,0:T(8,128)S(1)}, f32[512,512]{1,0:T(8,128)S(1)}) custom-call(f32[512,512]{1,0:T(8,128)S(1)} %get-tuple-element.48.mask_ref, f32[16,512]{1,0:T(8,128)S(1)} %get-tuple-element.44.a_ref, f32[1,2048]{1,0:T(1,128)S(1)} %bitcast.5, bf16[512,512]{1,0:T(8,128)(2,1)S(1)} %get-tuple-element.53.q_ref.rest_13_, ...), custom_call_target="tpu_custom_call" | custom-call | flops 1 | bytes 1 | tf_op jit(solution)/shard_map/intra_span/pallas_call | solution.py:305
  19.3 1.6 %intra_span.6 = (f32[512,512]{1,0:T(8,128)S(1)}, f32[512,512]{1,0:T(8,128)S(1)}, f32[512,512]{1,0:T(8,128)S(1)}) custom-call(f32[512,512]{1,0:T(8,128)S(1)} %get-tuple-element.48.mask_ref, f32[16,512]{1,0:T(8,128)S(1)} %get-tuple-element.44.a_ref, f32[1,2048]{1,0:T(1,128)S(1)} %bitcast.6, bf16[512,512]{1,0:T(8,128)(2,1)S(1)} %get-tuple-element.49.q_ref.rest_6_, ...), custom_call_target="tpu_custom_call" | custom-call | flops 1 | bytes 1 | tf_op jit(solution)/shard_map/intra_span/pallas_call | solution.py:305
  20.9 0.1 join_windows.3.refs_0_
  20.9 1.8 %collective-permute-done.odd_ref.rest_2_ = f32[520,128]{1,0:T(8,128)S(1)} collective-permute-done((f32[520,128]{1,0:T(8,128)S(1)}, f32[520,128]{1,0:T(8,128)S(1)}, u32[]{:S(2)}, u32[]{:S(2)}) %collective-permute-start) | collective-permute-done | bytes 266272 | tf_op jit(solution)/shard_map/ppermute | solution.py:436
  22.8 0.7 %collective-permute-start.4 = (f32[520,128]{1,0:T(8,128)S(1)}, f32[520,128]{1,0:T(8,128)S(1)}, u32[]{:S(2)}, u32[]{:S(2)}) collective-permute-start(f32[520,128]{1,0:T(8,128)S(1)} %get-tuple-element.66.refs_0_), channel_id=1, source_target_pairs={{0,2},{2,0},{4,6},{6,4},{8,10},{10,8},{12,14},{14,12},{1,3},{3,1},... | collective-permute-start | bytes 798728 | tf_op jit(solution)/shard_map/ppermute | solution.py:435
  23.5 2.3 %collective-permute-start.5 = (f32[520,128]{1,0:T(8,128)S(1)}, f32[520,128]{1,0:T(8,128)S(1)}, u32[]{:S(2)}, u32[]{:S(2)}) collective-permute-start(f32[520,128]{1,0:T(8,128)S(1)} %get-tuple-element.69), channel_id=1, source_target_pairs={{0,4},{2,6},{4,8},{6,10},{8,12},{10,14},{1,5},{3,7},{5,9},{7,11},{... | collective-permute-start | bytes 798728 | tf_op jit(solution)/shard_map/ppermute | solution.py:437
  25.8 1.6 %intra_span.7 = (f32[512,512]{1,0:T(8,128)S(1)}, f32[512,512]{1,0:T(8,128)S(1)}, f32[512,512]{1,0:T(8,128)S(1)}) custom-call(f32[512,512]{1,0:T(8,128)S(1)} %get-tuple-element.48.mask_ref, f32[16,512]{1,0:T(8,128)S(1)} %get-tuple-element.44.a_ref, f32[1,2048]{1,0:T(1,128)S(1)} %bitcast.7, bf16[512,512]{1,0:T(8,128)(2,1)S(1)} %get-tuple-element.70.q_ref.rest_13_, ...), custom_call_target="tpu_custom_call" | custom-call | flops 1 | bytes 1 | tf_op jit(solution)/shard_map/intra_span/pallas_call | solution.py:305
  27.3 2.1 %finish.2 = (bf16[512,2048]{1,0:T(8,128)(2,1)}, f32[1,16,128,128]{3,2,1,0:T(8,128)}) custom-call(s32[1]{0:T(128)} %bitcast.order_ref.refs_0_, s32[1,512]{1,0:T(1,128)S(1)} %get-tuple-element.43.seg_ref, f32[520,128]{1,0:T(8,128)S(1)} %second_message.1.even_ref.rest_0_, f32[520,128]{1,0:T(8,128)S(1)} %collective-permute-done.6.rest_1_, ...), custom_call_target="tpu_custom_call" | custom-call | flops 1 | bytes 1 | tf_op jit(solution)/shard_map/finish/pallas_call | solution.py:405
  29.5 0.3 collective-permute-done.4.rest_1_
  29.8 0.5 %collective-permute-done.5.rest_9_ = f32[520,128]{1,0:T(8,128)S(1)} collective-permute-done((f32[520,128]{1,0:T(8,128)S(1)}, f32[520,128]{1,0:T(8,128)S(1)}, u32[]{:S(2)}, u32[]{:S(2)}) %collective-permute-start.5) | collective-permute-done | bytes 266272 | tf_op jit(solution)/shard_map/ppermute | solution.py:437
  30.2 2.1 %finish.3 = (bf16[512,2048]{1,0:T(8,128)(2,1)}, f32[1,16,128,128]{3,2,1,0:T(8,128)}) custom-call(s32[1]{0:T(128)} %bitcast.order_ref.refs_0_, s32[1,512]{1,0:T(1,128)S(1)} %get-tuple-element.43.seg_ref, f32[520,128]{1,0:T(8,128)S(1)} %get-tuple-element.46.even_ref.rest_0_, ...), custom_call_target="tpu_custom_call", output_to_operand_aliasing={{0}: (16, {}), {1}: (17, {})} | custom-call | flops 1 | bytes 1 | tf_op jit(solution)/shard_map/finish/pallas_call | solution.py:405
  (7 shorter events, 0.1 us)
Async XLA Ops:
  2.8 11.7 %collective-permute-start.3 = (f32[520,128]{1,0:T(8,128)S(1)}, f32[520,128]{1,0:T(8,128)S(1)}, u32[]{:S(2)}, u32[]{:S(2)}) collective-permute-start(f32[520,128]{1,0:T(8,128)S(1)} %get-tuple-element.59.refs_1_.rest_7_), channel_id=1, source_target_pairs={{0,2},{2,0},{4,6},{6,4},{8,10},{10,8},{12,14},{14,12},{1,3},{3,1},... | collective-permute-start | bytes 798728 | tf_op jit(solution)/shard_map/ppermute | solution.py:435
  6.1 6.8 %copy-start = (f32[2048]{0:T(1024)S(1)}, f32[2048]{0:T(1024)}, u32[]{:S(2)}) copy-start(f32[2048]{0:T(1024)} %param.15) | copy-start | bytes 24580
  6.1 10.9 %collective-permute-start.2 = (f32[520,128]{1,0:T(8,128)S(1)}, f32[520,128]{1,0:T(8,128)S(1)}, u32[]{:S(2)}, u32[]{:S(2)}) collective-permute-start(f32[520,128]{1,0:T(8,128)S(1)} %second_message.1.even_ref.rest_0_), channel_id=1, source_target_pairs={{0,4},{2,6},{4,8},{6,10},{8,12},{10,14},{12,0},{14,2},{1,5},{3,7},... | collective-permute-start | bytes 798728 | tf_op jit(solution)/shard_map/ppermute | solution.py:436
  10.7 10.1 %collective-permute-start.1 = (f32[520,128]{1,0:T(8,128)S(1)}, f32[520,128]{1,0:T(8,128)S(1)}, u32[]{:S(2)}, u32[]{:S(2)}) collective-permute-start(f32[520,128]{1,0:T(8,128)S(1)} %get-tuple-element.47.refs_1_.rest_7_), channel_id=1, source_target_pairs={{0,2},{2,0},{4,6},{6,4},{8,10},{10,8},{12,14},{14,12},{1,3},{3,1},... | collective-permute-start | bytes 798728 | tf_op jit(solution)/shard_map/ppermute | solution.py:435
  11.3 11.4 %collective-permute-start = (f32[520,128]{1,0:T(8,128)S(1)}, f32[520,128]{1,0:T(8,128)S(1)}, u32[]{:S(2)}, u32[]{:S(2)}) collective-permute-start(f32[520,128]{1,0:T(8,128)S(1)} %get-tuple-element.46.even_ref.rest_0_), channel_id=1, source_target_pairs={{0,4},{2,6},{4,8},{6,10},{8,12},{10,14},{12,0},{14,2},{1,5},{3,7},... | collective-permute-start | bytes 798728 | tf_op jit(solution)/shard_map/ppermute | solution.py:436
  17.0 10.3 %collective-permute-start.6 = (f32[520,128]{1,0:T(8,128)S(1)}, f32[520,128]{1,0:T(8,128)S(1)}, u32[]{:S(2)}, u32[]{:S(2)}) collective-permute-start(f32[520,128]{1,0:T(8,128)S(1)} %get-tuple-element.63.refs_0_), channel_id=1, source_target_pairs={{0,2},{2,0},{4,6},{6,4},{8,10},{10,8},{12,14},{14,12},{1,3},{3,1},... | collective-permute-start | bytes 798728 | tf_op jit(solution)/shard_map/ppermute | solution.py:435
  17.1 10.2 %collective-permute-start.7 = (f32[520,128]{1,0:T(8,128)S(1)}, f32[520,128]{1,0:T(8,128)S(1)}, u32[]{:S(2)}, u32[]{:S(2)}) collective-permute-start(f32[520,128]{1,0:T(8,128)S(1)} %get-tuple-element.79), channel_id=1, source_target_pairs={{0,4},{2,6},{4,8},{6,10},{8,12},{10,14},{12,0},{14,2},{1,5},{3,7},... | collective-permute-start | bytes 798728 | tf_op jit(solution)/shard_map/ppermute | solution.py:436
  22.8 7.0 %collective-permute-start.4 = (f32[520,128]{1,0:T(8,128)S(1)}, f32[520,128]{1,0:T(8,128)S(1)}, u32[]{:S(2)}, u32[]{:S(2)}) collective-permute-start(f32[520,128]{1,0:T(8,128)S(1)} %get-tuple-element.66.refs_0_), channel_id=1, source_target_pairs={{0,2},{2,0},{4,6},{6,4},{8,10},{10,8},{12,14},{14,12},{1,3},{3,1},... | collective-permute-start | bytes 798728 | tf_op jit(solution)/shard_map/ppermute | solution.py:435
  23.5 6.8 %collective-permute-start.5 = (f32[520,128]{1,0:T(8,128)S(1)}, f32[520,128]{1,0:T(8,128)S(1)}, u32[]{:S(2)}, u32[]{:S(2)}) collective-permute-start(f32[520,128]{1,0:T(8,128)S(1)} %get-tuple-element.69), channel_id=1, source_target_pairs={{0,4},{2,6},{4,8},{6,10},{8,12},{10,14},{1,5},{3,7},{5,9},{7,11},{... | collective-permute-start | bytes 798728 | tf_op jit(solution)/shard_map/ppermute | solution.py:437
